TPU v7x, 32 devices: a whole 2x2x4 slice. The times are simulated.
32 devices in a mesh: section: 2 (over core), dp: 16 (over z, y, x).
Axes of the slice: x: 2, y: 2, z: 4, core: 2. Of those that a mesh axis runs over, the one named last changes fastest.
Arguments:
- ends: bfloat16 [2, 48, 282, 768], P('section', 'dp'), may hold values from -6 to 6
- counts: int32 [48], P('dp'), may hold values from 194 to 282, as said below
- keep: int32 [2, 48, 2], P('section', 'dp'), may hold values 0 or 1
- attn_gain: float32 [2, 768], P('section'), may hold values from 0.1 to 1.9
- attn_shift: float32 [2, 768], P('section'), may hold values from -4 to 4
- qkv_weight: bfloat16 [2, 768, 2304], P('section'), may hold values from -0.21875 to 0.21875
- query_bias: float32 [2, 768], P('section'), may hold values from -6 to 6
- value_bias: float32 [2, 768], P('section'), may hold values from -6 to 6
- proj_weight: bfloat16 [2, 768, 768], P('section'), may hold values from -1.25 to 1.25
- proj_bias: float32 [2, 768], P('section'), may hold values from -4 to 4
- mlp_gain: float32 [2, 768], P('section'), may hold values from 0.1 to 1.9
- mlp_shift: float32 [2, 768], P('section'), may hold values from -4 to 4
- up_weight: bfloat16 [2, 768, 3072], P('section'), may hold values from -0.21875 to 0.21875
- up_bias: float32 [2, 3072], P('section'), may hold values from -6 to 6
- down_weight: bfloat16 [2, 3072, 768], P('section'), may hold values from -0.109375 to 0.109375
- down_bias: float32 [2, 768], P('section'), may hold values from -4 to 4
Outputs:
- ends_out: bfloat16 [2, 48, 282, 768], P('section', 'dp')
- grad_attn_gain: float32 [2, 768], P('section')
- grad_attn_shift: float32 [2, 768], P('section')
- grad_qkv_weight: float32 [2, 768, 2304], P('section')
- grad_query_bias: float32 [2, 768], P('section')
- grad_value_bias: float32 [2, 768], P('section')
- grad_proj_weight: float32 [2, 768, 768], P('section')
- grad_proj_bias: float32 [2, 768], P('section')
- grad_mlp_gain: float32 [2, 768], P('section')
- grad_mlp_shift: float32 [2, 768], P('section')
- grad_up_weight: float32 [2, 768, 3072], P('section')
- grad_up_bias: float32 [2, 3072], P('section')
- grad_down_weight: float32 [2, 3072, 768], P('section')
- grad_down_bias: float32 [2, 768], P('section')
- rms: float32 [2, 3], P('section')
Inputs may be any that keep to these rules, and one draw needn't show every extreme that they name: Valid slots of each image; its first counts slots are tokens, the rest padding. Some image has 282 and some has 194.
All inputs are finite; a program needn't handle non-finite values. No bound on the sum of `keep` on one device may be relied on, other than what follows from the above.
Results may differ from a plain program's by a relative error of at most 0.012.
Values may be sent and summed in bfloat16 or wider, within the bound.
No kernel may reach another device: no remote copies, remote signals or barrier semaphores. Data moves between devices by JAX's collectives and lax.ppermute only.
A program may use at most 320 MiB of HBM per device.

v0:
```python
import jax
import jax.numpy as jnp
from jax import lax
from jax.sharding import PartitionSpec as P

HEADS = 12
MICRO = 3


keep_scale = 4.0 / 3.0
eps_norm = 1e-06


def passed_along(block, axis, distance):
    devices = range(lax.axis_size(axis))
    route = [(i - distance, i) for i in devices if i - distance in devices]
    return lax.ppermute(block, axis, route)


def standardize(stream):
    centred = stream - jnp.mean(stream, axis=-1, keepdims=True)
    inverse = lax.rsqrt(jnp.mean(centred * centred, axis=-1, keepdims=True) + eps_norm)
    return (centred * inverse, inverse)


def norm_back(grad_normed, normed, inverse):
    return inverse * (
        grad_normed
        - jnp.mean(grad_normed, axis=-1, keepdims=True)
        - normed * jnp.mean(grad_normed * normed, axis=-1, keepdims=True)
    )


def gelu_slope(hidden):
    cumulative = 0.5 * (1.0 + lax.erf(hidden * 0.7071067811865476))
    density = jnp.exp(-0.5 * hidden * hidden) * 0.3989422804014327
    return cumulative + hidden * density


def key_live(valid, slots):
    return jnp.arange(slots)[None, None, None, :] < valid[:, None, None, None]


def layer_forward(stream, weights, valid, keeping):
    (
        attn_gain,
        attn_shift,
        qkv_weight,
        query_bias,
        value_bias,
        proj_weight,
        proj_bias,
        mlp_gain,
        mlp_shift,
        up_weight,
        up_bias,
        down_weight,
        down_bias,
    ) = weights
    images, slots, width = stream.shape
    split_shape = (images, slots, HEADS, width // HEADS)
    factor = (width // HEADS) ** (-0.5)
    normed_attn, inverse_attn = standardize(stream)
    normed_in = (normed_attn * attn_gain + attn_shift).astype(jnp.bfloat16)
    joined = jnp.einsum("bsd,de->bse", normed_in, qkv_weight, preferred_element_type=jnp.float32)
    queries = (joined[..., :width] + query_bias).astype(jnp.bfloat16)
    key_rows = joined[..., width : 2 * width].astype(jnp.bfloat16)
    value_rows = (joined[..., 2 * width :] + value_bias).astype(jnp.bfloat16)
    scores = (
        jnp.einsum(
            "bqhe,bkhe->bhqk",
            queries.reshape(split_shape),
            key_rows.reshape(split_shape),
            preferred_element_type=jnp.float32,
        )
        * factor
    )
    scores = jnp.where(key_live(valid, slots), scores, -1e30)
    log_total = jax.nn.logsumexp(scores, axis=-1, keepdims=True)
    attention = jnp.exp(scores - log_total)
    mixed = (
        jnp.einsum(
            "bhqk,bkhe->bqhe",
            attention.astype(jnp.bfloat16),
            value_rows.reshape(split_shape),
            preferred_element_type=jnp.float32,
        )
        .reshape(images, slots, width)
        .astype(jnp.bfloat16)
    )
    attn_branch = keeping[:, 0, None, None] * (
        jnp.einsum("bsd,de->bse", mixed, proj_weight, preferred_element_type=jnp.float32)
        + proj_bias
    )
    middle = stream + attn_branch
    normed_mlp, inverse_mlp = standardize(middle)
    mlp_in = (normed_mlp * mlp_gain + mlp_shift).astype(jnp.bfloat16)
    hidden = (
        jnp.einsum("bsd,df->bsf", mlp_in, up_weight, preferred_element_type=jnp.float32) + up_bias
    )
    active = jax.nn.gelu(hidden, approximate=False).astype(jnp.bfloat16)
    mlp_branch = keeping[:, 1, None, None] * (
        jnp.einsum("bsf,fd->bsd", active, down_weight, preferred_element_type=jnp.float32)
        + down_bias
    )
    saved = (
        normed_attn,
        inverse_attn,
        normed_in,
        queries,
        key_rows,
        value_rows,
        log_total,
        mixed,
        normed_mlp,
        inverse_mlp,
        mlp_in,
        hidden,
        active,
    )
    return (middle + mlp_branch, attn_branch, mlp_branch, saved)


def layer_backward(saved, grad_out, weights, valid, keeping):
    (
        attn_gain,
        attn_shift,
        qkv_weight,
        query_bias,
        value_bias,
        proj_weight,
        proj_bias,
        mlp_gain,
        mlp_shift,
        up_weight,
        up_bias,
        down_weight,
        down_bias,
    ) = weights
    (
        normed_attn,
        inverse_attn,
        normed_in,
        queries,
        key_rows,
        value_rows,
        log_total,
        mixed,
        normed_mlp,
        inverse_mlp,
        mlp_in,
        hidden,
        active,
    ) = saved
    images, slots, width = grad_out.shape
    split_shape = (images, slots, HEADS, width // HEADS)
    factor = (width // HEADS) ** (-0.5)

    def summed(values):
        return jnp.sum(values.astype(jnp.float32), axis=(0, 1))

    grad_down_in = (grad_out * keeping[:, 1, None, None]).astype(jnp.bfloat16)
    grad_down_weight = jnp.einsum(
        "bsf,bsd->fd", active, grad_down_in, preferred_element_type=jnp.float32
    )
    grad_down_bias = summed(grad_down_in)
    grad_active = jnp.einsum(
        "bsd,fd->bsf", grad_down_in, down_weight, preferred_element_type=jnp.float32
    )
    grad_hidden = (grad_active * gelu_slope(hidden)).astype(jnp.bfloat16)
    grad_up_weight = jnp.einsum(
        "bsd,bsf->df", mlp_in, grad_hidden, preferred_element_type=jnp.float32
    )
    grad_up_bias = summed(grad_hidden)
    grad_mlp_in = jnp.einsum(
        "bsf,df->bsd", grad_hidden, up_weight, preferred_element_type=jnp.float32
    )
    grad_mlp_gain = jnp.sum(grad_mlp_in * normed_mlp, axis=(0, 1))
    grad_mlp_shift = jnp.sum(grad_mlp_in, axis=(0, 1))
    grad_middle = grad_out + norm_back(grad_mlp_in * mlp_gain, normed_mlp, inverse_mlp)
    grad_proj_out = (grad_middle * keeping[:, 0, None, None]).astype(jnp.bfloat16)
    grad_proj_weight = jnp.einsum(
        "bsd,bse->de", mixed, grad_proj_out, preferred_element_type=jnp.float32
    )
    grad_proj_bias = summed(grad_proj_out)
    grad_mixed = (
        jnp.einsum("bse,de->bsd", grad_proj_out, proj_weight, preferred_element_type=jnp.float32)
        .astype(jnp.bfloat16)
        .reshape(split_shape)
    )
    query_heads = queries.reshape(split_shape)
    key_heads = key_rows.reshape(split_shape)
    value_heads = value_rows.reshape(split_shape)
    scores = (
        jnp.einsum("bqhe,bkhe->bhqk", query_heads, key_heads, preferred_element_type=jnp.float32)
        * factor
    )
    attention = jnp.where(key_live(valid, slots), jnp.exp(scores - log_total), 0.0)
    grad_attention = jnp.einsum(
        "bqhe,bkhe->bhqk", grad_mixed, value_heads, preferred_element_type=jnp.float32
    )
    grad_values = jnp.einsum(
        "bhqk,bqhe->bkhe",
        attention.astype(jnp.bfloat16),
        grad_mixed,
        preferred_element_type=jnp.float32,
    ).astype(jnp.bfloat16)
    grad_scores = (
        attention * (grad_attention - jnp.sum(grad_attention * attention, axis=-1, keepdims=True))
    ).astype(jnp.bfloat16)
    grad_queries = (
        jnp.einsum("bhqk,bkhe->bqhe", grad_scores, key_heads, preferred_element_type=jnp.float32)
        * factor
    ).astype(jnp.bfloat16)
    grad_keys = (
        jnp.einsum("bhqk,bqhe->bkhe", grad_scores, query_heads, preferred_element_type=jnp.float32)
        * factor
    ).astype(jnp.bfloat16)
    flat_shape = (images, slots, width)
    grad_joined = jnp.concatenate(
        [
            grad_queries.reshape(flat_shape),
            grad_keys.reshape(flat_shape),
            grad_values.reshape(flat_shape),
        ],
        axis=-1,
    )
    grad_qkv_weight = jnp.einsum(
        "bsd,bse->de", normed_in, grad_joined, preferred_element_type=jnp.float32
    )
    grad_query_bias = summed(grad_queries.reshape(flat_shape))
    grad_value_bias = summed(grad_values.reshape(flat_shape))
    grad_norm_in = jnp.einsum(
        "bse,de->bsd", grad_joined, qkv_weight, preferred_element_type=jnp.float32
    )
    grad_attn_gain = jnp.sum(grad_norm_in * normed_attn, axis=(0, 1))
    grad_attn_shift = jnp.sum(grad_norm_in, axis=(0, 1))
    grad_stream = grad_middle + norm_back(grad_norm_in * attn_gain, normed_attn, inverse_attn)
    return (
        grad_stream,
        (
            grad_attn_gain,
            grad_attn_shift,
            grad_qkv_weight,
            grad_query_bias,
            grad_value_bias,
            grad_proj_weight,
            grad_proj_bias,
            grad_mlp_gain,
            grad_mlp_shift,
            grad_up_weight,
            grad_up_bias,
            grad_down_weight,
            grad_down_bias,
        ),
    )


def per_device(
    ends,
    counts,
    keep,
    attn_gain,
    attn_shift,
    qkv_weight,
    query_bias,
    value_bias,
    proj_weight,
    proj_bias,
    mlp_gain,
    mlp_shift,
    up_weight,
    up_bias,
    down_weight,
    down_bias,
):
    params = (
        attn_gain,
        attn_shift,
        qkv_weight,
        query_bias,
        value_bias,
        proj_weight,
        proj_bias,
        mlp_gain,
        mlp_shift,
        up_weight,
        up_bias,
        down_weight,
        down_bias,
    )
    weights = tuple((item[0] for item in params))
    section = lax.axis_index("section")
    first = section == 0
    images_dev, slots, width = (ends.shape[1], ends.shape[2], ends.shape[3])
    per_micro = images_dev // MICRO
    local = ends[0].reshape(MICRO, per_micro, slots, width)
    valid_all = counts.reshape(MICRO, per_micro)
    keep_all = (keep[0].astype(jnp.float32) * keep_scale).reshape(MICRO, per_micro, 2)
    position = jnp.arange(slots)

    def row_mask(valid):
        return (position[None, :] < valid[:, None]).astype(jnp.float32)[..., None]

    received = jnp.zeros((per_micro, slots, width), jnp.bfloat16)
    layer_inputs = []
    results = []
    totals = jnp.zeros((3,), jnp.float32)
    for step_index in range(MICRO + 1):
        micro_index = step_index - section
        present = (micro_index >= 0) & (micro_index < MICRO)
        chosen = jnp.clip(micro_index, 0, MICRO - 1)
        valid = valid_all[chosen]
        keeping = keep_all[chosen]
        rows = row_mask(valid)
        entering = jnp.where(first, local[min(step_index, MICRO - 1)], received)
        result, attn_branch, mlp_branch, saved = layer_forward(
            entering.astype(jnp.float32), weights, valid, keeping
        )
        squares = jnp.stack(
            [
                jnp.sum(result * result * rows),
                jnp.sum(attn_branch * attn_branch * rows),
                jnp.sum(mlp_branch * mlp_branch * rows),
            ]
        )
        totals = totals + jnp.where(present, squares, 0.0)
        layer_inputs.append(entering)
        results.append((result * rows).astype(jnp.bfloat16))
        received = passed_along(result.astype(jnp.bfloat16), "section", 1)
    inputs_stack = jnp.stack(layer_inputs)
    accum = tuple((jnp.zeros(item.shape, jnp.float32) for item in weights))
    back_received = jnp.zeros((per_micro, slots, width), jnp.bfloat16)
    returned = []
    for step_index in range(MICRO + 1):
        micro_index = step_index - 1 + section
        present = (micro_index >= 0) & (micro_index < MICRO)
        chosen = jnp.clip(micro_index, 0, MICRO - 1)
        valid = valid_all[chosen]
        keeping = keep_all[chosen]
        rows = row_mask(valid)
        forward_step = jnp.clip(micro_index + section, 0, MICRO)
        seed_grad = jnp.where(
            first, back_received.astype(jnp.float32), local[chosen].astype(jnp.float32) * rows
        )
        saved = layer_forward(
            inputs_stack[forward_step].astype(jnp.float32), weights, valid, keeping
        )[3]
        grad_stream, grads = layer_backward(saved, seed_grad, weights, valid, keeping)
        grads = tuple((jnp.where(present, item, 0.0) for item in grads))
        returned.append(grad_stream.astype(jnp.bfloat16))
        back_received = passed_along(grad_stream.astype(jnp.bfloat16), "section", -1)
        accum = tuple((left + right for left, right in zip(accum, grads)))
    count_total = jnp.sum(counts.astype(jnp.float32))
    summed_all = lax.psum(
        (
            accum[0],
            accum[1],
            accum[2],
            accum[3],
            accum[4],
            accum[5],
            accum[6],
            accum[7],
            accum[8],
            accum[9],
            accum[10],
            accum[11],
            accum[12],
            totals,
            count_total,
        ),
        "dp",
    )
    whole = summed_all[:13]
    stat_total = summed_all[13]
    count_sum = summed_all[14]
    rms_local = jnp.sqrt(stat_total / (count_sum * width))
    stacked = jnp.where(first, jnp.stack(returned[1:]), jnp.stack(results[1:]))
    stacked = stacked.reshape(1, images_dev, slots, width)
    return (
        stacked,
        whole[0][None],
        whole[1][None],
        whole[2][None],
        whole[3][None],
        whole[4][None],
        whole[5][None],
        whole[6][None],
        whole[7][None],
        whole[8][None],
        whole[9][None],
        whole[10][None],
        whole[11][None],
        whole[12][None],
        rms_local[None],
    )


def solution(mesh):
    return jax.shard_map(
        per_device,
        mesh=mesh,
        in_specs=(
            P("section", "dp", None, None),
            P("dp"),
            P("section", "dp", None),
            P("section", None),
            P("section", None),
            P("section", None, None),
            P("section", None),
            P("section", None),
            P("section", None, None),
            P("section", None),
            P("section", None),
            P("section", None),
            P("section", None, None),
            P("section", None),
            P("section", None, None),
            P("section", None),
        ),
        out_specs=(
            P("section", "dp", None, None),
            P("section", None),
            P("section", None),
            P("section", None, None),
            P("section", None),
            P("section", None),
            P("section", None, None),
            P("section", None),
            P("section", None),
            P("section", None),
            P("section", None, None),
            P("section", None),
            P("section", None, None),
            P("section", None),
            P("section", None),
        ),
        check_vma=False,
    )
```

profile of v0, /device:TPU:0, one launch (start us, length us, event | category | flops | bytes accessed | tf_op | source)
XLA Modules:
  0.0 1328.6 jit_solution(13692204090163352675)
XLA Ops:
  45.8 17.0 %multiply_reduce_fusion.15 = (f32[]{:T(128)}, f32[]{:T(128)}, f32[]{:T(128)}, bf16[1,282,768]{2,1,0:T(8,128)(2,1)}) fusion(f32[282]{0:T(512)} %get-tuple-element.253, f32[282,768]{1,0:T(8,128)} %copy-done.83, bf16[1,1,282,768]{3,2,1,0:T(8,128)(2,1)} %copy-done.33, f32[768]{0:T(1024)} %reduce.195, bf16[1,3072,768]{2,1,0:T(8,128)(2,1)} %param.30, ...), kind=kOutput, calls=%fused_computation.906 | convolution fusion | flops 2723226624 | bytes 11194696 | tf_op jit(solution)/shard_map/bsf,fd->bsd/dot_general | solution.py:103
  100.8 29.5 %multiply_reduce_fusion.12 = (f32[]{:T(128)}, f32[1,282,768]{2,1,0:T(8,128)}, f32[282,768]{1,0:T(8,128)}) fusion(f32[282]{0:T(512)} %get-tuple-element.251, f32[282,768]{1,0:T(8,128)} %copy-done.48, bf16[1,282,768]{2,1,0:T(8,128)(2,1)} %copy-done.35, f32[768]{0:T(1024)} %reduce.195, bf16[1,3072,768]{2,1,0:T(8,128)(2,1)} %param.30, f32[3072]{0:T(1024)} %bitcast.1087, ...), kind=kOutput, calls=%fused_computation.903 | convolution fusion | flops 2721710592 | bytes 12494144 | tf_op jit(solution)/shard_map/bsf,fd->bsd/dot_general | solution.py:103
  165.5 17.5 %multiply_reduce_fusion.9 = (f32[]{:T(128)}, f32[1,282,768]{2,1,0:T(8,128)}, f32[282,768]{1,0:T(8,128)}) fusion(f32[282]{0:T(512)} %get-tuple-element.249, f32[282,768]{1,0:T(8,128)} %copy-done.49, bf16[1,282,768]{2,1,0:T(8,128)(2,1)} %copy-done.31, f32[768]{0:T(1024)} %reduce.195, bf16[1,3072,768]{2,1,0:T(8,128)(2,1)} %param.30, f32[3072]{0:T(1024)} %bitcast.1088, ...), kind=kOutput, calls=%fused_computation.900 | convolution fusion | flops 2721710592 | bytes 12494144 | tf_op jit(solution)/shard_map/bsf,fd->bsd/dot_general | solution.py:103
  219.3 4.3 fusion.555
  230.7 6.2 convert_reduce_fusion.3
  246.1 5.0 multiply_reduce_fusion.3
  263.5 13.4 %fusion.281 = f32[3072,768]{1,0:T(8,128)} fusion(f32[282,3072]{1,0:T(8,128)S(1)} %copy-done.215, f32[]{:T(128)} %bitcast.66, f32[282]{0:T(512)S(1)} %copy-done.154, pred[]{:T(512)S(6)} %eq.3, bf16[1,3,282,768]{3,2,1,0:T(8,128)(2,1)} %param.16, s32[]{:T(128)S(6)} %min.37), kind=kOutput, calls=%fused_computation.370 | convolution fusion | flops 1388035584 | bytes 13346413 | tf_op jit(solution)/shard_map/bsf,bsd->fd/dot_general | solution.py:163
  276.9 5.5 fusion.1196
  324.4 4.2 fusion.553
  355.0 5.9 fusion.78
  363.2 5.1 fusion.786
  384.7 5.0 multiply_reduce_fusion.2
  396.0 11.6 fusion.279
  407.6 5.4 fusion.1197
  419.3 5.9 fusion.785
  440.0 5.0 multiply_reduce_fusion.1
  451.3 11.4 fusion.277
  462.7 5.4 fusion.1198
  474.4 5.9 fusion.784
  495.4 5.5 convert_reduce_fusion.12
  500.9 4.6 multiply_reduce_fusion
  510.4 17.3 %add_bitcast_fusion = f32[1,3072,768]{2,1,0:T(8,128)} fusion(f32[3072,768]{1,0:T(8,128)} %fusion.277, f32[3072,768]{1,0:T(8,128)} %fusion.279, f32[3072,768]{1,0:T(8,128)} %fusion.281, pred[]{:T(512)S(6)} %and.28, pred[]{:T(512)S(6)} %and.27, pred[]{:T(512)S(6)} %and.26, pred[]{:T(512)S(6)} %and.25, f32[282,3072]{1,0:T(8,128)} %fusion.78, ...), kind=kOutput, calls=%fused_computation | convolution fusion | flops 1403467776 | bytes 41647108 | tf_op jit(solution)/shard_map/bsf,bsd->fd/dot_general | solution.py:163
  527.8 11.4 add_bitcast_fusion.1
  539.3 5.0 add_bitcast_fusion.3
  544.4 10.9 add_bitcast_fusion.2
  581.0 17.1 %multiply_reduce_fusion.5 = (f32[]{:T(128)}, f32[]{:T(128)}, f32[282,768]{1,0:T(8,128)}) fusion(f32[282,768]{1,0:T(8,128)} %copy-done.47, f32[282]{0:T(512)} %fusion.1183, f32[768]{0:T(1024)} %reduce.195, bf16[1,3072,768]{2,1,0:T(8,128)(2,1)} %param.30, f32[3072]{0:T(1024)} %bitcast.1089, bf16[1,768,3072]{2,1,0:T(8,128)(2,1)} %param.28, ...), kind=kOutput, calls=%fused_computation.896 | convolution fusion | flops 2721710592 | bytes 11627844 | tf_op jit(solution)/shard_map/bsf,fd->bsd/dot_general | solution.py:103
  601.3 8.3 fusion.902
  617.6 4.8 fusion.683
  623.6 83.8 %all-reduce = (f32[1,768]{1,0:T(1,128)}, f32[1,768]{1,0:T(1,128)}, f32[1,768]{1,0:T(1,128)}, f32[1,768]{1,0:T(1,128)}, f32[1,768]{1,0:T(1,128)}, /*index=5*/f32[...) all-reduce(f32[1,768]{1,0:T(1,128)} %broadcast_in_dim.300, ...), channel_id=1, replica_groups=mesh['section'=2,'dp'=16] {'dp'}, use_global_device_ids=true, to_apply=%region_72.73 | all-reduce | flops 9220 | bytes 73760 | tf_op jit(solution)/shard_map/psum | solution.py:355
  714.7 585.5 %all-reduce.4.cloned.1.call-done = (f32[1,768,2304]{2,1,0:T(8,128)}, f32[1,768,768]{2,1,0:T(8,128)}, f32[1,768,3072]{2,1,0:T(8,128)}, f32[1,3072,768]{2,1,0:T(8,128)}) async-done(((f32[1,768,2304]{2,1,0:T(8,128)}, f32[1,768,768]{2,1,0:T(8,128)}, f32[1,768,3072]{2,1,0:T(8,128)}, f32[1,3072,768]{2,1,0:T(8,128)}), (f32[1,768,2304]{2,1,0:T(8,128)}, f32[1,768,768]{2,1,0:T(8,128)}, f32[1,768,3072]{2,1,0:T(8,128)}, ...) | async-done | bytes 28311568 | tf_op jit(solution)/shard_map/psum | solution.py:355
  1300.2 6.6 copy.167
  1308.2 9.3 copy.169
  (794 shorter events, 371.2 us)
Async XLA Ops:
  7.2 1293.0 %all-reduce.4.cloned.1.call-start = ((), (), s32[]{:S(2)}) async-start(), calls=%async_computation | async-start | bytes 56623104 | tf_op jit(solution)/shard_map/psum | solution.py:355
  62.8 13.0 collective-permute-start
  132.6 6.5 collective-permute-start.1
  185.4 6.5 collective-permute-start.2
  226.1 13.2 copy-start.29
  226.1 13.2 copy-start.119
  226.4 12.9 copy-start.137
  254.2 28.2 %copy-start.57 = (bf16[12,64,282]{2,1,0:T(8,128)(2,1)}, bf16[12,64,282]{2,1,0:T(8,128)(2,1)S(1)}, u32[]{:S(2)}) copy-start(bf16[12,64,282]{2,1,0:T(8,128)(2,1)S(1)} %get-tuple-element.230) | copy-start | bytes 1299460
  255.2 27.1 %copy-start.59 = (bf16[12,64,282]{2,1,0:T(8,128)(2,1)}, bf16[12,64,282]{2,1,0:T(8,128)(2,1)S(1)}, u32[]{:S(2)}) copy-start(bf16[12,64,282]{2,1,0:T(8,128)(2,1)S(1)} %fusion.544) | copy-start | bytes 1299460
  257.3 25.1 %copy-start.85 = (bf16[12,64,282]{2,1,0:T(8,128)(2,1)}, bf16[12,64,282]{2,1,0:T(8,128)(2,1)S(1)}, u32[]{:S(2)}) copy-start(bf16[12,64,282]{2,1,0:T(8,128)(2,1)S(1)} %get-tuple-element.238) | copy-start | bytes 1299460
  263.4 13.4 %copy-start.30 = (f32[282,768]{1,0:T(8,128)S(1)}, f32[282,768]{1,0:T(8,128)}, u32[]{:S(2)}) copy-start(f32[282,768]{1,0:T(8,128)} %copy-done.29) | copy-start | bytes 2598916
  263.4 13.4 %copy-start.78 = (bf16[282,3072]{1,0:T(8,128)(2,1)S(1)}, bf16[282,3072]{1,0:T(8,128)(2,1)}, u32[]{:S(2)}) copy-start(bf16[282,3072]{1,0:T(8,128)(2,1)} %copy-done.77) | copy-start | bytes 5197828
  263.4 13.4 %copy-start.120 = (f32[282]{0:T(512)S(1)}, f32[282]{0:T(512)}, u32[]{:S(2)}) copy-start(f32[282]{0:T(512)} %copy-done.119) | copy-start | bytes 3388
  263.4 13.4 %copy-start.138 = (f32[282]{0:T(512)S(1)}, f32[282]{0:T(512)}, u32[]{:S(2)}) copy-start(f32[282]{0:T(512)} %copy-done.137) | copy-start | bytes 3388
  285.9 82.4 %collective-permute-start.3 = (bf16[1,282,768]{2,1,0:T(8,128)(2,1)}, bf16[1,282,768]{2,1,0:T(8,128)(2,1)}, u32[]{:S(2)}, u32[]{:S(2)}) collective-permute-start(bf16[1,282,768]{2,1,0:T(8,128)(2,1)} %fusion.808), channel_id=1, source_target_pairs={{16,0},{17,1},{18,2},{19,3},{20,4},{21,5},{22,6},{23,7},{24,8},{25... | collective-permute-start | bytes 1299464 | tf_op jit(solution)/shard_map/ppermute | solution.py:17
  355.0 15.9 %slice-start.15 = ((s8[4718592]{0:T(1024)(128)(4,1)}), s8[4194304]{0:T(1024)(128)(4,1)S(1)}, s32[]{:S(2)}) async-start(s8[4718592]{0:T(1024)(128)(4,1)} %bitcast.1068), calls=%async_computation.16 | async-start | bytes 8388608
  396.0 11.6 copy-start.28
  396.0 11.6 copy-start.80
  396.0 11.6 copy-start.118
  396.0 11.6 copy-start.136
  415.4 11.7 slice-start.17
  415.8 9.4 collective-permute-start.4
  470.5 11.7 slice-start.19
  470.9 9.4 collective-permute-start.5
  507.2 37.1 %slice-start.8 = ((s8[7077888]{0:T(1024)(128)(4,1)}), s8[4194304]{0:T(1024)(128)(4,1)S(1)}, s32[]{:S(2)}) async-start(s8[7077888]{0:T(1024)(128)(4,1)} %bitcast.972), calls=%async_computation.9 | async-start | bytes 8388608
  508.6 35.7 %copy-start.61 = (bf16[12,64,282]{2,1,0:T(8,128)(2,1)}, bf16[12,64,282]{2,1,0:T(8,128)(2,1)S(1)}, u32[]{:S(2)}) copy-start(bf16[12,64,282]{2,1,0:T(8,128)(2,1)S(1)} %get-tuple-element.224) | copy-start | bytes 1299460
  510.4 17.3 %copy-start.22 = (f32[282,768]{1,0:T(8,128)S(1)}, f32[282,768]{1,0:T(8,128)}, u32[]{:S(2)}) copy-start(f32[282,768]{1,0:T(8,128)} %copy-done.20) | copy-start | bytes 2598916
  510.4 17.3 %copy-start.130 = (f32[282]{0:T(512)S(1)}, f32[282]{0:T(512)}, u32[]{:S(2)}) copy-start(f32[282]{0:T(512)} %copy-done.128) | copy-start | bytes 3388
  510.4 17.4 %copy-start.157 = (f32[282]{0:T(512)S(1)}, f32[282]{0:T(512)}, u32[]{:S(2)}) copy-start(f32[282]{0:T(512)} %copy-done.155) | copy-start | bytes 3388
  510.4 33.9 %slice-start.9 = ((s8[7077888]{0:T(1024)(128)(4,1)}), s8[2883584]{0:T(1024)(128)(4,1)S(1)}, s32[]{:S(2)}) async-start(s8[7077888]{0:T(1024)(128)(4,1)} %bitcast.972), calls=%async_computation.10 | async-start | bytes 5767168
  559.6 13.1 copy-start.193
  581.0 36.5 %copy-start.149 = (f32[282]{0:T(512)S(1)}, f32[282]{0:T(512)}, u32[]{:S(2)}) copy-start(f32[282]{0:T(512)} %copy-done.147) | copy-start | bytes 3388
  (224 other events, 989.7 us)
Sparse Core Ops, SparseCore 0:
  555.4 744.7 all-reduce.3
where the time goes:
time: 1340 us; the launch traced here: 1330 us
  waiting for transfers between devices  586 us (44%)
  matrix products  381 us (28%)
  local copies, waits for them, and re-layouts  133 us (10%)
  other arithmetic  117 us (9%)
  blocking collectives  83.8 us (6%)
  between operations  18.2 us (1%)
    psum x1, waiting for transfers between devices, per_device(): lax.psum((accum[0], accum[1], accum[2], accum[3], accum[4], accum[5], acc...  585 us
    psum x1, blocking collectives, per_device(): lax.psum((accum[0], accum[1], accum[2], accum[3], accum[4], accum[5], acc...  83.8 us
    dot_general x4, matrix products, layer_forward(): jnp.einsum('bsf,fd->bsd', active, down_weight, preferred_element_type=jnp...  81.1 us
    dot_general x4, matrix products, layer_backward(): jnp.einsum('bsf,bsd->fd', active, grad_down_in, preferred_element_type=jn...  53.7 us
    unnamed x502, local copies, waits for them, and re-layouts  46.1 us
    dot_general x8, matrix products, layer_forward(): jnp.einsum('bhqk,bkhe->bqhe', attention.astype(jnp.bfloat16), value_rows....  30.6 us
    slice x16, local copies, waits for them, and re-layouts, layer_forward(): key_rows = joined[..., width:2 * width].astype(jnp.bfloat16)  28.1 us
    dot_general x4, matrix products, layer_backward(): jnp.einsum('bsd,bse->de', normed_in, grad_joined, preferred_element_type=...  27.7 us
  transfers between devices with their start and end apart: 7, of which 1 were waited for; matrix products, arithmetic and copies ran while one was open for 14% of the time, Pallas kernels for 0%

commit v1 on v0

v1 whole, which is shorter than its diff:
```python
import functools

import jax
import jax.numpy as jnp
from jax import lax
from jax.experimental import pallas as pl
from jax.experimental.pallas import tpu as pltpu
from jax.sharding import PartitionSpec as P

HEADS = 12
CHUNKS = 16
TILE = 256
KEEP_SCALE = 4.0 / 3.0
EPS = 1e-06
F32 = jnp.float32
BF16 = jnp.bfloat16
VMEM = pl.BlockSpec(memory_space=pltpu.VMEM)
SMEM = pl.BlockSpec(memory_space=pltpu.SMEM)


def dot_nn(left, right):
    return lax.dot_general(left, right, (((1,), (0,)), ((), ())), preferred_element_type=F32)


def dot_nt(left, right):
    return lax.dot_general(left, right, (((1,), (1,)), ((), ())), preferred_element_type=F32)


def dot_tn(left, right):
    return lax.dot_general(left, right, (((0,), (0,)), ((), ())), preferred_element_type=F32)


def call(body, operands, outs, scratch=(), flops=0, limit=48):
    in_specs = [SMEM if jnp.issubdtype(o.dtype, jnp.integer) or o.ndim == 1 else VMEM for o in operands]
    out_specs = [SMEM if o.shape == (8,) else VMEM for o in outs]
    moved = sum(o.size * o.dtype.itemsize for o in operands) + sum(
        o.size * o.dtype.itemsize for o in outs
    )
    return pl.pallas_call(
        body,
        out_shape=list(outs),
        in_specs=in_specs,
        out_specs=out_specs,
        scratch_shapes=list(scratch),
        compiler_params=pltpu.CompilerParams(vmem_limit_bytes=limit << 20),
        cost_estimate=pl.CostEstimate(flops=int(flops), bytes_accessed=int(moved), transcendentals=0),
    )(*operands)


def shaped(*shape, dtype=BF16):
    return jax.ShapeDtypeStruct(shape, dtype)


def standardize(stream):
    centred = stream - jnp.mean(stream, axis=-1, keepdims=True)
    inverse = lax.rsqrt(jnp.mean(centred * centred, axis=-1, keepdims=True) + EPS)
    return centred * inverse, inverse


def norm_back(grad, normed, inverse):
    return inverse * (
        grad
        - jnp.mean(grad, axis=-1, keepdims=True)
        - normed * jnp.mean(grad * normed, axis=-1, keepdims=True)
    )


def lanes(start, size):
    return pl.ds(pl.multiple_of(start, 128), size)


def rows_at(start, size):
    return pl.ds(pl.multiple_of(start, 16), size)


def row_mask(length, valid):
    return lax.broadcasted_iota(jnp.int32, (length, 1), 0) < valid


def qkv_kernel(length, images, act, x, gain, shift, weight, qb, vb, n1, qkv):
    @pl.when(act[0] == 1)
    def _():
        width = x.shape[1]

        def norm(i, _):
            r = rows_at(i * (length // 2), length // 2)
            normed, _inv = standardize(x[r, :].astype(F32))
            n1[r, :] = (normed * gain[...] + shift[...]).astype(BF16)
            return 0

        lax.fori_loop(0, images * 2, norm, 0)
        tiles = width // TILE
        for part, bias in ((0, qb), (1, None), (2, vb)):

            def tile(t, _, part=part, bias=bias):
                at = lanes(part * width + t * TILE, TILE)
                out = dot_nn(n1[...], weight[:, at])
                if bias is not None:
                    out = out + bias[:, lanes(t * TILE, TILE)]
                qkv[:, at] = out.astype(BF16)
                return 0

            lax.fori_loop(0, tiles, tile, 0)


def attend_kernel(length, images, act, valid, qkv, probs, mixed):
    width = mixed.shape[1]
    pairs = width // 128
    low = lax.broadcasted_iota(jnp.int32, (1, 128), 1) < 64

    @pl.when(act[0] == 1)
    def _():
        def pair(step, _):
            i = step // pairs
            p = step - i * pairs
            r = rows_at(i * length, length)
            q = qkv[r, lanes(p * 128, 128)] * jnp.asarray(0.125, BF16)
            k = qkv[r, lanes(width + p * 128, 128)]
            v = qkv[r, lanes(2 * width + p * 128, 128)]
            zero = jnp.zeros_like(q)
            stacked = jnp.concatenate([jnp.where(low, q, zero), jnp.where(low, zero, q)], axis=0)
            scores = dot_nt(stacked, k)
            live = lax.broadcasted_iota(jnp.int32, (1, length), 1) < valid[i]
            scores = jnp.where(live, scores, -1e30)
            top = jnp.max(scores, axis=-1, keepdims=True)
            e = jnp.exp(scores - top)
            total = jnp.sum(e, axis=-1, keepdims=True)
            prob = (e * (1.0 / total)).astype(BF16)
            probs[rows_at(step * 2 * length, 2 * length), :] = prob
            out = dot_nn(prob, v)
            mixed[r, lanes(p * 128, 128)] = jnp.where(low, out[:length], out[length:]).astype(BF16)
            return 0

        lax.fori_loop(0, images * pairs, pair, 0)


def up_kernel(
    length, images, act, keep, valid, x, mixed, pw, pb, gain, shift, uw, ub, h1, n2, slope, gact, stat
):
    @pl.when(act[0] == 1)
    def _():
        width = x.shape[1]
        hidden = gact.shape[1]
        total = jnp.zeros((length, width), F32)
        for i in range(images):
            r = slice(i * length, (i + 1) * length)
            a = keep[2 * i] * (dot_nn(mixed[r, :], pw[...]) + pb[...])
            total = total + jnp.where(row_mask(length, valid[i]), a * a, 0.0)
            h = x[r, :].astype(F32) + a
            h1[r, :] = h
            normed, _inv = standardize(h)
            n2[r, :] = (normed * gain[...] + shift[...]).astype(BF16)
        stat[0] = jnp.sum(total)

        def tile(t, _):
            at = lanes(t * TILE, TILE)
            for i in range(images):
                r = slice(i * length, (i + 1) * length)
                u = dot_nn(n2[r, :], uw[:, at]) + ub[:, at]
                cdf = 0.5 * (1.0 + lax.erf(u * 0.7071067811865476))
                gact[r, at] = (u * cdf).astype(BF16)
                slope[r, at] = (cdf + u * (jnp.exp(-0.5 * u * u) * 0.3989422804014327)).astype(BF16)
            return 0

        lax.fori_loop(0, hidden // TILE, tile, 0)


def down_kernel(length, images, act, keep, valid, h1, gact, dw, db, h2, stat):
    @pl.when(act[0] == 1)
    def _():
        width = h1.shape[1]
        tiles = width // TILE
        stat[0] = 0.0
        stat[1] = 0.0

        def tile(step, _):
            i = step // tiles
            r = rows_at(i * length, length)
            at = lanes((step - i * tiles) * TILE, TILE)
            m = keep[2 * i + 1] * (dot_nn(gact[r, :], dw[:, at]) + db[:, at])
            h = h1[r, at] + m
            mask = row_mask(length, valid[i])
            stat[0] += jnp.sum(jnp.where(mask, h * h, 0.0))
            stat[1] += jnp.sum(jnp.where(mask, m * m, 0.0))
            h2[r, at] = h.astype(BF16)
            return 0

        lax.fori_loop(0, images * tiles, tile, 0)


def scatter_chunks(code, unit, chunk_of, pieces):
    starts = (8, 4, 2, 1, 0)
    counts = (8, 4, 2, 1, 1)
    for ref, start, count in zip(pieces, starts, counts):
        for j in range(count):
            which = jnp.bitwise_xor(code, start + j)
            chunk_of(which, ref, j * unit)


def down_back_kernel(length, images, act, code, keep, dh2, gact, slope, dw, *refs):
    *pieces, du, vec, dz, full = refs

    @pl.when(act[0] == 1)
    def _():
        width = dh2.shape[1]
        hidden = gact.shape[1]
        total = jnp.zeros((1, width), F32)
        for i in range(images):
            r = slice(i * length, (i + 1) * length)
            z = (keep[2 * i + 1] * dh2[r, :].astype(F32)).astype(BF16)
            dz[r, :] = z
            total = total + jnp.sum(z.astype(F32), axis=0, keepdims=True)
        vec[0:1, :] = total

        def wtile(t, _):
            at = pl.multiple_of(t * 512, 512)
            full[pl.ds(at, 512), :] = dot_tn(gact[:, pl.ds(at, 512)], dz[...]).astype(BF16)
            return 0

        lax.fori_loop(0, hidden // 512, wtile, 0)
        unit = hidden // CHUNKS

        def move(which, ref, at):
            ref[at : at + unit, :] = full[rows_at(which * unit, unit), :]

        scatter_chunks(code[0], unit, move, pieces)

        def tile(t, _):
            at = lanes(t * TILE, TILE)
            d = dot_nt(dz[...], dw[rows_at(t * TILE, TILE), :])
            d = (d * slope[:, at].astype(F32)).astype(BF16)
            du[:, at] = d
            return 0

        lax.fori_loop(0, hidden // TILE, tile, 0)


def up_back_kernel(
    length, images, act, code, keep, dh2, n2, du, uw, h1, gain, mixed, pw, *refs
):
    *pieces, dh1, dmix, vec, uvec, dy, upf, projf = refs

    @pl.when(act[0] == 1)
    def _():
        width = dh2.shape[1]
        hidden = du.shape[1]

        def wtile(t, _):
            at = lanes(t * 512, 512)
            upf[:, at] = dot_tn(n2[...], du[:, at]).astype(BF16)
            uvec[:, at] = jnp.sum(du[:, at].astype(F32), axis=0, keepdims=True)
            return 0

        lax.fori_loop(0, hidden // 512, wtile, 0)
        dgain = jnp.zeros((1, width), F32)
        dshift = jnp.zeros((1, width), F32)
        dpb = jnp.zeros((1, width), F32)
        for i in range(images):
            r = slice(i * length, (i + 1) * length)
            dn2 = dot_nt(du[r, :], uw[...])
            normed, inverse = standardize(h1[r, :])
            dgain = dgain + jnp.sum(dn2 * normed, axis=0, keepdims=True)
            dshift = dshift + jnp.sum(dn2, axis=0, keepdims=True)
            d = dh2[r, :].astype(F32) + norm_back(dn2 * gain[...], normed, inverse)
            dh1[r, :] = d
            y = (keep[2 * i] * d).astype(BF16)
            dy[r, :] = y
            dpb = dpb + jnp.sum(y.astype(F32), axis=0, keepdims=True)
            dmix[r, :] = dot_nt(y, pw[...]).astype(BF16)
        vec[0:1, :] = dgain
        vec[1:2, :] = dshift
        vec[2:3, :] = dpb
        projf[...] = dot_tn(mixed[...], dy[...]).astype(BF16)
        blocks = hidden // width
        unit = width // CHUNKS
        whole = unit * (blocks + 1)

        def move(which, ref, at):
            r = rows_at(which * unit, unit)
            for b in range(blocks):
                ref[at + b * unit : at + (b + 1) * unit, :] = upf[r, b * width : (b + 1) * width]
            ref[at + blocks * unit : at + whole, :] = projf[r, :]

        scatter_chunks(code[0], whole, move, pieces)


def attend_back_kernel(length, images, act, qkv, probs, mixed, dmix, dj):
    width = mixed.shape[1]
    pairs = width // 128
    low = lax.broadcasted_iota(jnp.int32, (1, 128), 1) < 64

    @pl.when(act[0] == 1)
    def _():
        def pair(step, _):
            i = step // pairs
            p = step - i * pairs
            r = rows_at(i * length, length)
            at = lanes(p * 128, 128)
            k_at = lanes(width + p * 128, 128)
            v_at = lanes(2 * width + p * 128, 128)
            scale = jnp.asarray(0.125, BF16)
            q = qkv[r, at] * scale
            k = qkv[r, k_at]
            v = qkv[r, v_at]
            o = mixed[r, at].astype(F32)
            g = dmix[r, at]

            def stack(a):
                zero = jnp.zeros_like(a)
                return jnp.concatenate([jnp.where(low, a, zero), jnp.where(low, zero, a)], axis=0)

            both = stack(g)
            prod = g.astype(F32) * o
            side = jnp.concatenate(
                [
                    jnp.sum(jnp.where(low, prod, 0.0), axis=-1, keepdims=True),
                    jnp.sum(jnp.where(low, 0.0, prod), axis=-1, keepdims=True),
                ],
                axis=0,
            )
            prob = probs[rows_at(step * 2 * length, 2 * length), :]
            dp = dot_nt(both, v)
            ds = (prob.astype(F32) * (dp - side)).astype(BF16)
            dj[r, v_at] = dot_tn(prob, both).astype(BF16)
            dq = dot_nn(ds, k)
            dj[r, at] = (0.125 * jnp.where(low, dq[:length], dq[length:])).astype(BF16)
            dj[r, k_at] = dot_tn(ds, stack(q)).astype(BF16)
            return 0

        lax.fori_loop(0, images * pairs, pair, 0)


def qkv_back_kernel(length, images, act, code, x, n1, dj, weight, gain, dh1, *refs):
    *pieces, dx, vec, full = refs

    @pl.when(act[0] == 1)
    def _():
        width = x.shape[1]
        three = dj.shape[1]

        def wtile(t, _):
            at = lanes(t * TILE, TILE)
            full[:, at] = dot_tn(n1[...], dj[:, at]).astype(BF16)
            return 0

        lax.fori_loop(0, three // TILE, wtile, 0)
        dgain = jnp.zeros((1, width), F32)
        dshift = jnp.zeros((1, width), F32)
        dqb = jnp.zeros((1, width), F32)
        dvb = jnp.zeros((1, width), F32)
        for i in range(images):
            r = slice(i * length, (i + 1) * length)
            dqb = dqb + jnp.sum(dj[r, 0:width].astype(F32), axis=0, keepdims=True)
            dvb = dvb + jnp.sum(dj[r, 2 * width :].astype(F32), axis=0, keepdims=True)
            dn1 = dot_nt(dj[r, :], weight[...])
            normed, inverse = standardize(x[r, :].astype(F32))
            dgain = dgain + jnp.sum(dn1 * normed, axis=0, keepdims=True)
            dshift = dshift + jnp.sum(dn1, axis=0, keepdims=True)
            d = dh1[r, :] + norm_back(dn1 * gain[...], normed, inverse)
            dx[r, :] = d.astype(BF16)
        vec[0:1, :] = dgain
        vec[1:2, :] = dshift
        vec[2:3, :] = dqb
        vec[3:4, :] = dvb
        blocks = three // width
        unit = width // CHUNKS

        def move(which, ref, at):
            r = rows_at(which * unit, unit)
            for b in range(blocks):
                ref[at + b * unit : at + (b + 1) * unit, :] = full[r, b * width : (b + 1) * width]

        scatter_chunks(code[0], blocks * unit, move, pieces)


def piece_shapes(unit, width):
    return [shaped(n * unit, width) for n in (8, 4, 2, 1, 1)]


def forward(act, valid, keep, x, w, length, images):
    (ag, ac, qkvw, qb, vb, pw, pb, mg, mc, uw, ub, dw, db) = w
    tokens, width = x.shape
    hidden = uw.shape[1]
    half = width * width * tokens * 2
    n1, qkv = call(
        functools.partial(qkv_kernel, length, images),
        (act, x, ag, ac, qkvw, qb, vb),
        (shaped(tokens, width), shaped(tokens, 3 * width)),
        flops=3 * half,
    )
    probs, mixed = call(
        functools.partial(attend_kernel, length, images),
        (act, valid, qkv),
        (shaped(images * HEADS * length, length), shaped(tokens, width)),
        flops=2 * half,
    )
    h1, n2, slope, gact, stat_a = call(
        functools.partial(up_kernel, length, images),
        (act, keep, valid, x, mixed, pw, pb, mg, mc, uw, ub),
        (
            shaped(tokens, width, dtype=F32),
            shaped(tokens, width),
            shaped(tokens, hidden),
            shaped(tokens, hidden),
            shaped(8, dtype=F32),
        ),
        flops=5 * half,
    )
    h2, stat_m = call(
        functools.partial(down_kernel, length, images),
        (act, keep, valid, h1, gact, dw, db),
        (shaped(tokens, width), shaped(8, dtype=F32)),
        flops=4 * half,
    )
    stats = jnp.stack([stat_m[0], stat_a[0], stat_m[1]])
    return h2, stats, (x, n1, qkv, probs, mixed, h1, n2, slope, gact)


def down_back(act, code, keep, seed, saved, w, length, images):
    (ag, ac, qkvw, qb, vb, pw, pb, mg, mc, uw, ub, dw, db) = w
    (x, n1, qkv, probs, mixed, h1, n2, slope, gact) = saved
    tokens, width = x.shape
    hidden = uw.shape[1]
    half = width * width * tokens * 2
    *pieces, du, vec = call(
        functools.partial(down_back_kernel, length, images),
        (act, code, keep, seed, gact, slope, dw),
        (
            *piece_shapes(hidden // CHUNKS, width),
            shaped(tokens, hidden),
            shaped(8, width, dtype=F32),
        ),
        scratch=(pltpu.VMEM((tokens, width), BF16), pltpu.VMEM((hidden, width), BF16)),
        flops=8 * half,
    )
    return pieces, du, vec


def up_back(act, code, keep, seed, du, saved, w, length, images):
    (ag, ac, qkvw, qb, vb, pw, pb, mg, mc, uw, ub, dw, db) = w
    (x, n1, qkv, probs, mixed, h1, n2, slope, gact) = saved
    tokens, width = x.shape
    hidden = uw.shape[1]
    half = width * width * tokens * 2
    *pieces, dh1, dmix, vec, uvec = call(
        functools.partial(up_back_kernel, length, images),
        (act, code, keep, seed, n2, du, uw, h1, mg, mixed, pw),
        (
            *piece_shapes((hidden + width) // CHUNKS, width),
            shaped(tokens, width, dtype=F32),
            shaped(tokens, width),
            shaped(8, width, dtype=F32),
            shaped(1, hidden, dtype=F32),
        ),
        scratch=(
            pltpu.VMEM((tokens, width), BF16),
            pltpu.VMEM((width, hidden), BF16),
            pltpu.VMEM((width, width), BF16),
        ),
        flops=10 * half,
    )
    return pieces, dh1, dmix, vec, uvec


def qkv_back(act, code, dh1, dmix, saved, w, length, images):
    (ag, ac, qkvw, qb, vb, pw, pb, mg, mc, uw, ub, dw, db) = w
    (x, n1, qkv, probs, mixed, h1, n2, slope, gact) = saved
    tokens, width = x.shape
    half = width * width * tokens * 2
    (dj,) = call(
        functools.partial(attend_back_kernel, length, images),
        (act, qkv, probs, mixed, dmix),
        (shaped(tokens, 3 * width),),
        flops=4 * half,
    )
    *pieces, dx, vec = call(
        functools.partial(qkv_back_kernel, length, images),
        (act, code, x, n1, dj, qkvw, ag, dh1),
        (
            *piece_shapes(3 * width // CHUNKS, width),
            shaped(tokens, width),
            shaped(8, width, dtype=F32),
        ),
        scratch=(pltpu.VMEM((width, 3 * width), BF16),),
        flops=6 * half,
    )
    return pieces, dx, vec


def orders(bits):
    if bits == 4:
        return ((0, 1, 2, 3), (1, 0, 2, 3), (2, 3, 0, 1))
    plain = tuple(range(bits))
    return (plain, plain, plain)


def flipped(block, bit, sections, size):
    route = [(s * size + i, s * size + (i ^ (1 << bit))) for s in sections for i in range(size)]
    return lax.ppermute(block, ("section", "dp"), route)


def chunk_code(order, place):
    code = jnp.zeros((), jnp.int32)
    for k, bit in enumerate(order):
        code = code + (((place >> bit) & 1) << (len(order) - 1 - k))
    return code


def reduce_parts(pieces, order, sections, size):
    unit = pieces[-1].shape[0]
    if size != CHUNKS:
        whole = lax.psum(jnp.concatenate(pieces[::-1]), "dp")
        return whole[: 8 * unit], whole[8 * unit :]
    arrived = []
    for k in range(4):
        count = unit * (8 >> k)
        part = pieces[k]
        if arrived:
            total = part.astype(F32)
            for r in arrived:
                total = total + r[count : 2 * count].astype(F32)
            part = total.astype(BF16)
        arrived.append(flipped(part, order[k], sections, size))
    total = pieces[4].astype(F32)
    for r in arrived:
        total = total + r[:unit].astype(F32)
    have = total.astype(BF16)
    for k in (3, 2, 1):
        have = jnp.concatenate([have, flipped(have, order[k], sections, size)])
    return have, flipped(have, order[0], sections, size)


def settle(code, use, sets, blocks, shapes):
    unit = sets[0][0].shape[0] // 8
    width = sets[0][0].shape[1]
    rows = unit // sum(blocks)

    def body(scalars, *refs):
        ins, outs = refs[:4], refs[4:]
        j = pl.program_id(0)
        for s in range(2):
            for h in range(2):

                @pl.when((scalars[1] == s) & ((j >= 8) == (h == 1)))
                def _(src=ins[2 * s + h]):
                    at = 0
                    for count, out in zip(blocks, outs):
                        for b in range(count):
                            out[:, b * width : (b + 1) * width] = src[at : at + rows, :].astype(F32)
                            at += rows

    lower = pl.BlockSpec((unit, width), lambda j, s: (jnp.minimum(j, 7), 0))
    upper = pl.BlockSpec((unit, width), lambda j, s: (jnp.maximum(j - 8, 0), 0))
    outs = [shaped(*s, dtype=F32) for s in shapes]
    out_specs = [
        pl.BlockSpec((rows, count * width), lambda j, s: (jnp.bitwise_xor(s[0], j), 0))
        for count in blocks
    ]
    moved = sum(o.size * 4 for o in outs) * 2
    return pl.pallas_call(
        body,
        out_shape=outs,
        grid_spec=pltpu.PrefetchScalarGridSpec(
            num_scalar_prefetch=1,
            grid=(CHUNKS,),
            in_specs=[lower, upper, lower, upper],
            out_specs=out_specs,
        ),
        compiler_params=pltpu.CompilerParams(vmem_limit_bytes=16 << 20),
        cost_estimate=pl.CostEstimate(flops=0, bytes_accessed=moved, transcendentals=0),
    )(jnp.stack([code, use]), *sets[0], *sets[1])


def per_device(size, ends, counts, keep, *params):
    w = [item if item.ndim == 2 else item[0] for item in params]
    section = lax.axis_index("section")
    place = lax.axis_index("dp")
    first = section == 0
    images, slots, width = ends.shape[1:]
    hidden = w[9].shape[1]
    length = -(-slots // 32) * 32
    padded = ((0, 0), (0, length - slots), (0, 0))
    bits = size.bit_length() - 1
    ways = orders(bits)
    if size == CHUNKS:
        codes = [chunk_code(o, place) for o in ways]
    else:
        codes = [jnp.zeros((), jnp.int32)] * 3
    acts = [(section == s).astype(jnp.int32).reshape(1) for s in (0, 1)]
    keeping = (keep[0].astype(F32) * KEEP_SCALE).reshape(-1)
    live = (jnp.arange(slots)[None, :] < counts[:, None])[..., None]

    x0 = jnp.pad(ends[0], padded).reshape(images * length, width)
    seed1 = jnp.pad(jnp.where(live, ends[0], jnp.zeros((), BF16)), padded)
    seed1 = seed1.reshape(images * length, width)

    def crossed(block, source):
        route = [(source * size + i, (1 - source) * size + i) for i in range(size)]
        return lax.ppermute(block, ("section", "dp"), route)

    out0, stats0, saved0 = forward(acts[0], counts, keeping, x0, w, length, images)
    x1 = crossed(out0, 0)
    out1, stats1, saved1 = forward(acts[1], counts, keeping, x1, w, length, images)

    def backward(which, seed, saved):
        act = acts[which]
        scalar = [c.reshape(1) for c in codes]
        pa, du, va = down_back(act, scalar[0], keeping, seed, saved, w, length, images)
        ra = reduce_parts(pa, ways[0], (which,), size)
        pb, dh1, dmix, vb, uvec = up_back(
            act, scalar[1], keeping, seed, du, saved, w, length, images
        )
        rb = reduce_parts(pb, ways[1], (which,), size)
        pc, dx, vc = qkv_back(act, scalar[2], dh1, dmix, saved, w, length, images)
        rc = reduce_parts(pc, ways[2], (which,), size)
        vec = jnp.concatenate([vc[:4], vb[:3], va[:1], uvec.reshape(-1, width)])
        return dx, vec, (ra, rb, rc)

    dx1, vec1, red1 = backward(1, seed1, saved1)
    seed0 = crossed(dx1, 1)
    dx0, vec0, red0 = backward(0, seed0, saved0)

    stats = jnp.where(first, stats0, stats1)
    extra = jnp.concatenate([stats, jnp.sum(counts.astype(F32)).reshape(1)])
    extra = jnp.pad(extra, (0, width - 4)).reshape(1, width)
    vec = jnp.concatenate([jnp.where(first, vec0, vec1), extra])
    for bit in range(bits):
        vec = vec + flipped(vec, bit, (0, 1), size)

    use = section.astype(jnp.int32)
    blocks = hidden // width
    (g_down,) = settle(codes[0], use, (red0[0], red1[0]), (1,), [(hidden, width)])
    g_up, g_proj = settle(
        codes[1], use, (red0[1], red1[1]), (blocks, 1), [(width, hidden), (width, width)]
    )
    (g_qkv,) = settle(codes[2], use, (red0[2], red1[2]), (3,), [(width, 3 * width)])

    shown = jnp.where(first, dx0, out1).reshape(images, length, width)[:, :slots]
    shown = jnp.where(live, shown, jnp.zeros((), BF16))[None]
    rms = jnp.sqrt(vec[-1, 0:3] / (vec[-1, 3] * width)).reshape(1, 3)
    row = lambda k: vec[k : k + 1]
    g_ub = vec[8 : 8 + blocks].reshape(1, hidden)
    return (
        shown,
        row(0),
        row(1),
        g_qkv[None],
        row(2),
        row(3),
        g_proj[None],
        row(6),
        row(4),
        row(5),
        g_up[None],
        g_ub,
        g_down[None],
        row(7),
        rms,
    )


def solution(mesh):
    flat = P("section", None)
    deep = P("section", None, None)
    split = P("section", "dp", None, None)
    ranks = (flat, flat, deep, flat, flat, deep, flat, flat, flat, deep, flat, deep, flat)
    return jax.shard_map(
        functools.partial(per_device, mesh.shape["dp"]),
        mesh=mesh,
        in_specs=(split, P("dp"), P("section", "dp", None), *ranks),
        out_specs=(split, *ranks, flat),
        check_vma=False,
    )
```

time: 1340 us -> 691 us (0.52)
  matrix products: 381 us -> 0 us
  waiting for transfers between devices: 586 us -> 268 us
  Pallas kernels: 0 us -> 213 us
  starting transfers between devices: 10 us -> 131 us
  local copies, waits for them, and re-layouts: 133 us -> 35.6 us
  other arithmetic: 117 us -> 30.4 us
  blocking collectives: 83.8 us -> 0 us
  between operations: 18.2 us -> 3.44 us
    psum x1 -> x0, waiting for transfers between devices: 585 us -> none  [per_device(): lax.psum((accum[0], accum[1], accum[2], accum[3], accum[4], accum[5], acc...]
    dot_general x88 -> x0, matrix products: 381 us -> none  [the longest x4 81.1 us: layer_forward(): jnp.einsum('bsf,fd->bsd', active, down_weight, preferred_element_type=jnp...]
    ppermute x6 -> x54, waiting for transfers between devices: 0.02 us -> 268 us  [the longest x52 200 us: flipped(): return lax.ppermute(block, ('section', 'dp'), route)]
    pallas_call x0 -> x19, Pallas kernels: none -> 213 us  [the longest x16 190 us: call(): pl.pallas_call(body, out_shape=list(outs), in_specs=in_specs, out_specs=o...]
    ppermute x6 -> x54, starting transfers between devices: 10 us -> 131 us  [the longest x52 128 us: flipped(): return lax.ppermute(block, ('section', 'dp'), route)]
    psum x1 -> x0, blocking collectives: 83.8 us -> none  [per_device(): lax.psum((accum[0], accum[1], accum[2], accum[3], accum[4], accum[5], acc...]
    reduce_sum x37 -> x1, other arithmetic: 47.7 us -> 0.6 us  [per_device(): extra = jnp.concatenate([stats, jnp.sum(counts.astype(F32)).reshape(1)])]
    convert_element_type x20 -> x0, local copies, waits for them, and re-layouts: 41.6 us -> none  [the longest x8 16.7 us: layer_forward(): value_rows = (joined[..., 2 * width:] + value_bias).astype(jnp.bfloat16)]
  transfers between devices with their start and end apart: 7 -> 54, of which waited for: 1 -> 15; matrix products, arithmetic and copies ran while one was open for 14% -> 6% of each run, Pallas kernels for 0% -> 15%
where the time goes in v1:
time: 691 us; the launch traced here: 682 us
  waiting for transfers between devices  268 us (39%)
  Pallas kernels  213 us (31%)
  starting transfers between devices  131 us (19%)
  local copies, waits for them, and re-layouts  35.6 us (5%)
  other arithmetic  30.4 us (4%)
    ppermute x52, waiting for transfers between devices, flipped(): return lax.ppermute(block, ('section', 'dp'), route)  200 us
    pallas_call x16, Pallas kernels, call(): pl.pallas_call(body, out_shape=list(outs), in_specs=in_specs, out_specs=o...  190 us
    ppermute x52, starting transfers between devices, flipped(): return lax.ppermute(block, ('section', 'dp'), route)  128 us
    ppermute x2, waiting for transfers between devices, crossed(): return lax.ppermute(block, ('section', 'dp'), route)  67.9 us
    unnamed x178, local copies, waits for them, and re-layouts  25.4 us
    pallas_call x3, Pallas kernels, settle(): pl.pallas_call(body, out_shape=outs, grid_spec=pltpu.PrefetchScalarGridSp...  23.1 us
    convert_element_type x18, other arithmetic, reduce_parts(): part = total.astype(BF16)  14.6 us
  transfers between devices with their start and end apart: 54, of which 15 were waited for; matrix products, arithmetic and copies ran while one was open for 6% of the time, Pallas kernels for 15%

profile of v1, /device:TPU:0, one launch (start us, length us, event | category | flops | bytes accessed | tf_op | source)
XLA Modules:
  0.0 681.7 jit_solution(9560463465390167292)
XLA Ops:
  5.0 8.1 %shard_map.271 = (bf16[864,768]{1,0:T(8,128)(2,1)S(1)}, bf16[864,2304]{1,0:T(8,128)(2,1)}) custom-call(s32[1]{0:T(128)} %bitcast.act, bf16[864,768]{1,0:T(8,128)(2,1)S(1)} %bitcast.29, f32[1,768]{1,0:T(1,128)S(1)} %copy-done.67, f32[1,768]{1,0:T(1,128)S(1)} %copy-done.58, bf16[768,2304]{1,0:T(8,128)(2,1)S(1)} %bitcast.38, f32[1,768]{1,0:T(1,128)S(1)} %copy-done.59, ...), custom_call_target="tpu_custom_call" | custom-call | flops 3057647616 | bytes 10186756 | tf_op jit(solution)/shard_map/pallas_call | solution.py:39
  16.4 17.0 %shard_map.272 = (bf16[10368,288]{1,0:T(8,128)(2,1)}, bf16[864,768]{1,0:T(8,128)(2,1)S(1)}) custom-call(s32[1]{0:T(128)} %bitcast.act, s32[3]{0:T(128)S(1)} %copy-done.45, bf16[864,2304]{1,0:T(8,128)(2,1)S(1)} %copy-done), custom_call_target="tpu_custom_call" | custom-call | flops 2038431744 | bytes 11280400 | tf_op jit(solution)/shard_map/pallas_call | solution.py:39
  33.4 19.1 %shard_map.273 = (f32[864,768]{1,0:T(8,128)}, bf16[864,768]{1,0:T(8,128)(2,1)S(1)}, bf16[864,3072]{1,0:T(8,128)(2,1)}, bf16[864,3072]{1,0:T(8,128)(2,1)}, f32[8]{0:T(128)S(1)}) custom-call(s32[1]{0:T(128)} %bitcast.act, f32[6]{0:T(128)S(1)} %mul.14.keep, s32[3]{0:T(128)S(1)} %copy-done.45, bf16[864,768]{1,0:T(8,128)(2,1)S(1)} %bitcast.30, ...), custom_call_target="tpu_custom_call" | custom-call | flops 5096079360 | bytes 23172168 | tf_op jit(solution)/shard_map/pallas_call | solution.py:39
  55.4 12.3 %shard_map.274 = (bf16[864,768]{1,0:T(8,128)(2,1)}, f32[8]{0:T(128)S(1)}) custom-call(s32[1]{0:T(128)} %bitcast.act, f32[6]{0:T(128)S(1)} %mul.14.keep, s32[3]{0:T(128)S(1)} %copy-done.45, f32[864,768]{1,0:T(8,128)S(1)} %copy-done.70, bf16[864,3072]{1,0:T(8,128)(2,1)} %get-tuple-element.90.gact, bf16[3072,768]{1,0:T(8,128)(2,1)} %bitcast.50, ...), custom_call_target="tpu_custom_call" | custom-call | flops 4076863488 | bytes 14011464 | tf_op jit(solution)/shard_map/pallas_call | solution.py:39
  83.3 8.0 %shard_map.277 = (f32[864,768]{1,0:T(8,128)}, bf16[864,768]{1,0:T(8,128)(2,1)S(1)}, bf16[864,3072]{1,0:T(8,128)(2,1)}, bf16[864,3072]{1,0:T(8,128)(2,1)}, f32[8]{0:T(128)S(1)}) custom-call(s32[1]{0:T(128)} %bitcast.6.act, f32[6]{0:T(128)S(1)} %mul.14.keep, s32[3]{0:T(128)S(1)} %copy-done.45, bf16[864,768]{1,0:T(8,128)(2,1)} %collective-permute-done.x, ...), custom_call_target="tpu_custom_call" | custom-call | flops 5096079360 | bytes 23172168 | tf_op jit(solution)/shard_map/pallas_call | solution.py:39
  91.3 8.4 %shard_map.278 = (bf16[1536,768]{1,0:T(8,128)(2,1)S(1)}, bf16[768,768]{1,0:T(8,128)(2,1)S(1)}, bf16[384,768]{1,0:T(8,128)(2,1)S(1)}, bf16[192,768]{1,0:T(8,128)(...) custom-call(s32[1]{0:T(128)} %bitcast.6.act, s32[1]{0:T(128)} %bitcast.11.code, ...), custom_call_target="tpu_custom_call" | custom-call | flops 8153726976 | bytes 26714144 | tf_op jit(solution)/shard_map/pallas_call | solution.py:39
  104.5 8.4 %shard_map.279 = (bf16[1920,768]{1,0:T(8,128)(2,1)}, bf16[960,768]{1,0:T(8,128)(2,1)}, bf16[480,768]{1,0:T(8,128)(2,1)S(1)}, bf16[240,768]{1,0:T(8,128)(2,1)S(1)...) custom-call(s32[1]{0:T(128)} %bitcast.6.act, ...), custom_call_target="tpu_custom_call" | custom-call | flops 10192158720 | bytes 27761696 | tf_op jit(solution)/shard_map/pallas_call | solution.py:39
  113.0 6.9 %shard_map.280.dj = bf16[864,2304]{1,0:T(8,128)(2,1)} custom-call(s32[1]{0:T(128)} %bitcast.6.act, bf16[864,2304]{1,0:T(8,128)(2,1)} %get-tuple-element.93.qkv, bf16[10368,288]{1,0:T(8,128)(2,1)} %get-tuple-element.94.probs, bf16[864,768]{1,0:T(8,128)(2,1)S(1)} %copy-done.5, bf16[864,768]{1,0:T(8,128)(2,1)S(1)} %get-tuple-element.101.dmix), custom_call_target="tpu_custom_call" | custom-call | flops 4076863488 | bytes 16588804 | tf_op jit(solution)/shard_map/pallas_call | solution.py:39
  119.9 6.5 shard_map.281
  150.1 66.6 %collective-permute-done.1.dh2 = bf16[864,768]{1,0:T(8,128)(2,1)} collective-permute-done((bf16[864,768]{1,0:T(8,128)(2,1)}, bf16[864,768]{1,0:T(8,128)(2,1)}, u32[]{:S(2)}, u32[]{:S(2)}) %collective-permute-start.1) | collective-permute-done | bytes 1327136 | tf_op jit(solution)/shard_map/ppermute | solution.py:599
  216.8 22.1 %shard_map.282 = (bf16[1536,768]{1,0:T(8,128)(2,1)S(1)}, bf16[768,768]{1,0:T(8,128)(2,1)S(1)}, bf16[384,768]{1,0:T(8,128)(2,1)S(1)}, bf16[192,768]{1,0:T(8,128)(...) custom-call(s32[1]{0:T(128)} %bitcast.act, s32[1]{0:T(128)} %bitcast.11.code, ...), custom_call_target="tpu_custom_call" | custom-call | flops 8153726976 | bytes 26714144 | tf_op jit(solution)/shard_map/pallas_call | solution.py:39
  243.6 25.7 %shard_map.283 = (bf16[1920,768]{1,0:T(8,128)(2,1)}, bf16[960,768]{1,0:T(8,128)(2,1)}, bf16[480,768]{1,0:T(8,128)(2,1)S(1)}, bf16[240,768]{1,0:T(8,128)(2,1)S(1)...) custom-call(s32[1]{0:T(128)} %bitcast.act, ...), custom_call_target="tpu_custom_call" | custom-call | flops 10192158720 | bytes 27761696 | tf_op jit(solution)/shard_map/pallas_call | solution.py:39
  269.3 20.5 %shard_map.284.dj = bf16[864,2304]{1,0:T(8,128)(2,1)} custom-call(s32[1]{0:T(128)} %bitcast.act, bf16[864,2304]{1,0:T(8,128)(2,1)} %get-tuple-element.86.qkv, bf16[10368,288]{1,0:T(8,128)(2,1)} %get-tuple-element.87.probs, bf16[864,768]{1,0:T(8,128)(2,1)S(1)} %copy-done.3, bf16[864,768]{1,0:T(8,128)(2,1)S(1)} %get-tuple-element.107.dmix), custom_call_target="tpu_custom_call" | custom-call | flops 4076863488 | bytes 16588804 | tf_op jit(solution)/shard_map/pallas_call | solution.py:39
  294.3 15.5 %shard_map.285 = (bf16[1152,768]{1,0:T(8,128)(2,1)}, bf16[576,768]{1,0:T(8,128)(2,1)S(1)}, bf16[288,768]{1,0:T(8,128)(2,1)S(1)}, bf16[144,768]{1,0:T(8,128)(2,1)...) custom-call(s32[1]{0:T(128)} %bitcast.act, s32[1]{0:T(128)} %bitcast.1.code, ...), custom_call_target="tpu_custom_call" | custom-call | flops 6115295232 | bytes 17722376 | tf_op jit(solution)/shard_map/pallas_call | solution.py:39
  319.5 46.3 %collective-permute-done.3 = f32[13,768]{1,0:T(8,128)S(1)} collective-permute-done((f32[13,768]{1,0:T(8,128)S(1)}, f32[13,768]{1,0:T(8,128)S(1)}, u32[]{:S(2)}, u32[]{:S(2)}) %collective-permute-start.3) | collective-permute-done | bytes 39968 | tf_op jit(solution)/shard_map/ppermute | solution.py:499
  381.9 24.2 %collective-permute-done.6 = bf16[1152,768]{1,0:T(8,128)(2,1)S(1)} collective-permute-done((bf16[1152,768]{1,0:T(8,128)(2,1)}, bf16[1152,768]{1,0:T(8,128)(2,1)S(1)}, u32[]{:S(2)}, u32[]{:S(2)}) %collective-permute-start.6) | collective-permute-done | bytes 1769504 | tf_op jit(solution)/shard_map/ppermute | solution.py:499
  407.0 5.7 collective-permute-start.7
  423.3 30.9 %collective-permute-done.7 = bf16[576,768]{1,0:T(8,128)(2,1)S(1)} collective-permute-done((bf16[576,768]{1,0:T(8,128)(2,1)S(1)}, bf16[576,768]{1,0:T(8,128)(2,1)S(1)}, u32[]{:S(2)}, u32[]{:S(2)}) %collective-permute-start.7) | collective-permute-done | bytes 884768 | tf_op jit(solution)/shard_map/ppermute | solution.py:499
  455.1 6.1 collective-permute-start.39
  476.8 12.1 %collective-permute-done.24 = bf16[480,768]{1,0:T(8,128)(2,1)S(1)} collective-permute-done((bf16[480,768]{1,0:T(8,128)(2,1)S(1)}, bf16[480,768]{1,0:T(8,128)(2,1)S(1)}, u32[]{:S(2)}, u32[]{:S(2)}) %collective-permute-start.24) | collective-permute-done | bytes 737312 | tf_op jit(solution)/shard_map/ppermute | solution.py:499
  491.1 8.6 %collective-permute-start.25 = (bf16[240,768]{1,0:T(8,128)(2,1)S(1)}, bf16[240,768]{1,0:T(8,128)(2,1)S(1)}, u32[]{:S(2)}, u32[]{:S(2)}) collective-permute-start(bf16[240,768]{1,0:T(8,128)(2,1)S(1)} %add_convert_fusion.15), channel_id=1, source_target_pairs={{0,8},{1,9},{2,10},{3,11},{4,12},{5,13},{6,14},{7,15},{8,0},{9,1},... | collective-permute-start | bytes 1105928 | tf_op jit(solution)/shard_map/ppermute | solution.py:499
  501.8 6.5 collective-permute-done.25
  510.5 5.3 collective-permute-start.26
  526.3 7.3 %collective-permute-start.27 = (bf16[480,768]{1,0:T(8,128)(2,1)S(1)}, bf16[480,768]{1,0:T(8,128)(2,1)S(1)}, u32[]{:S(2)}, u32[]{:S(2)}) collective-permute-start(bf16[480,768]{1,0:T(8,128)(2,1)S(1)} %pad_maximum_fusion.12), channel_id=1, source_target_pairs={{0,4},{1,5},{2,6},{3,7},{4,0},{5,1},{6,2},{7,3},{8,12},{9,13},{10,... | collective-permute-start | bytes 2211848 | tf_op jit(solution)/shard_map/ppermute | solution.py:499
  544.7 10.0 %collective-permute-done.27 = bf16[480,768]{1,0:T(8,128)(2,1)S(1)} collective-permute-done((bf16[480,768]{1,0:T(8,128)(2,1)S(1)}, bf16[480,768]{1,0:T(8,128)(2,1)S(1)}, u32[]{:S(2)}, u32[]{:S(2)}) %collective-permute-start.27) | collective-permute-done | bytes 737312 | tf_op jit(solution)/shard_map/ppermute | solution.py:499
  576.7 26.2 %collective-permute-done.11 = bf16[288,768]{1,0:T(8,128)(2,1)S(1)} collective-permute-done((bf16[288,768]{1,0:T(8,128)(2,1)S(1)}, bf16[288,768]{1,0:T(8,128)(2,1)S(1)}, u32[]{:S(2)}, u32[]{:S(2)}) %collective-permute-start.11) | collective-permute-done | bytes 442400 | tf_op jit(solution)/shard_map/ppermute | solution.py:499
  603.8 5.5 collective-permute-start.12
  614.8 16.0 %collective-permute-done.5 = f32[13,768]{1,0:T(8,128)S(1)} collective-permute-done((f32[13,768]{1,0:T(8,128)S(1)}, f32[13,768]{1,0:T(8,128)S(1)}, u32[]{:S(2)}, u32[]{:S(2)}) %collective-permute-start.5) | collective-permute-done | bytes 39968 | tf_op jit(solution)/shard_map/ppermute | solution.py:499
  640.8 17.3 %collective-permute-done.13.refs_1_ = bf16[1152,768]{1,0:T(8,128)(2,1)S(1)} collective-permute-done((bf16[1152,768]{1,0:T(8,128)(2,1)S(1)}, bf16[1152,768]{1,0:T(8,128)(2,1)S(1)}, u32[]{:S(2)}, u32[]{:S(2)}) %collective-permute-start.13) | collective-permute-done | bytes 1769504 | tf_op jit(solution)/shard_map/ppermute | solution.py:499
  658.1 7.2 %shard_map.287 = f32[768,2304]{1,0:T(8,128)} custom-call(s32[2]{0:T(128)S(1)} %pad_add_fusion.scalars, bf16[1152,768]{1,0:T(8,128)(2,1)S(1)} %pad_maximum_fusion.4.refs_0_, bf16[1152,768]{1,0:T(8,128)(2,1)S(1)} %collective-permute-done.13.refs_1_, bf16[1152,768]{1,0:T(8,128)(2,1)S(1)} %pad_maximum_fusion.5.refs_2_, ...), custom_call_target="tpu_custom_call" | custom-call | bytes 14155776 | tf_op jit(solution)/shard_map/pallas_call | solution.py:560
  665.3 7.8 %shard_map.289 = f32[3072,768]{1,0:T(8,128)} custom-call(s32[2]{0:T(128)S(1)} %pad_add_fusion.2.scalars, bf16[1536,768]{1,0:T(8,128)(2,1)S(1)} %pad_maximum_fusion.2.refs_0_, bf16[1536,768]{1,0:T(8,128)(2,1)S(1)} %collective-permute-done.45.refs_1_, bf16[1536,768]{1,0:T(8,128)(2,1)S(1)} %pad_maximum_fusion.3.refs_2_, ...), custom_call_target="tpu_custom_call" | custom-call | bytes 18874368 | tf_op jit(solution)/shard_map/pallas_call | solution.py:560
  673.1 8.1 %shard_map.288 = (f32[768,3072]{1,0:T(8,128)}, f32[768,768]{1,0:T(8,128)}) custom-call(s32[2]{0:T(128)S(1)} %pad_add_fusion.1.scalars, bf16[1920,768]{1,0:T(8,128)(2,1)S(1)} %pad_maximum_fusion.refs_0_, bf16[1920,768]{1,0:T(8,128)(2,1)S(1)} %collective-permute-done.29.refs_1_, bf16[1920,768]{1,0:T(8,128)(2,1)S(1)} %pad_maximum_fusion.1.refs_2_, ...), custom_call_target="tpu_custom_call" | custom-call | bytes 23592960 | tf_op jit(solution)/shard_map/pallas_call | solution.py:560
  (353 shorter events, 181.8 us)
Async XLA Ops:
  127.2 89.6 %collective-permute-start.1 = (bf16[864,768]{1,0:T(8,128)(2,1)}, bf16[864,768]{1,0:T(8,128)(2,1)}, u32[]{:S(2)}, u32[]{:S(2)}) collective-permute-start(bf16[864,768]{1,0:T(8,128)(2,1)} %get-tuple-element.103), channel_id=1, source_target_pairs={{16,0},{17,1},{18,2},{19,3},{20,4},{21,5},{22,6},{23,7},{24,8},{25... | collective-permute-start | bytes 3981320 | tf_op jit(solution)/shard_map/ppermute | solution.py:599
  143.9 172.9 %collective-permute-start.14 = (bf16[1152,768]{1,0:T(8,128)(2,1)}, bf16[1152,768]{1,0:T(8,128)(2,1)}, u32[]{:S(2)}, u32[]{:S(2)}) collective-permute-start(bf16[1152,768]{1,0:T(8,128)(2,1)} %get-tuple-element.129), channel_id=1, source_target_pairs={{16,20},{17,21},{18,22},{19,23},{20,16},{21,17},{22,18},{23,19},{2... | collective-permute-start | bytes 5308424 | tf_op jit(solution)/shard_map/ppermute | solution.py:499
  145.7 229.2 %collective-permute-start.46 = (bf16[1536,768]{1,0:T(8,128)(2,1)}, bf16[1536,768]{1,0:T(8,128)(2,1)}, u32[]{:S(2)}, u32[]{:S(2)}) collective-permute-start(bf16[1536,768]{1,0:T(8,128)(2,1)} %copy-done.51), channel_id=1, source_target_pairs={{16,17},{17,16},{18,19},{19,18},{20,21},{21,20},{22,23},{23,22},{2... | collective-permute-start | bytes 7077896 | tf_op jit(solution)/shard_map/ppermute | solution.py:499
  147.8 229.5 %collective-permute-start.30 = (bf16[1920,768]{1,0:T(8,128)(2,1)}, bf16[1920,768]{1,0:T(8,128)(2,1)}, u32[]{:S(2)}, u32[]{:S(2)}) collective-permute-start(bf16[1920,768]{1,0:T(8,128)(2,1)} %get-tuple-element.139), channel_id=1, source_target_pairs={{16,18},{17,19},{18,16},{19,17},{20,22},{21,23},{22,20},{23,21},{2... | collective-permute-start | bytes 8847368 | tf_op jit(solution)/shard_map/ppermute | solution.py:499
  309.9 103.9 %collective-permute-start.22 = (bf16[1920,768]{1,0:T(8,128)(2,1)}, bf16[1920,768]{1,0:T(8,128)(2,1)S(1)}, u32[]{:S(2)}, u32[]{:S(2)}) collective-permute-start(bf16[1920,768]{1,0:T(8,128)(2,1)} %get-tuple-element.134), channel_id=1, source_target_pairs={{0,2},{1,3},{2,0},{3,1},{4,6},{5,7},{6,4},{7,5},{8,10},{9,11},{10,... | collective-permute-start | bytes 8847368 | tf_op jit(solution)/shard_map/ppermute | solution.py:499
  318.2 52.1 %collective-permute-start.15 = (bf16[576,768]{1,0:T(8,128)(2,1)S(1)}, bf16[576,768]{1,0:T(8,128)(2,1)S(1)}, u32[]{:S(2)}, u32[]{:S(2)}) collective-permute-start(bf16[576,768]{1,0:T(8,128)(2,1)S(1)} %add_convert_fusion.4), channel_id=1, source_target_pairs={{16,24},{17,25},{18,26},{19,27},{20,28},{21,29},{22,30},{23,31},{2... | collective-permute-start | bytes 2654216 | tf_op jit(solution)/shard_map/ppermute | solution.py:499
  319.3 46.5 %collective-permute-start.3 = (f32[13,768]{1,0:T(8,128)S(1)}, f32[13,768]{1,0:T(8,128)S(1)}, u32[]{:S(2)}, u32[]{:S(2)}) collective-permute-start(f32[13,768]{1,0:T(8,128)S(1)} %fusion.5), channel_id=1, source_target_pairs={{0,2},{1,3},{2,0},{3,1},{4,6},{5,7},{6,4},{7,5},{8,10},{9,11},{10,... | collective-permute-start | bytes 119816 | tf_op jit(solution)/shard_map/ppermute | solution.py:499
  365.8 40.3 %collective-permute-start.6 = (bf16[1152,768]{1,0:T(8,128)(2,1)}, bf16[1152,768]{1,0:T(8,128)(2,1)S(1)}, u32[]{:S(2)}, u32[]{:S(2)}) collective-permute-start(bf16[1152,768]{1,0:T(8,128)(2,1)} %get-tuple-element.124), channel_id=1, source_target_pairs={{0,4},{1,5},{2,6},{3,7},{4,0},{5,1},{6,2},{7,3},{8,12},{9,13},{10,... | collective-permute-start | bytes 5308424 | tf_op jit(solution)/shard_map/ppermute | solution.py:499
  370.3 52.0 %collective-permute-start.38 = (bf16[1536,768]{1,0:T(8,128)(2,1)S(1)}, bf16[1536,768]{1,0:T(8,128)(2,1)S(1)}, u32[]{:S(2)}, u32[]{:S(2)}) collective-permute-start(bf16[1536,768]{1,0:T(8,128)(2,1)S(1)} %copy-done.53), channel_id=1, source_target_pairs={{0,1},{1,0},{2,3},{3,2},{4,5},{5,4},{6,7},{7,6},{8,9},{9,8},{10,11... | collective-permute-start | bytes 7077896 | tf_op jit(solution)/shard_map/ppermute | solution.py:499
  377.4 37.6 %collective-permute-start.47 = (bf16[768,768]{1,0:T(8,128)(2,1)S(1)}, bf16[768,768]{1,0:T(8,128)(2,1)S(1)}, u32[]{:S(2)}, u32[]{:S(2)}) collective-permute-start(bf16[768,768]{1,0:T(8,128)(2,1)S(1)} %add_convert_fusion.2), channel_id=1, source_target_pairs={{16,18},{17,19},{18,16},{19,17},{20,22},{21,23},{22,20},{23,21},{2... | collective-permute-start | bytes 3538952 | tf_op jit(solution)/shard_map/ppermute | solution.py:499
  380.0 81.4 %collective-permute-start.31 = (bf16[960,768]{1,0:T(8,128)(2,1)S(1)}, bf16[960,768]{1,0:T(8,128)(2,1)S(1)}, u32[]{:S(2)}, u32[]{:S(2)}) collective-permute-start(bf16[960,768]{1,0:T(8,128)(2,1)S(1)} %add_convert_fusion), channel_id=1, source_target_pairs={{16,17},{17,16},{18,19},{19,18},{20,21},{21,20},{22,23},{23,22},{2... | collective-permute-start | bytes 4423688 | tf_op jit(solution)/shard_map/ppermute | solution.py:499
  407.0 47.3 %collective-permute-start.7 = (bf16[576,768]{1,0:T(8,128)(2,1)S(1)}, bf16[576,768]{1,0:T(8,128)(2,1)S(1)}, u32[]{:S(2)}, u32[]{:S(2)}) collective-permute-start(bf16[576,768]{1,0:T(8,128)(2,1)S(1)} %add_convert_fusion.5), channel_id=1, source_target_pairs={{0,8},{1,9},{2,10},{3,11},{4,12},{5,13},{6,14},{7,15},{8,0},{9,1},... | collective-permute-start | bytes 2654216 | tf_op jit(solution)/shard_map/ppermute | solution.py:499
  414.9 53.2 %collective-permute-start.23 = (bf16[960,768]{1,0:T(8,128)(2,1)S(1)}, bf16[960,768]{1,0:T(8,128)(2,1)S(1)}, u32[]{:S(2)}, u32[]{:S(2)}) collective-permute-start(bf16[960,768]{1,0:T(8,128)(2,1)S(1)} %add_convert_fusion.1), channel_id=1, source_target_pairs={{0,1},{1,0},{2,3},{3,2},{4,5},{5,4},{6,7},{7,6},{8,9},{9,8},{10,11... | collective-permute-start | bytes 4423688 | tf_op jit(solution)/shard_map/ppermute | solution.py:499
  419.8 121.0 %collective-permute-start.4 = (f32[13,768]{1,0:T(8,128)S(1)}, f32[13,768]{1,0:T(8,128)S(1)}, u32[]{:S(2)}, u32[]{:S(2)}) collective-permute-start(f32[13,768]{1,0:T(8,128)S(1)} %add.235), channel_id=1, source_target_pairs={{0,4},{1,5},{2,6},{3,7},{4,0},{5,1},{6,2},{7,3},{8,12},{9,13},{10,... | collective-permute-start | bytes 119816 | tf_op jit(solution)/shard_map/ppermute | solution.py:499
  422.3 32.9 %collective-permute-start.19 = (bf16[288,768]{1,0:T(8,128)(2,1)S(1)}, bf16[288,768]{1,0:T(8,128)(2,1)S(1)}, u32[]{:S(2)}, u32[]{:S(2)}) collective-permute-start(bf16[288,768]{1,0:T(8,128)(2,1)S(1)} %pad_maximum_fusion.17), channel_id=1, source_target_pairs={{16,17},{17,16},{18,19},{19,18},{20,21},{21,20},{22,23},{23,22},{2... | collective-permute-start | bytes 1327112 | tf_op jit(solution)/shard_map/ppermute | solution.py:499
  461.4 39.6 %collective-permute-start.8 = (bf16[288,768]{1,0:T(8,128)(2,1)S(1)}, bf16[288,768]{1,0:T(8,128)(2,1)S(1)}, u32[]{:S(2)}, u32[]{:S(2)}) collective-permute-start(bf16[288,768]{1,0:T(8,128)(2,1)S(1)} %add_convert_fusion.11), channel_id=1, source_target_pairs={{0,1},{1,0},{2,3},{3,2},{4,5},{5,4},{6,7},{7,6},{8,9},{9,8},{10,11... | collective-permute-start | bytes 1327112 | tf_op jit(solution)/shard_map/ppermute | solution.py:499
  473.9 98.8 %collective-permute-start.20 = (bf16[576,768]{1,0:T(8,128)(2,1)S(1)}, bf16[576,768]{1,0:T(8,128)(2,1)S(1)}, u32[]{:S(2)}, u32[]{:S(2)}) collective-permute-start(bf16[576,768]{1,0:T(8,128)(2,1)S(1)} %pad_maximum_fusion.11), channel_id=1, source_target_pairs={{16,24},{17,25},{18,26},{19,27},{20,28},{21,29},{22,30},{23,31},{2... | collective-permute-start | bytes 2654216 | tf_op jit(solution)/shard_map/ppermute | solution.py:499
  488.9 26.9 %collective-permute-start.40 = (bf16[384,768]{1,0:T(8,128)(2,1)S(1)}, bf16[384,768]{1,0:T(8,128)(2,1)S(1)}, u32[]{:S(2)}, u32[]{:S(2)}) collective-permute-start(bf16[384,768]{1,0:T(8,128)(2,1)S(1)} %add_convert_fusion.9), channel_id=1, source_target_pairs={{0,4},{1,5},{2,6},{3,7},{4,0},{5,1},{6,2},{7,3},{8,12},{9,13},{10,... | collective-permute-start | bytes 1769480 | tf_op jit(solution)/shard_map/ppermute | solution.py:499
  526.3 28.4 %collective-permute-start.27 = (bf16[480,768]{1,0:T(8,128)(2,1)S(1)}, bf16[480,768]{1,0:T(8,128)(2,1)S(1)}, u32[]{:S(2)}, u32[]{:S(2)}) collective-permute-start(bf16[480,768]{1,0:T(8,128)(2,1)S(1)} %pad_maximum_fusion.12), channel_id=1, source_target_pairs={{0,4},{1,5},{2,6},{3,7},{4,0},{5,1},{6,2},{7,3},{8,12},{9,13},{10,... | collective-permute-start | bytes 2211848 | tf_op jit(solution)/shard_map/ppermute | solution.py:499
  534.7 22.2 %collective-permute-start.42 = (bf16[192,768]{1,0:T(8,128)(2,1)S(1)}, bf16[192,768]{1,0:T(8,128)(2,1)S(1)}, u32[]{:S(2)}, u32[]{:S(2)}) collective-permute-start(bf16[192,768]{1,0:T(8,128)(2,1)S(1)} %add_convert_fusion.18), channel_id=1, source_target_pairs={{0,8},{1,9},{2,10},{3,11},{4,12},{5,13},{6,14},{7,15},{8,0},{9,1},... | collective-permute-start | bytes 884744 | tf_op jit(solution)/shard_map/ppermute | solution.py:499
  539.9 63.8 %collective-permute-start.36 = (bf16[960,768]{1,0:T(8,128)(2,1)S(1)}, bf16[960,768]{1,0:T(8,128)(2,1)S(1)}, u32[]{:S(2)}, u32[]{:S(2)}) collective-permute-start(bf16[960,768]{1,0:T(8,128)(2,1)S(1)} %pad_maximum_fusion.7), channel_id=1, source_target_pairs={{16,17},{17,16},{18,19},{19,18},{20,21},{21,20},{22,23},{23,22},{2... | collective-permute-start | bytes 4423688 | tf_op jit(solution)/shard_map/ppermute | solution.py:499
  556.8 52.8 %collective-permute-start.28 = (bf16[960,768]{1,0:T(8,128)(2,1)S(1)}, bf16[960,768]{1,0:T(8,128)(2,1)S(1)}, u32[]{:S(2)}, u32[]{:S(2)}) collective-permute-start(bf16[960,768]{1,0:T(8,128)(2,1)S(1)} %pad_maximum_fusion.6), channel_id=1, source_target_pairs={{0,1},{1,0},{2,3},{3,2},{4,5},{5,4},{6,7},{7,6},{8,9},{9,8},{10,11... | collective-permute-start | bytes 4423688 | tf_op jit(solution)/shard_map/ppermute | solution.py:499
  564.0 38.9 %collective-permute-start.11 = (bf16[288,768]{1,0:T(8,128)(2,1)S(1)}, bf16[288,768]{1,0:T(8,128)(2,1)S(1)}, u32[]{:S(2)}, u32[]{:S(2)}) collective-permute-start(bf16[288,768]{1,0:T(8,128)(2,1)S(1)} %pad_maximum_fusion.16), channel_id=1, source_target_pairs={{0,1},{1,0},{2,3},{3,2},{4,5},{5,4},{6,7},{7,6},{8,9},{9,8},{10,11... | collective-permute-start | bytes 1327112 | tf_op jit(solution)/shard_map/ppermute | solution.py:499
  571.8 39.0 %collective-permute-start.52 = (bf16[768,768]{1,0:T(8,128)(2,1)S(1)}, bf16[768,768]{1,0:T(8,128)(2,1)S(1)}, u32[]{:S(2)}, u32[]{:S(2)}) collective-permute-start(bf16[768,768]{1,0:T(8,128)(2,1)S(1)} %pad_maximum_fusion.9), channel_id=1, source_target_pairs={{16,18},{17,19},{18,16},{19,17},{20,22},{21,23},{22,20},{23,21},{2... | collective-permute-start | bytes 3538952 | tf_op jit(solution)/shard_map/ppermute | solution.py:499
  572.6 42.0 %collective-permute-start.44 = (bf16[768,768]{1,0:T(8,128)(2,1)S(1)}, bf16[768,768]{1,0:T(8,128)(2,1)S(1)}, u32[]{:S(2)}, u32[]{:S(2)}) collective-permute-start(bf16[768,768]{1,0:T(8,128)(2,1)S(1)} %pad_maximum_fusion.8), channel_id=1, source_target_pairs={{0,2},{1,3},{2,0},{3,1},{4,6},{5,7},{6,4},{7,5},{8,10},{9,11},{10,... | collective-permute-start | bytes 3538952 | tf_op jit(solution)/shard_map/ppermute | solution.py:499
  602.9 30.8 %collective-permute-start.21 = (bf16[1152,768]{1,0:T(8,128)(2,1)S(1)}, bf16[1152,768]{1,0:T(8,128)(2,1)S(1)}, u32[]{:S(2)}, u32[]{:S(2)}) collective-permute-start(bf16[1152,768]{1,0:T(8,128)(2,1)S(1)} %pad_maximum_fusion.5.refs_2_), channel_id=1, source_target_pairs={{16,20},{17,21},{18,22},{19,23},{20,16},{21,17},{22,18},{23,19},{2... | collective-permute-start | bytes 5308424 | tf_op jit(solution)/shard_map/ppermute | solution.py:499
  603.8 27.9 %collective-permute-start.12 = (bf16[576,768]{1,0:T(8,128)(2,1)S(1)}, bf16[576,768]{1,0:T(8,128)(2,1)S(1)}, u32[]{:S(2)}, u32[]{:S(2)}) collective-permute-start(bf16[576,768]{1,0:T(8,128)(2,1)S(1)} %pad_maximum_fusion.10), channel_id=1, source_target_pairs={{0,8},{1,9},{2,10},{3,11},{4,12},{5,13},{6,14},{7,15},{8,0},{9,1},... | collective-permute-start | bytes 2654216 | tf_op jit(solution)/shard_map/ppermute | solution.py:499
  609.6 63.5 %collective-permute-start.37 = (bf16[1920,768]{1,0:T(8,128)(2,1)S(1)}, bf16[1920,768]{1,0:T(8,128)(2,1)S(1)}, u32[]{:S(2)}, u32[]{:S(2)}) collective-permute-start(bf16[1920,768]{1,0:T(8,128)(2,1)S(1)} %pad_maximum_fusion.1.refs_2_), channel_id=1, source_target_pairs={{16,18},{17,19},{18,16},{19,17},{20,22},{21,23},{22,20},{23,21},{2... | collective-permute-start | bytes 8847368 | tf_op jit(solution)/shard_map/ppermute | solution.py:499
  610.8 62.3 %collective-permute-start.29 = (bf16[1920,768]{1,0:T(8,128)(2,1)S(1)}, bf16[1920,768]{1,0:T(8,128)(2,1)S(1)}, u32[]{:S(2)}, u32[]{:S(2)}) collective-permute-start(bf16[1920,768]{1,0:T(8,128)(2,1)S(1)} %pad_maximum_fusion.refs_0_), channel_id=1, source_target_pairs={{0,2},{1,3},{2,0},{3,1},{4,6},{5,7},{6,4},{7,5},{8,10},{9,11},{10,... | collective-permute-start | bytes 8847368 | tf_op jit(solution)/shard_map/ppermute | solution.py:499
  630.8 34.5 %collective-permute-start.53 = (bf16[1536,768]{1,0:T(8,128)(2,1)S(1)}, bf16[1536,768]{1,0:T(8,128)(2,1)S(1)}, u32[]{:S(2)}, u32[]{:S(2)}) collective-permute-start(bf16[1536,768]{1,0:T(8,128)(2,1)S(1)} %pad_maximum_fusion.3.refs_2_), channel_id=1, source_target_pairs={{16,17},{17,16},{18,19},{19,18},{20,21},{21,20},{22,23},{23,22},{2... | collective-permute-start | bytes 7077896 | tf_op jit(solution)/shard_map/ppermute | solution.py:499
  631.6 33.7 %collective-permute-start.45 = (bf16[1536,768]{1,0:T(8,128)(2,1)S(1)}, bf16[1536,768]{1,0:T(8,128)(2,1)S(1)}, u32[]{:S(2)}, u32[]{:S(2)}) collective-permute-start(bf16[1536,768]{1,0:T(8,128)(2,1)S(1)} %pad_maximum_fusion.2.refs_0_), channel_id=1, source_target_pairs={{0,1},{1,0},{2,3},{3,2},{4,5},{5,4},{6,7},{7,6},{8,9},{9,8},{10,11... | collective-permute-start | bytes 7077896 | tf_op jit(solution)/shard_map/ppermute | solution.py:499
  633.7 24.4 %collective-permute-start.13 = (bf16[1152,768]{1,0:T(8,128)(2,1)S(1)}, bf16[1152,768]{1,0:T(8,128)(2,1)S(1)}, u32[]{:S(2)}, u32[]{:S(2)}) collective-permute-start(bf16[1152,768]{1,0:T(8,128)(2,1)S(1)} %pad_maximum_fusion.4.refs_0_), channel_id=1, source_target_pairs={{0,4},{1,5},{2,6},{3,7},{4,0},{5,1},{6,2},{7,3},{8,12},{9,13},{10,... | collective-permute-start | bytes 5308424 | tf_op jit(solution)/shard_map/ppermute | solution.py:499
  (110 other events, 1449.2 us)

commit v2 on v1

v2 whole, which is shorter than its diff:
```python
import functools

import jax
import jax.numpy as jnp
from jax import lax
from jax.experimental import pallas as pl
from jax.experimental.pallas import tpu as pltpu
from jax.sharding import PartitionSpec as P

HEADS = 12
CHUNKS = 16
TILE = 256
WIDE = 512
UNROLL = 2
KEEP_SCALE = 4.0 / 3.0
EPS = 1e-06
F32 = jnp.float32
BF16 = jnp.bfloat16
VMEM = pl.BlockSpec(memory_space=pltpu.VMEM)
SMEM = pl.BlockSpec(memory_space=pltpu.SMEM)
ANY = pl.BlockSpec(memory_space=pl.ANY)
HBM = pl.BlockSpec(memory_space=pltpu.HBM)
AG, AC, QB, VB, PB, MG, MC, DB, UB = range(9)


def dot_nn(left, right):
    return lax.dot_general(left, right, (((1,), (0,)), ((), ())), preferred_element_type=F32)


def dot_nt(left, right):
    return lax.dot_general(left, right, (((1,), (1,)), ((), ())), preferred_element_type=F32)


def dot_tn(left, right):
    return lax.dot_general(left, right, (((0,), (0,)), ((), ())), preferred_element_type=F32)


def shaped(*shape, dtype=BF16):
    return jax.ShapeDtypeStruct(shape, dtype)


def scratch(*shape, dtype=BF16):
    return pltpu.VMEM(shape, dtype)


def standardize(stream):
    centred = stream - jnp.mean(stream, axis=-1, keepdims=True)
    inverse = lax.rsqrt(jnp.mean(centred * centred, axis=-1, keepdims=True) + EPS)
    return centred * inverse, inverse


def norm_back(grad, normed, inverse):
    return inverse * (
        grad
        - jnp.mean(grad, axis=-1, keepdims=True)
        - normed * jnp.mean(grad * normed, axis=-1, keepdims=True)
    )


def lanes(start, size):
    return pl.ds(pl.multiple_of(start, 128), size)


def rows_at(start, size):
    return pl.ds(pl.multiple_of(start, 16), size)


def row_mask(length, valid):
    return lax.broadcasted_iota(jnp.int32, (length, 1), 0) < valid


class Copies:
    def __init__(self, sems):
        self.sems, self.used, self.out = sems, 0, []

    def start(self, src, dst):
        copy = pltpu.make_async_copy(src, dst, self.sems.at[self.used])
        self.used += 1
        copy.start()
        return copy

    def send(self, src, dst):
        self.out.append(self.start(src, dst))

    def finish(self):
        for copy in self.out:
            copy.wait()


def forward_kernel(image, skip, *refs):
    (act, valid, keep, vecs, x_in, qkvw_in, pw_in, uw_in, dw_in) = refs[:9]
    refs = refs[:9] + refs[9 + skip :]
    outs, stat, refs = refs[9:18], refs[18], refs[19:]
    (x, qkvw, pw, uw, dw, n1, qkv, probs, mixed, h1, n2, slope, gact, h2, sems) = refs
    (n1_out, qkv_out, probs_out, mixed_out, h1_out, n2_out, slope_out, gact_out, h2_out) = outs
    length, width = x.shape
    hidden = uw.shape[1]
    tiles = width // TILE
    low = lax.broadcasted_iota(jnp.int32, (1, 128), 1) < 64

    @pl.when(act[0] == 1)
    def _():
        copies = Copies(sems)
        get_x = copies.start(x_in, x)
        get_qkvw = copies.start(qkvw_in, qkvw)
        get_pw = copies.start(pw_in, pw)
        get_uw = copies.start(uw_in, uw)
        get_dw = copies.start(dw_in, dw)

        get_x.wait()
        normed, _inv = standardize(x[...].astype(F32))
        n1[...] = (normed * vecs[AG : AG + 1, :] + vecs[AC : AC + 1, :]).astype(BF16)
        copies.send(n1, n1_out)
        get_qkvw.wait()
        for part, bias in ((0, QB), (1, None), (2, VB)):
            for t in range(tiles):
                at = slice(part * width + t * TILE, part * width + (t + 1) * TILE)
                out = dot_nn(n1[...], qkvw[:, at])
                if bias is not None:
                    out = out + vecs[bias : bias + 1, t * TILE : (t + 1) * TILE]
                if part == 0:
                    out = out * 0.125
                qkv[:, at] = out.astype(BF16)
        copies.send(qkv, qkv_out)

        live = lax.broadcasted_iota(jnp.int32, (1, length), 1) < valid[image]

        def pair(p, _):
            q = qkv[:, lanes(p * 128, 128)]
            k = qkv[:, lanes(width + p * 128, 128)]
            v = qkv[:, lanes(2 * width + p * 128, 128)]
            zero = jnp.zeros_like(q)
            stacked = jnp.concatenate([jnp.where(low, q, zero), jnp.where(low, zero, q)], axis=0)
            scores = dot_nt(stacked, k)
            scores = jnp.where(live, scores, -1e30)
            top = jnp.max(scores, axis=-1, keepdims=True)
            e = jnp.exp(scores - top)
            total = jnp.sum(e, axis=-1, keepdims=True)
            prob = (e * (1.0 / total)).astype(BF16)
            probs[rows_at(p * 2 * length, 2 * length), :] = prob
            out = dot_nn(prob, v)
            mixed[:, lanes(p * 128, 128)] = jnp.where(low, out[:length], out[length:]).astype(BF16)
            return 0

        lax.fori_loop(0, width // 128, pair, 0, unroll=UNROLL)
        copies.send(probs, probs_out)
        copies.send(mixed, mixed_out)

        get_pw.wait()
        mask = row_mask(length, valid[image])
        a = keep[2 * image] * (dot_nn(mixed[...], pw[...]) + vecs[PB : PB + 1, :])
        stat[1] = jnp.sum(jnp.where(mask, a * a, 0.0))
        h = x[...].astype(F32) + a
        h1[...] = h
        normed, _inv = standardize(h)
        n2[...] = (normed * vecs[MG : MG + 1, :] + vecs[MC : MC + 1, :]).astype(BF16)
        copies.send(h1, h1_out)
        copies.send(n2, n2_out)

        get_uw.wait()

        def tile(t, _):
            at = lanes(t * TILE, TILE)
            ub = vecs[pl.ds(UB + t // tiles, 1), lanes((t % tiles) * TILE, TILE)]
            u = dot_nn(n2[...], uw[:, at]) + ub
            cdf = 0.5 * (1.0 + lax.erf(u * 0.7071067811865476))
            gact[:, at] = (u * cdf).astype(BF16)
            slope[:, at] = (cdf + u * (jnp.exp(-0.5 * u * u) * 0.3989422804014327)).astype(BF16)
            return 0

        lax.fori_loop(0, hidden // TILE, tile, 0, unroll=UNROLL)
        copies.send(gact, gact_out)
        copies.send(slope, slope_out)

        get_dw.wait()
        sum_h = 0.0
        sum_m = 0.0
        for t in range(tiles):
            at = slice(t * TILE, (t + 1) * TILE)
            m = keep[2 * image + 1] * (dot_nn(gact[...], dw[:, at]) + vecs[DB : DB + 1, at])
            h = h1[:, at] + m
            sum_h += jnp.sum(jnp.where(mask, h * h, 0.0))
            sum_m += jnp.sum(jnp.where(mask, m * m, 0.0))
            h2[:, at] = h.astype(BF16)
        stat[0] = sum_h
        stat[2] = sum_m
        copies.send(h2, h2_out)
        copies.finish()


def backward_kernel(image, skip, *refs):
    (act, keep, vecs, seed_in, dw_in, slope_in, uw_in, h1_in, pw_in) = refs[:9]
    (qkv_in, mixed_in, probs_in, x_in, qkvw_in) = refs[9:14]
    refs = refs[14 + skip :]
    (du_out, dy_out, dj_out, dx_out, vec) = refs[:5]
    (seed, dw, slope, uw, h1, pw, qkv, mixed, probs, x, qkvw, du, dy, dj, dx, dmix, dh1, sems) = refs[5:]
    length, width = x.shape
    hidden = uw.shape[1]
    low = lax.broadcasted_iota(jnp.int32, (1, 128), 1) < 64

    @pl.when(act[0] == 1)
    def _():
        copies = Copies(sems)
        get_seed = copies.start(seed_in, seed)
        get_dw = copies.start(dw_in, dw)
        get_slope = copies.start(slope_in, slope)
        get_uw = copies.start(uw_in, uw)
        get_h1 = copies.start(h1_in, h1)
        get_pw = copies.start(pw_in, pw)
        get = [
            copies.start(a, b) for a, b in ((qkv_in, qkv), (mixed_in, mixed), (probs_in, probs))
        ]
        get_x = copies.start(x_in, x)
        get_qkvw = copies.start(qkvw_in, qkvw)

        get_seed.wait()
        z = (keep[2 * image + 1] * seed[...].astype(F32)).astype(BF16)
        dx[...] = z
        vec[3:4, :] = jnp.sum(z.astype(F32), axis=0, keepdims=True)
        get_dw.wait()
        get_slope.wait()
        tiles = width // TILE

        def tile(t, _):
            at = lanes(t * TILE, TILE)
            d = dot_nt(dx[...], dw[rows_at(t * TILE, TILE), :])
            d = (d * slope[:, at].astype(F32)).astype(BF16)
            du[:, at] = d
            vec[pl.ds(4 + t // tiles, 1), lanes((t % tiles) * TILE, TILE)] = jnp.sum(
                d.astype(F32), axis=0, keepdims=True
            )
            return 0

        lax.fori_loop(0, hidden // TILE, tile, 0, unroll=UNROLL)
        copies.send(du, du_out)
        get_uw.wait()
        get_h1.wait()
        dn2 = dot_nt(du[...], uw[...])
        normed, inverse = standardize(h1[...])
        vec[1:2, :] = jnp.sum(dn2 * normed, axis=0, keepdims=True)
        vec[2:3, :] = jnp.sum(dn2, axis=0, keepdims=True)
        d = seed[...].astype(F32) + norm_back(dn2 * vecs[MG : MG + 1, :], normed, inverse)
        dh1[...] = d
        y = (keep[2 * image] * d).astype(BF16)
        dy[...] = y
        vec[0:1, :] = jnp.sum(y.astype(F32), axis=0, keepdims=True)
        copies.send(dy, dy_out)
        get_pw.wait()
        dmix[...] = dot_nt(dy[...], pw[...]).astype(BF16)
        for copy in get:
            copy.wait()

        def pair(p, _):
            at = lanes(p * 128, 128)
            k_at = lanes(width + p * 128, 128)
            v_at = lanes(2 * width + p * 128, 128)
            q = qkv[:, at]
            k = qkv[:, k_at]
            v = qkv[:, v_at]
            g = dmix[:, at]

            def stack(a):
                zero = jnp.zeros_like(a)
                return jnp.concatenate([jnp.where(low, a, zero), jnp.where(low, zero, a)], axis=0)

            both = stack(g)
            prod = g.astype(F32) * mixed[:, at].astype(F32)
            side = jnp.concatenate(
                [
                    jnp.sum(jnp.where(low, prod, 0.0), axis=-1, keepdims=True),
                    jnp.sum(jnp.where(low, 0.0, prod), axis=-1, keepdims=True),
                ],
                axis=0,
            )
            prob = probs[rows_at(p * 2 * length, 2 * length), :]
            dp = dot_nt(both, v)
            ds = (prob.astype(F32) * (dp - side)).astype(BF16)
            dj[:, v_at] = dot_tn(prob, both).astype(BF16)
            dq = dot_nn(ds, k)
            dj[:, at] = (0.125 * jnp.where(low, dq[:length], dq[length:])).astype(BF16)
            dj[:, k_at] = dot_tn(ds, stack(q)).astype(BF16)
            return 0

        lax.fori_loop(0, width // 128, pair, 0, unroll=UNROLL)
        copies.send(dj, dj_out)
        get_x.wait()
        get_qkvw.wait()
        vec[10:11, :] = jnp.sum(dj[:, 0:width].astype(F32), axis=0, keepdims=True)
        vec[11:12, :] = jnp.sum(dj[:, 2 * width :].astype(F32), axis=0, keepdims=True)
        dn1 = dot_nt(dj[...], qkvw[...])
        normed, inverse = standardize(x[...].astype(F32))
        vec[8:9, :] = jnp.sum(dn1 * normed, axis=0, keepdims=True)
        vec[9:10, :] = jnp.sum(dn1, axis=0, keepdims=True)
        d = dh1[...] + norm_back(dn1 * vecs[AG : AG + 1, :], normed, inverse)
        dx[...] = d.astype(BF16)
        copies.send(dx, dx_out)
        copies.finish()


def send_chunks(copies, code, full, pieces):
    rows = full.shape[1] // CHUNKS
    for ref, start in zip(pieces, (8, 4, 2, 1, 0)):
        for j in range(ref.shape[0]):
            which = jnp.bitwise_xor(code, start + j)
            copies.send(full.at[:, rows_at(which * rows, rows), :], ref.at[j])


def gather_rows(copies, ins, held):
    rows = ins[0].shape[0]
    return [
        copies.start(one, held.at[pl.ds(i * rows, rows), :]) for i, one in enumerate(ins)
    ]


def down_grad_kernel(images, skip, *refs):
    act, codes, keep, refs = *refs[:3], refs[3:]
    seed_in, gact_in, refs = refs[:images], refs[images : 2 * images], refs[2 * images + skip :]
    pieces, (dz, gact, full, sems) = refs[:5], refs[5:]

    @pl.when(act[0] == 1)
    def _():
        copies = Copies(sems)
        get = gather_rows(copies, seed_in, dz) + gather_rows(copies, gact_in, gact)
        for copy in get[:images]:
            copy.wait()
        length = dz.shape[0] // images
        for i in range(images):
            r = slice(i * length, (i + 1) * length)
            dz[r, :] = (keep[2 * i + 1] * dz[r, :].astype(F32)).astype(BF16)
        for copy in get[images:]:
            copy.wait()

        def tile(t, _):
            at = pl.multiple_of(t * WIDE, WIDE)
            full[0, pl.ds(at, WIDE), :] = dot_tn(gact[:, pl.ds(at, WIDE)], dz[...]).astype(BF16)
            return 0

        lax.fori_loop(0, gact.shape[1] // WIDE, tile, 0)
        send_chunks(copies, codes[0], full, pieces)
        copies.finish()


def up_grad_kernel(images, skip, *refs):
    act, codes, refs = *refs[:2], refs[2:]
    n = images
    ins, refs = [refs[k * n : (k + 1) * n] for k in range(2)], refs[2 * n + skip :]
    pieces, (n2, du, full, sems) = refs[:5], refs[5:]

    @pl.when(act[0] == 1)
    def _():
        copies = Copies(sems)
        get = [gather_rows(copies, i, h) for i, h in zip(ins, (n2, du))]
        tiles = full.shape[2] // TILE
        for copy in get[0] + get[1]:
            copy.wait()

        def tile(t, _):
            at = lanes(t * TILE, TILE)
            to = lanes((t % tiles) * TILE, TILE)
            full[t // tiles, :, to] = dot_tn(n2[...], du[:, at]).astype(BF16)
            return 0

        lax.fori_loop(0, du.shape[1] // TILE, tile, 0)
        send_chunks(copies, codes[1], full, pieces)
        copies.finish()


def qkv_grad_kernel(images, skip, *refs):
    act, codes, refs = *refs[:2], refs[2:]
    n = images
    ins, refs = [refs[k * n : (k + 1) * n] for k in range(4)], refs[4 * n + skip :]
    pieces, (n1, dj, mixed, dy, full, sems) = refs[:5], refs[5:]

    @pl.when(act[0] == 1)
    def _():
        copies = Copies(sems)
        get = [gather_rows(copies, i, h) for i, h in zip(ins, (n1, dj, mixed, dy))]
        tiles = full.shape[2] // TILE
        for copy in get[0] + get[1]:
            copy.wait()

        def tile(t, _):
            at = lanes(t * TILE, TILE)
            to = lanes((t % tiles) * TILE, TILE)
            full[t // tiles, :, to] = dot_tn(n1[...], dj[:, at]).astype(BF16)
            return 0

        lax.fori_loop(0, dj.shape[1] // TILE, tile, 0)
        for copy in get[2] + get[3]:
            copy.wait()
        full[full.shape[0] - 1] = dot_tn(mixed[...], dy[...]).astype(BF16)
        send_chunks(copies, codes[2], full, pieces)
        copies.finish()


def call(body, scalars, vecs, arrays, over, after, outs, held, copies, flops, limit):
    tail = [*after, *(o for o, _ in over)]
    ops = (*scalars, *vecs, *arrays, *tail)
    first = len(scalars) + len(vecs) + len(arrays) + len(after)

    def place(o):
        if o.shape == (8,):
            return SMEM
        return VMEM if o.dtype == F32 and o.shape[0] == 16 else HBM

    moved = sum(o.size * o.dtype.itemsize for o in arrays) + sum(o.size * o.dtype.itemsize for o in outs)
    return pl.pallas_call(
        body,
        out_shape=list(outs),
        in_specs=[SMEM] * len(scalars) + [VMEM] * len(vecs) + [ANY] * (len(arrays) + len(tail)),
        out_specs=[place(o) for o in outs],
        scratch_shapes=[*held, pltpu.SemaphoreType.DMA((copies,))],
        input_output_aliases={first + k: out for k, (_, out) in enumerate(over)},
        compiler_params=pltpu.CompilerParams(vmem_limit_bytes=limit << 20),
        cost_estimate=pl.CostEstimate(flops=int(flops), bytes_accessed=int(moved), transcendentals=0),
    )(*ops)


def piece_shapes(blocks, rows, width):
    return [shaped(n, blocks, rows, width) for n in (8, 4, 2, 1, 1)]


def like(*arrays):
    return [scratch(*a.shape, dtype=a.dtype) for a in arrays]


def forward(act, valid, keep, x, vecs, mats, image, after):
    qkvw, pw, uw, dw = mats
    length, width = x.shape
    hidden = uw.shape[1]
    thin, wide = shaped(length, width), shaped(length, hidden)
    outs = [
        thin,
        shaped(length, 3 * width),
        shaped(HEADS * length, length),
        thin,
        shaped(length, width, dtype=F32),
        thin,
        wide,
        wide,
        thin,
    ]
    *saved, h2, stat = call(
        functools.partial(forward_kernel, image, len(after)),
        (act, valid, keep),
        (vecs,),
        (x, qkvw, pw, uw, dw),
        (),
        after,
        [*outs, shaped(8, dtype=F32)],
        like(x, qkvw, pw, uw, dw, *outs),
        14,
        flops=2 * length * width * width * 14,
        limit=48,
    )
    return h2, stat, (x, *saved)


def backward(act, keep, seed, saved, vecs, mats, image, after):
    qkvw, pw, uw, dw = mats
    (x, n1, qkv, probs, mixed, h1, n2, slope, gact) = saved
    length, width = x.shape
    thin = shaped(length, width)
    outs = [slope, thin, qkv, thin]
    ins = (seed, dw, slope, uw, h1, pw, qkv, mixed, probs, x, qkvw)
    return call(
        functools.partial(backward_kernel, image, len(after)),
        (act, keep),
        (vecs,),
        ins,
        (),
        after,
        [*outs, shaped(16, width, dtype=F32)],
        like(*ins, *outs, thin, h1),
        15,
        flops=2 * length * width * width * 16,
        limit=48,
    )


def grads_call(body, scalars, groups, over, full, after):
    images = len(groups[0])
    length = groups[0][0].shape[0]
    held = [scratch(images * length, g[0].shape[1]) for g in groups]
    return call(
        functools.partial(body, images, len(over) + len(after)),
        scalars,
        (),
        [one for g in groups for one in g],
        over,
        after,
        piece_shapes(full[0], full[1] // CHUNKS, full[2]),
        [*held, scratch(*full)],
        len(groups) * images + CHUNKS,
        flops=2 * images * length * full[0] * full[1] * full[2],
        limit=48,
    )


def orders(bits):
    if bits == 4:
        return ((0, 1, 2, 3), (1, 2, 0, 3), (2, 0, 1, 3))
    plain = tuple(range(bits))
    return (plain, plain, plain)


def flipped(block, bit, sections, size):
    route = [(s * size + i, s * size + (i ^ (1 << bit))) for s in sections for i in range(size)]
    return lax.ppermute(block, ("section", "dp"), route)


def chunk_code(order, place):
    code = jnp.zeros((), jnp.int32)
    for k, bit in enumerate(order):
        code = code + (((place >> bit) & 1) << (len(order) - 1 - k))
    return code


STEPS = (
    (0, 1), (3, 0), (1, 1), (2, 1), (0, 2), (3, 1), (1, 2), (2, 2), (0, 3), (3, 2), (1, 3), (2, 3),
    (0, 4), (3, 3), (1, 4), (2, 4), (0, 5), (1, 5), (2, 5), (0, 6), (1, 6), (2, 6), (0, 7), (1, 7), (2, 7),
)


class Sum:
    def __init__(self, pieces, order, first):
        self.pieces, self.order, self.arrived, self.have = pieces, order, [first], None

    def send(self, step, after):
        if step < 5:
            count = 8 >> step
            parts = [self.pieces[step].astype(F32)]
            low = count if step < 4 else 0
            high = 2 * count if step < 4 else 1
            for r in self.arrived:
                parts.append(r[low:high].astype(F32))
            block = sum(parts[1:], parts[0]).astype(BF16)
        else:
            block = jnp.concatenate([self.have, self.last])
        block, _ = lax.optimization_barrier((block, after))
        return block

    def run(self, step, after, size):
        block = self.send(step, after)
        bit = self.order[step] if step < 4 else self.order[7 - step]
        got = flipped(block, bit, (0, 1), size)
        if step < 4:
            self.arrived.append(got)
        else:
            self.have, self.last = block, got
        return block


def settle(code, halves, blocks, shapes, after):
    _, _, rows, width = halves[0].shape

    def body(scalars, lower, upper, _, *outs):
        j = pl.program_id(0)
        for src, here in ((lower, j < 8), (upper, j >= 8)):

            @pl.when(here)
            def _(src=src):
                at = 0
                for count, out in zip(blocks, outs):
                    for b in range(count):
                        out[:, b * width : (b + 1) * width] = src[0, at].astype(F32)
                        at += 1

    block = (1, *halves[0].shape[1:])
    outs = [shaped(*s, dtype=F32) for s in shapes]
    return pl.pallas_call(
        body,
        out_shape=outs,
        grid_spec=pltpu.PrefetchScalarGridSpec(
            num_scalar_prefetch=1,
            grid=(CHUNKS,),
            in_specs=[
                pl.BlockSpec(block, lambda j, s: (jnp.minimum(j, 7), 0, 0, 0)),
                pl.BlockSpec(block, lambda j, s: (jnp.maximum(j - 8, 0), 0, 0, 0)),
                ANY,
            ],
            out_specs=[
                pl.BlockSpec((rows, count * width), lambda j, s: (jnp.bitwise_xor(s[0], j), 0))
                for count in blocks
            ],
        ),
        compiler_params=pltpu.CompilerParams(vmem_limit_bytes=16 << 20),
        cost_estimate=pl.CostEstimate(
            flops=0, bytes_accessed=sum(o.size * 6 for o in outs), transcendentals=0
        ),
    )(code.reshape(1), *halves, after)


def per_device(size, ends, counts, keep, *params):
    ag, ac, qkvw, qb, vb, pw, pb, mg, mc, uw, ub, dw, db = params
    mats = [item[0] for item in (qkvw, pw, uw, dw)]
    section = lax.axis_index("section")
    place = lax.axis_index("dp")
    first = section == 0
    images, slots, width = ends.shape[1:]
    hidden = ub.shape[1]
    blocks = hidden // width
    vecs = jnp.concatenate([ag, ac, qb, vb, pb, mg, mc, db, ub.reshape(blocks, width)])
    length = -(-slots // 32) * 32
    bits = size.bit_length() - 1
    ways = orders(bits)
    if size == CHUNKS:
        codes = [chunk_code(o, place) for o in ways]
    else:
        codes = [jnp.zeros((), jnp.int32)] * 3
    coded = jnp.stack(codes)
    acts = [(section == s).astype(jnp.int32).reshape(1) for s in (0, 1)]
    keeping = (keep[0].astype(F32) * KEEP_SCALE).reshape(-1)
    live = (jnp.arange(slots)[None, :] < counts[:, None])[..., None]

    def padded(block):
        return jnp.pad(block, ((0, length - slots), (0, 0)))

    def crossed(block, source):
        route = [(source * size + i, (1 - source) * size + i) for i in range(size)]
        return lax.ppermute(block, ("section", "dp"), route)

    every = range(images)
    early = size == CHUNKS
    acts_on = {0: acts[0], 1: acts[1]}
    token = []

    def forwards(which, xs):
        ran = []
        for i in every:
            ran.append(forward(acts_on[which], counts, keeping, xs[i], vecs, mats, i, list(token)))
            token[:] = [ran[-1][2][1]]
        return ran

    def backwards(which, seeds, kept, gates=()):
        back = []
        for i in every:
            after = [*token, *(gates if i == images - 1 else ())]
            back.append(backward(acts_on[which], keeping, seeds[i], kept[i], vecs, mats, i, after))
            token[:] = [back[-1][0]]
        return back

    def grads(kernel, which, groups, old, full):
        over = [(p, k) for k, p in enumerate(old) if k > 0 or not early]
        scalars = (acts_on[which], coded)
        if kernel is down_grad_kernel:
            scalars = (*scalars, keeping)
        pieces = grads_call(kernel, scalars, groups, over, full, list(token))
        token[:] = [pieces[0]]
        return pieces

    def column(kept, k):
        return [one[k] for one in kept]

    down_full, up_full, qkv_full = (1, hidden, width), (blocks, width, width), (4, width, width)

    x0 = [padded(ends[0, i]) for i in every]
    ran0 = forwards(0, x0)
    x1 = [crossed(ran0[i][0], 0) for i in every]
    ran1 = forwards(1, x1)
    kept0, kept1 = ([r[2] for r in ran] for ran in (ran0, ran1))

    def weight_grads(which, kept, back, old):
        pb = grads(up_grad_kernel, which, (column(kept, 6), column(back, 0)), old[0], up_full)
        sources = (column(kept, 1), column(back, 2), column(kept, 4), column(back, 1))
        pc = grads(qkv_grad_kernel, which, sources, old[1], qkv_full)
        return pb, pc

    seed1 = [padded(jnp.where(live[i], ends[0, i], jnp.zeros((), BF16))) for i in every]
    pa1 = grads(down_grad_kernel, 1, (seed1, column(kept1, 8)), (), down_full)
    gates = ()
    if early:
        ra1 = flipped(pa1[0], ways[0][0], (1,), size)
        gates = (ra1,)
    back1 = backwards(1, seed1, kept1, gates)
    seed0 = [crossed(back1[i][3], 1) for i in every]
    pb1, pc1 = weight_grads(1, kept1, back1, ((), ()))
    if early:
        rb1 = flipped(pb1[0], ways[1][0], (1,), size)
        rc1 = flipped(pc1[0], ways[2][0], (1,), size)
    back0 = backwards(0, seed0, kept0)
    pa = grads(down_grad_kernel, 0, (seed0, column(kept0, 8)), pa1, down_full)
    pb, pc = weight_grads(0, kept0, back0, (pb1, pc1))

    def both(a, b):
        return jnp.where(first, sum(a[1:], a[0]), sum(b[1:], b[0]))

    made = both(column(back0, 4), column(back1, 4))
    stats = both(column(ran0, 1), column(ran1, 1))[:3]
    extra = jnp.concatenate([stats, jnp.sum(counts.astype(F32)).reshape(1)])
    extra = jnp.pad(extra, (0, width - 4)).reshape(1, width)
    vec = jnp.concatenate([made[:12], extra])

    if early:
        sums = []
        for p, one, way in zip((pa, pb, pc), (ra1, rb1, rc1), ways):
            got = flipped(p[0], way[0], (0,), size)
            sums.append(Sum(p, way, jnp.where(first, got, one)))
        after = pc[4]
        for which, step in STEPS:
            if which == 3:
                vec, _ = lax.optimization_barrier((vec, after))
                after = vec
                vec = vec + flipped(vec, step, (0, 1), size)
            else:
                after = sums[which].run(step, after, size)
        halves = [(s.have, s.last) for s in sums]
    else:
        halves = []
        for p in (pa, pb, pc):
            whole = lax.psum(jnp.concatenate(p[::-1]), "dp")
            halves.append((whole[:8], whole[8:]))
        for bit in range(bits):
            vec = vec + flipped(vec, bit, (0, 1), size)
        after = vec

    (g_down,) = settle(codes[0], halves[0], (1,), [(hidden, width)], after)
    g_qkv, g_proj = settle(
        codes[2], halves[2], (3, 1), [(width, 3 * width), (width, width)], g_down
    )
    (g_up,) = settle(codes[1], halves[1], (blocks,), [(width, hidden)], g_qkv)

    shown = jnp.stack([jnp.where(first, back0[i][3], ran1[i][0])[:slots] for i in every])
    shown = jnp.where(live, shown, jnp.zeros((), BF16))[None]
    rms = jnp.sqrt(vec[-1, 0:3] / (vec[-1, 3] * width)).reshape(1, 3)
    row = lambda k: vec[k : k + 1]
    return (
        shown,
        row(8),
        row(9),
        g_qkv[None],
        row(10),
        row(11),
        g_proj[None],
        row(0),
        row(1),
        row(2),
        g_up[None],
        vec[4 : 4 + blocks].reshape(1, hidden),
        g_down[None],
        row(3),
        rms,
    )


def solution(mesh):
    flat = P("section", None)
    deep = P("section", None, None)
    split = P("section", "dp", None, None)
    ranks = (flat, flat, deep, flat, flat, deep, flat, flat, flat, deep, flat, deep, flat)
    return jax.shard_map(
        functools.partial(per_device, mesh.shape["dp"]),
        mesh=mesh,
        in_specs=(split, P("dp"), P("section", "dp", None), *ranks),
        out_specs=(split, *ranks, flat),
        check_vma=False,
    )
```

time: 691 us -> 502 us (0.73)
  the two profiles are of different devices: /device:TPU:0 before, /device:TPU:8 now
where the time goes in v2:
time: 502 us; the launch traced here: 494 us
  waiting for transfers between devices  205 us (41%)
  Pallas kernels  165 us (33%)
  starting transfers between devices  56.7 us (11%)
  local copies, waits for them, and re-layouts  48.7 us (10%)
  other arithmetic  14.8 us (3%)
    ppermute x31, waiting for transfers between devices, flipped(): return lax.ppermute(block, ('section', 'dp'), route)  177 us
    pallas_call x18, Pallas kernels, call(): pl.pallas_call(body, out_shape=list(outs), in_specs=[SMEM] * len(scalars)...  144 us
    ppermute x31, starting transfers between devices, flipped(): return lax.ppermute(block, ('section', 'dp'), route)  46.7 us
    unnamed x207, local copies, waits for them, and re-layouts  44.8 us
    ppermute x6, waiting for transfers between devices, crossed(): return lax.ppermute(block, ('section', 'dp'), route)  28.2 us
    pallas_call x3, Pallas kernels, settle(): pl.pallas_call(body, out_shape=outs, grid_spec=pltpu.PrefetchScalarGridSp...  21 us
  transfers between devices with their start and end apart: 37, of which 22 were waited for; matrix products, arithmetic and copies ran while one was open for 3% of the time, Pallas kernels for 23%

profile of v2, /device:TPU:8, one launch (start us, length us, event | category | flops | bytes accessed | tf_op | source)
XLA Modules:
  0.0 493.6 jit_solution(16947972603838940609)
XLA Ops:
  6.0 16.5 %shard_map.271 = (bf16[288,768]{1,0:T(8,128)(2,1)S(1)}, bf16[288,2304]{1,0:T(8,128)(2,1)S(1)}, bf16[3456,288]{1,0:T(8,128)(2,1)}, bf16[288,768]{1,0:T(8,128)(2,1...) custom-call(s32[1]{0:T(128)} %bitcast.refs_0_, ...), custom_call_target="tpu_custom_call" | custom-call | flops 4756340736 | bytes 24109088 | tf_op jit(solution)/shard_map/pallas_call | solution.py:407
  26.5 16.5 %shard_map.272 = (bf16[288,768]{1,0:T(8,128)(2,1)S(1)}, bf16[288,2304]{1,0:T(8,128)(2,1)S(1)}, bf16[3456,288]{1,0:T(8,128)(2,1)}, bf16[288,768]{1,0:T(8,128)(2,1...) custom-call(s32[1]{0:T(128)} %bitcast.refs_0_, ...), custom_call_target="tpu_custom_call" | custom-call | flops 4756340736 | bytes 24109088 | tf_op jit(solution)/shard_map/pallas_call | solution.py:407
  47.0 17.0 %shard_map.273 = (bf16[288,768]{1,0:T(8,128)(2,1)S(1)}, bf16[288,2304]{1,0:T(8,128)(2,1)S(1)}, bf16[3456,288]{1,0:T(8,128)(2,1)}, bf16[288,768]{1,0:T(8,128)(2,1...) custom-call(s32[1]{0:T(128)} %bitcast.refs_0_, ...), custom_call_target="tpu_custom_call" | custom-call | flops 4756340736 | bytes 24109088 | tf_op jit(solution)/shard_map/pallas_call | solution.py:407
  105.8 23.4 %collective-permute-done.3.refs_3_ = bf16[288,768]{1,0:T(8,128)(2,1)} collective-permute-done((bf16[288,768]{1,0:T(8,128)(2,1)}, bf16[288,768]{1,0:T(8,128)(2,1)}, u32[]{:S(2)}, u32[]{:S(2)}) %collective-permute-start.3) | collective-permute-done | bytes 442400 | tf_op jit(solution)/shard_map/ppermute | solution.py:621
  129.2 16.0 %shard_map.283 = (bf16[288,3072]{1,0:T(8,128)(2,1)}, bf16[288,768]{1,0:T(8,128)(2,1)S(1)}, bf16[288,2304]{1,0:T(8,128)(2,1)S(1)}, bf16[288,768]{1,0:T(8,128)(2,1)S(1)}, f32[16,768]{1,0:T(8,128)S(1)}) custom-call(s32[1]{0:T(128)} %bitcast.refs_0_, f32[6]{0:T(128)S(1)} %mul.14.refs_2_.refs_1_, f32[12,768]{1,0:T(8,128)S(1)} %concatenate.43.refs_3_.refs_2_, ...), custom_call_target="tpu_custom_call" | custom-call | flops 5435817984 | bytes 25485312 | tf_op jit(solution)/shard_map/pallas_call | solution.py:407
  148.9 15.8 %shard_map.284 = (bf16[288,3072]{1,0:T(8,128)(2,1)}, bf16[288,768]{1,0:T(8,128)(2,1)S(1)}, bf16[288,2304]{1,0:T(8,128)(2,1)S(1)}, bf16[288,768]{1,0:T(8,128)(2,1)S(1)}, f32[16,768]{1,0:T(8,128)S(1)}) custom-call(s32[1]{0:T(128)} %bitcast.refs_0_, f32[6]{0:T(128)S(1)} %mul.14.refs_2_.refs_1_, f32[12,768]{1,0:T(8,128)S(1)} %concatenate.43.refs_3_.refs_2_, ...), custom_call_target="tpu_custom_call" | custom-call | flops 5435817984 | bytes 25485312 | tf_op jit(solution)/shard_map/pallas_call | solution.py:407
  169.7 16.2 %shard_map.285 = (bf16[288,3072]{1,0:T(8,128)(2,1)}, bf16[288,768]{1,0:T(8,128)(2,1)S(1)}, bf16[288,2304]{1,0:T(8,128)(2,1)S(1)}, bf16[288,768]{1,0:T(8,128)(2,1)S(1)}, f32[16,768]{1,0:T(8,128)S(1)}) custom-call(s32[1]{0:T(128)} %bitcast.refs_0_, f32[6]{0:T(128)S(1)} %mul.14.refs_2_.refs_1_, f32[12,768]{1,0:T(8,128)S(1)} %concatenate.43.refs_3_.refs_2_, ...), custom_call_target="tpu_custom_call" | custom-call | flops 5435817984 | bytes 25485312 | tf_op jit(solution)/shard_map/pallas_call | solution.py:407
  189.7 11.2 %shard_map.286 = (bf16[8,1,192,768]{3,2,1,0:T(8,128)(2,1)}, bf16[4,1,192,768]{3,2,1,0:T(8,128)(2,1)S(1)}, bf16[2,1,192,768]{3,2,1,0:T(8,128)(2,1)S(1)}, bf16[1,1...) custom-call(s32[1]{0:T(128)} %bitcast.refs_0_, ...), custom_call_target="tpu_custom_call", output_to_operand_aliasing={{1}: (10, {}), {2}: (11, {}), {3}: (12, {}), {4}: (13, {})} | custom-call | flops 4076863488 | bytes 11354112 | tf_op jit(solution)/shard_map/pallas_call | solution.py:407
  208.6 12.8 %shard_map.287 = (bf16[8,4,48,768]{3,2,1,0:T(8,128)(2,1)}, bf16[4,4,48,768]{3,2,1,0:T(8,128)(2,1)S(1)}, bf16[2,4,48,768]{3,2,1,0:T(8,128)(2,1)S(1)}, bf16[1,4,48...) custom-call(s32[1]{0:T(128)} %bitcast.refs_0_, ...), custom_call_target="tpu_custom_call", output_to_operand_aliasing={{1}: (9, {}), {2}: (10, {}), {3}: (11, {}), {4}: (12, {})} | custom-call | flops 4076863488 | bytes 11354112 | tf_op jit(solution)/shard_map/pallas_call | solution.py:407
  227.0 12.7 %shard_map.288 = (bf16[8,4,48,768]{3,2,1,0:T(8,128)(2,1)}, bf16[4,4,48,768]{3,2,1,0:T(8,128)(2,1)}, bf16[2,4,48,768]{3,2,1,0:T(8,128)(2,1)S(1)}, bf16[1,4,48,768...) custom-call(s32[1]{0:T(128)} %bitcast.refs_0_, ...), custom_call_target="tpu_custom_call", output_to_operand_aliasing={{1}: (15, {}), {2}: (16, {}), {3}: (17, {}), {4}: (18, {})} | custom-call | flops 4076863488 | bytes 12681216 | tf_op jit(solution)/shard_map/pallas_call | solution.py:407
  246.3 31.5 %collective-permute-done.12 = bf16[8,4,48,768]{3,2,1,0:T(8,128)(2,1)} collective-permute-done((bf16[8,4,48,768]{3,2,1,0:T(8,128)(2,1)}, bf16[8,4,48,768]{3,2,1,0:T(8,128)(2,1)}, u32[]{:S(2)}, u32[]{:S(2)}) %collective-permute-start.12) | collective-permute-done | bytes 2359328 | tf_op jit(solution)/shard_map/ppermute | solution.py:509
  280.4 10.7 %collective-permute-done.10 = bf16[8,4,48,768]{3,2,1,0:T(8,128)(2,1)S(1)} collective-permute-done((bf16[8,4,48,768]{3,2,1,0:T(8,128)(2,1)}, bf16[8,4,48,768]{3,2,1,0:T(8,128)(2,1)S(1)}, u32[]{:S(2)}, u32[]{:S(2)}) %collective-permute-start.10) | collective-permute-done | bytes 2359328 | tf_op jit(solution)/shard_map/ppermute | solution.py:509
  293.7 15.7 %collective-permute-done.8 = f32[13,768]{1,0:T(8,128)S(1)} collective-permute-done((f32[13,768]{1,0:T(8,128)S(1)}, f32[13,768]{1,0:T(8,128)S(1)}, u32[]{:S(2)}, u32[]{:S(2)}) %collective-permute-start.8) | collective-permute-done | bytes 39968 | tf_op jit(solution)/shard_map/ppermute | solution.py:509
  317.0 8.4 %collective-permute-done.14 = f32[13,768]{1,0:T(8,128)S(1)} collective-permute-done((f32[13,768]{1,0:T(8,128)S(1)}, f32[13,768]{1,0:T(8,128)S(1)}, u32[]{:S(2)}, u32[]{:S(2)}) %collective-permute-start.14) | collective-permute-done | bytes 39968 | tf_op jit(solution)/shard_map/ppermute | solution.py:509
  332.7 4.8 collective-permute-done.18
  337.5 11.1 %collective-permute-done.19 = bf16[1,1,192,768]{3,2,1,0:T(8,128)(2,1)S(1)} collective-permute-done((bf16[1,1,192,768]{3,2,1,0:T(8,128)(2,1)S(1)}, bf16[1,1,192,768]{3,2,1,0:T(8,128)(2,1)S(1)}, u32[]{:S(2)}, u32[]{:S(2)}) %collective-permute-start.19) | collective-permute-done | bytes 294944 | tf_op jit(solution)/shard_map/ppermute | solution.py:509
  348.9 3.5 collective-permute-start.27
  352.4 5.8 %collective-permute-done.24 = bf16[1,4,48,768]{3,2,1,0:T(8,128)(2,1)S(1)} collective-permute-done((bf16[1,4,48,768]{3,2,1,0:T(8,128)(2,1)S(1)}, bf16[1,4,48,768]{3,2,1,0:T(8,128)(2,1)S(1)}, u32[]{:S(2)}, u32[]{:S(2)}) %collective-permute-start.24) | collective-permute-done | bytes 294944 | tf_op jit(solution)/shard_map/ppermute | solution.py:509
  358.4 3.5 collective-permute-start.26
  362.0 7.2 %collective-permute-done.23 = bf16[1,4,48,768]{3,2,1,0:T(8,128)(2,1)S(1)} collective-permute-done((bf16[1,4,48,768]{3,2,1,0:T(8,128)(2,1)S(1)}, bf16[1,4,48,768]{3,2,1,0:T(8,128)(2,1)S(1)}, u32[]{:S(2)}, u32[]{:S(2)}) %collective-permute-start.23) | collective-permute-done | bytes 294944 | tf_op jit(solution)/shard_map/ppermute | solution.py:509
  369.3 3.4 collective-permute-start.25
  375.8 4.9 collective-permute-done.25
  380.8 7.6 %collective-permute-done.30 = bf16[2,1,192,768]{3,2,1,0:T(8,128)(2,1)S(1)} collective-permute-done((bf16[2,1,192,768]{3,2,1,0:T(8,128)(2,1)S(1)}, bf16[2,1,192,768]{3,2,1,0:T(8,128)(2,1)S(1)}, u32[]{:S(2)}, u32[]{:S(2)}) %collective-permute-start.30) | collective-permute-done | bytes 589856 | tf_op jit(solution)/shard_map/ppermute | solution.py:509
  393.1 19.1 %collective-permute-done.33 = bf16[4,1,192,768]{3,2,1,0:T(8,128)(2,1)S(1)} collective-permute-done((bf16[4,1,192,768]{3,2,1,0:T(8,128)(2,1)S(1)}, bf16[4,1,192,768]{3,2,1,0:T(8,128)(2,1)S(1)}, u32[]{:S(2)}, u32[]{:S(2)}) %collective-permute-start.33) | collective-permute-done | bytes 1179680 | tf_op jit(solution)/shard_map/ppermute | solution.py:509
  412.4 5.6 %collective-permute-done.32 = bf16[4,4,48,768]{3,2,1,0:T(8,128)(2,1)S(1)} collective-permute-done((bf16[4,4,48,768]{3,2,1,0:T(8,128)(2,1)S(1)}, bf16[4,4,48,768]{3,2,1,0:T(8,128)(2,1)S(1)}, u32[]{:S(2)}, u32[]{:S(2)}) %collective-permute-start.32) | collective-permute-done | bytes 1179680 | tf_op jit(solution)/shard_map/ppermute | solution.py:509
  418.2 3.8 collective-permute-done.31
  425.1 3.6 collective-permute-start.22
  430.1 32.4 %collective-permute-done.22 = f32[13,768]{1,0:T(8,128)S(1)} collective-permute-done((f32[13,768]{1,0:T(8,128)S(1)}, f32[13,768]{1,0:T(8,128)S(1)}, u32[]{:S(2)}, u32[]{:S(2)}) %collective-permute-start.22) | collective-permute-done | bytes 39968 | tf_op jit(solution)/shard_map/ppermute | solution.py:509
  465.4 7.1 %shard_map.289._ = f32[3072,768]{1,0:T(8,128)} custom-call(s32[1]{0:T(128)} %bitcast.9.scalars, bf16[8,1,192,768]{3,2,1,0:T(8,128)(2,1)S(1)} %pad_maximum_fusion.2.lower, bf16[8,1,192,768]{3,2,1,0:T(8,128)(2,1)S(1)} %collective-permute-done.35.upper, bf16[8,4,48,768]{3,2,1,0:T(8,128)(2,1)S(1)} %pad_maximum_fusion._.lower), custom_call_target="tpu_custom_call" | custom-call | bytes 14155776 | tf_op jit(solution)/shard_map/pallas_call | solution.py:571
  472.5 3.7 copy-done.1
  476.2 6.9 %shard_map.290 = (f32[768,2304]{1,0:T(8,128)}, f32[768,768]{1,0:T(8,128)}) custom-call(s32[1]{0:T(128)} %bitcast.11.scalars, bf16[8,4,48,768]{3,2,1,0:T(8,128)(2,1)S(1)} %pad_maximum_fusion._.lower, bf16[8,4,48,768]{3,2,1,0:T(8,128)(2,1)S(1)} %collective-permute-done.34.upper, f32[3072,768]{1,0:T(8,128)S(1)} %copy-done.1), custom_call_target="tpu_custom_call" | custom-call | bytes 14155776 | tf_op jit(solution)/shard_map/pallas_call | solution.py:571
  486.1 7.0 %shard_map.291 = f32[768,3072]{1,0:T(8,128)} custom-call(s32[1]{0:T(128)} %bitcast.10.scalars, bf16[8,4,48,768]{3,2,1,0:T(8,128)(2,1)S(1)} %pad_maximum_fusion.1.lower, bf16[8,4,48,768]{3,2,1,0:T(8,128)(2,1)S(1)} %collective-permute-done.36.upper, f32[768,2304]{1,0:T(8,128)S(1)} %copy-done.2), custom_call_target="tpu_custom_call" | custom-call | bytes 14155776 | tf_op jit(solution)/shard_map/pallas_call | solution.py:571
  (327 shorter events, 124.9 us)
Async XLA Ops:
  24.3 47.9 %collective-permute-start = (bf16[288,768]{1,0:T(8,128)(2,1)}, bf16[288,768]{1,0:T(8,128)(2,1)}, u32[]{:S(2)}, u32[]{:S(2)}) collective-permute-start(bf16[288,768]{1,0:T(8,128)(2,1)} %get-tuple-element.162), channel_id=1, source_target_pairs={{0,16},{1,17},{2,18},{3,19},{4,20},{5,21},{6,22},{7,23},{8,24},{9,... | collective-permute-start | bytes 1327112 | tf_op jit(solution)/shard_map/ppermute | solution.py:621
  44.9 31.3 %collective-permute-start.1 = (bf16[288,768]{1,0:T(8,128)(2,1)}, bf16[288,768]{1,0:T(8,128)(2,1)}, u32[]{:S(2)}, u32[]{:S(2)}) collective-permute-start(bf16[288,768]{1,0:T(8,128)(2,1)} %get-tuple-element.172), channel_id=1, source_target_pairs={{0,16},{1,17},{2,18},{3,19},{4,20},{5,21},{6,22},{7,23},{8,24},{9,... | collective-permute-start | bytes 1327112 | tf_op jit(solution)/shard_map/ppermute | solution.py:621
  92.3 36.9 %collective-permute-start.3 = (bf16[288,768]{1,0:T(8,128)(2,1)}, bf16[288,768]{1,0:T(8,128)(2,1)}, u32[]{:S(2)}, u32[]{:S(2)}) collective-permute-start(bf16[288,768]{1,0:T(8,128)(2,1)} %get-tuple-element.180), channel_id=1, source_target_pairs={{16,0},{17,1},{18,2},{19,3},{20,4},{21,5},{22,6},{23,7},{24,8},{25... | collective-permute-start | bytes 1327112 | tf_op jit(solution)/shard_map/ppermute | solution.py:621
  95.4 53.5 %collective-permute-start.5 = (bf16[288,768]{1,0:T(8,128)(2,1)}, bf16[288,768]{1,0:T(8,128)(2,1)}, u32[]{:S(2)}, u32[]{:S(2)}) collective-permute-start(bf16[288,768]{1,0:T(8,128)(2,1)} %get-tuple-element.212), channel_id=1, source_target_pairs={{16,0},{17,1},{18,2},{19,3},{20,4},{21,5},{22,6},{23,7},{24,8},{25... | collective-permute-start | bytes 1327112 | tf_op jit(solution)/shard_map/ppermute | solution.py:621
  99.7 70.0 %collective-permute-start.6 = (bf16[288,768]{1,0:T(8,128)(2,1)}, bf16[288,768]{1,0:T(8,128)(2,1)S(1)}, u32[]{:S(2)}, u32[]{:S(2)}) collective-permute-start(bf16[288,768]{1,0:T(8,128)(2,1)} %get-tuple-element.221), channel_id=1, source_target_pairs={{16,0},{17,1},{18,2},{19,3},{20,4},{21,5},{22,6},{23,7},{24,8},{25... | collective-permute-start | bytes 1327112 | tf_op jit(solution)/shard_map/ppermute | solution.py:621
  200.9 42.9 %collective-permute-start.7 = (bf16[8,1,192,768]{3,2,1,0:T(8,128)(2,1)}, bf16[8,1,192,768]{3,2,1,0:T(8,128)(2,1)}, u32[]{:S(2)}, u32[]{:S(2)}) collective-permute-start(bf16[8,1,192,768]{3,2,1,0:T(8,128)(2,1)} %get-tuple-element.251.refs_8_), channel_id=1, source_target_pairs={{0,1},{1,0},{2,3},{3,2},{4,5},{5,4},{6,7},{7,6},{8,9},{9,8},{10,11... | collective-permute-start | bytes 7077896 | tf_op jit(solution)/shard_map/ppermute | solution.py:509
  203.4 42.9 %collective-permute-start.13 = (bf16[8,4,48,768]{3,2,1,0:T(8,128)(2,1)}, bf16[8,4,48,768]{3,2,1,0:T(8,128)(2,1)}, u32[]{:S(2)}, u32[]{:S(2)}) collective-permute-start(bf16[8,4,48,768]{3,2,1,0:T(8,128)(2,1)} %get-tuple-element.208.refs_14_), channel_id=1, source_target_pairs={{16,18},{17,19},{18,16},{19,17},{20,22},{21,23},{22,20},{23,21},{2... | collective-permute-start | bytes 7077896 | tf_op jit(solution)/shard_map/ppermute | solution.py:509
  221.5 56.4 %collective-permute-start.12 = (bf16[8,4,48,768]{3,2,1,0:T(8,128)(2,1)}, bf16[8,4,48,768]{3,2,1,0:T(8,128)(2,1)}, u32[]{:S(2)}, u32[]{:S(2)}) collective-permute-start(bf16[8,4,48,768]{3,2,1,0:T(8,128)(2,1)} %get-tuple-element.265.refs_14_), channel_id=1, source_target_pairs={{0,2},{1,3},{2,0},{3,1},{4,6},{5,7},{6,4},{7,5},{8,10},{9,11},{10,... | collective-permute-start | bytes 7077896 | tf_op jit(solution)/shard_map/ppermute | solution.py:509
  224.9 55.5 %collective-permute-start.11 = (bf16[8,4,48,768]{3,2,1,0:T(8,128)(2,1)}, bf16[8,4,48,768]{3,2,1,0:T(8,128)(2,1)}, u32[]{:S(2)}, u32[]{:S(2)}) collective-permute-start(bf16[8,4,48,768]{3,2,1,0:T(8,128)(2,1)} %get-tuple-element.209.refs_14_), channel_id=1, source_target_pairs={{16,20},{17,21},{18,22},{19,23},{20,16},{21,17},{22,18},{23,19},{2... | collective-permute-start | bytes 7077896 | tf_op jit(solution)/shard_map/ppermute | solution.py:509
  239.8 51.3 %collective-permute-start.10 = (bf16[8,4,48,768]{3,2,1,0:T(8,128)(2,1)}, bf16[8,4,48,768]{3,2,1,0:T(8,128)(2,1)S(1)}, u32[]{:S(2)}, u32[]{:S(2)}) collective-permute-start(bf16[8,4,48,768]{3,2,1,0:T(8,128)(2,1)} %get-tuple-element.275), channel_id=1, source_target_pairs={{0,4},{1,5},{2,6},{3,7},{4,0},{5,1},{6,2},{7,3},{8,12},{9,13},{10,... | collective-permute-start | bytes 7077896 | tf_op jit(solution)/shard_map/ppermute | solution.py:509
  246.0 63.5 %collective-permute-start.9 = (bf16[4,1,192,768]{3,2,1,0:T(8,128)(2,1)S(1)}, bf16[4,1,192,768]{3,2,1,0:T(8,128)(2,1)S(1)}, u32[]{:S(2)}, u32[]{:S(2)}) collective-permute-start(bf16[4,1,192,768]{3,2,1,0:T(8,128)(2,1)S(1)} %add_convert_fusion.2), channel_id=1, source_target_pairs={{0,2},{1,3},{2,0},{3,1},{4,6},{5,7},{6,4},{7,5},{8,10},{9,11},{10,... | collective-permute-start | bytes 3538952 | tf_op jit(solution)/shard_map/ppermute | solution.py:509
  280.1 33.0 %collective-permute-start.17 = (bf16[4,4,48,768]{3,2,1,0:T(8,128)(2,1)S(1)}, bf16[4,4,48,768]{3,2,1,0:T(8,128)(2,1)S(1)}, u32[]{:S(2)}, u32[]{:S(2)}) collective-permute-start(bf16[4,4,48,768]{3,2,1,0:T(8,128)(2,1)S(1)} %add_convert_fusion), channel_id=1, source_target_pairs={{0,4},{1,5},{2,6},{3,7},{4,0},{5,1},{6,2},{7,3},{8,12},{9,13},{10,... | collective-permute-start | bytes 3538952 | tf_op jit(solution)/shard_map/ppermute | solution.py:509
  291.6 23.0 %collective-permute-start.16 = (bf16[4,4,48,768]{3,2,1,0:T(8,128)(2,1)S(1)}, bf16[4,4,48,768]{3,2,1,0:T(8,128)(2,1)S(1)}, u32[]{:S(2)}, u32[]{:S(2)}) collective-permute-start(bf16[4,4,48,768]{3,2,1,0:T(8,128)(2,1)S(1)} %add_convert_fusion.1), channel_id=1, source_target_pairs={{0,1},{1,0},{2,3},{3,2},{4,5},{5,4},{6,7},{7,6},{8,9},{9,8},{10,11... | collective-permute-start | bytes 3538952 | tf_op jit(solution)/shard_map/ppermute | solution.py:509
  293.2 16.3 %collective-permute-start.8 = (f32[13,768]{1,0:T(8,128)S(1)}, f32[13,768]{1,0:T(8,128)S(1)}, u32[]{:S(2)}, u32[]{:S(2)}) collective-permute-start(f32[13,768]{1,0:T(8,128)S(1)} %pad_maximum_fusion.9), channel_id=1, source_target_pairs={{0,1},{1,0},{2,3},{3,2},{4,5},{5,4},{6,7},{7,6},{8,9},{9,8},{10,11... | collective-permute-start | bytes 119816 | tf_op jit(solution)/shard_map/ppermute | solution.py:509
  309.7 16.3 %collective-permute-start.15 = (bf16[2,1,192,768]{3,2,1,0:T(8,128)(2,1)S(1)}, bf16[2,1,192,768]{3,2,1,0:T(8,128)(2,1)S(1)}, u32[]{:S(2)}, u32[]{:S(2)}) collective-permute-start(bf16[2,1,192,768]{3,2,1,0:T(8,128)(2,1)S(1)} %add_convert_fusion.5), channel_id=1, source_target_pairs={{0,4},{1,5},{2,6},{3,7},{4,0},{5,1},{6,2},{7,3},{8,12},{9,13},{10,... | collective-permute-start | bytes 1769480 | tf_op jit(solution)/shard_map/ppermute | solution.py:509
  313.3 16.1 %collective-permute-start.21 = (bf16[2,4,48,768]{3,2,1,0:T(8,128)(2,1)S(1)}, bf16[2,4,48,768]{3,2,1,0:T(8,128)(2,1)S(1)}, u32[]{:S(2)}, u32[]{:S(2)}) collective-permute-start(bf16[2,4,48,768]{3,2,1,0:T(8,128)(2,1)S(1)} %add_convert_fusion.3), channel_id=1, source_target_pairs={{0,1},{1,0},{2,3},{3,2},{4,5},{5,4},{6,7},{7,6},{8,9},{9,8},{10,11... | collective-permute-start | bytes 1769480 | tf_op jit(solution)/shard_map/ppermute | solution.py:509
  314.9 16.8 %collective-permute-start.20 = (bf16[2,4,48,768]{3,2,1,0:T(8,128)(2,1)S(1)}, bf16[2,4,48,768]{3,2,1,0:T(8,128)(2,1)S(1)}, u32[]{:S(2)}, u32[]{:S(2)}) collective-permute-start(bf16[2,4,48,768]{3,2,1,0:T(8,128)(2,1)S(1)} %add_convert_fusion.4), channel_id=1, source_target_pairs={{0,2},{1,3},{2,0},{3,1},{4,6},{5,7},{6,4},{7,5},{8,10},{9,11},{10,... | collective-permute-start | bytes 1769480 | tf_op jit(solution)/shard_map/ppermute | solution.py:509
  326.2 22.5 %collective-permute-start.19 = (bf16[1,1,192,768]{3,2,1,0:T(8,128)(2,1)S(1)}, bf16[1,1,192,768]{3,2,1,0:T(8,128)(2,1)S(1)}, u32[]{:S(2)}, u32[]{:S(2)}) collective-permute-start(bf16[1,1,192,768]{3,2,1,0:T(8,128)(2,1)S(1)} %add_convert_fusion.11), channel_id=1, source_target_pairs={{0,8},{1,9},{2,10},{3,11},{4,12},{5,13},{6,14},{7,15},{8,0},{9,1},... | collective-permute-start | bytes 884744 | tf_op jit(solution)/shard_map/ppermute | solution.py:509
  329.5 28.7 %collective-permute-start.24 = (bf16[1,4,48,768]{3,2,1,0:T(8,128)(2,1)S(1)}, bf16[1,4,48,768]{3,2,1,0:T(8,128)(2,1)S(1)}, u32[]{:S(2)}, u32[]{:S(2)}) collective-permute-start(bf16[1,4,48,768]{3,2,1,0:T(8,128)(2,1)S(1)} %add_convert_fusion.8), channel_id=1, source_target_pairs={{0,8},{1,9},{2,10},{3,11},{4,12},{5,13},{6,14},{7,15},{8,0},{9,1},... | collective-permute-start | bytes 884744 | tf_op jit(solution)/shard_map/ppermute | solution.py:509
  331.9 37.3 %collective-permute-start.23 = (bf16[1,4,48,768]{3,2,1,0:T(8,128)(2,1)S(1)}, bf16[1,4,48,768]{3,2,1,0:T(8,128)(2,1)S(1)}, u32[]{:S(2)}, u32[]{:S(2)}) collective-permute-start(bf16[1,4,48,768]{3,2,1,0:T(8,128)(2,1)S(1)} %add_convert_fusion.9), channel_id=1, source_target_pairs={{0,8},{1,9},{2,10},{3,11},{4,12},{5,13},{6,14},{7,15},{8,0},{9,1},... | collective-permute-start | bytes 884744 | tf_op jit(solution)/shard_map/ppermute | solution.py:509
  348.9 23.9 %collective-permute-start.27 = (bf16[1,1,192,768]{3,2,1,0:T(8,128)(2,1)S(1)}, bf16[1,1,192,768]{3,2,1,0:T(8,128)(2,1)S(1)}, u32[]{:S(2)}, u32[]{:S(2)}) collective-permute-start(bf16[1,1,192,768]{3,2,1,0:T(8,128)(2,1)S(1)} %add_convert_fusion.10), channel_id=1, source_target_pairs={{0,8},{1,9},{2,10},{3,11},{4,12},{5,13},{6,14},{7,15},{8,0},{9,1},... | collective-permute-start | bytes 884744 | tf_op jit(solution)/shard_map/ppermute | solution.py:509
  358.4 17.1 %collective-permute-start.26 = (bf16[1,4,48,768]{3,2,1,0:T(8,128)(2,1)S(1)}, bf16[1,4,48,768]{3,2,1,0:T(8,128)(2,1)S(1)}, u32[]{:S(2)}, u32[]{:S(2)}) collective-permute-start(bf16[1,4,48,768]{3,2,1,0:T(8,128)(2,1)S(1)} %add_convert_fusion.6), channel_id=1, source_target_pairs={{0,8},{1,9},{2,10},{3,11},{4,12},{5,13},{6,14},{7,15},{8,0},{9,1},... | collective-permute-start | bytes 884744 | tf_op jit(solution)/shard_map/ppermute | solution.py:509
  372.8 15.6 %collective-permute-start.30 = (bf16[2,1,192,768]{3,2,1,0:T(8,128)(2,1)S(1)}, bf16[2,1,192,768]{3,2,1,0:T(8,128)(2,1)S(1)}, u32[]{:S(2)}, u32[]{:S(2)}) collective-permute-start(bf16[2,1,192,768]{3,2,1,0:T(8,128)(2,1)S(1)} %pad_maximum_fusion.8), channel_id=1, source_target_pairs={{0,4},{1,5},{2,6},{3,7},{4,0},{5,1},{6,2},{7,3},{8,12},{9,13},{10,... | collective-permute-start | bytes 1769480 | tf_op jit(solution)/shard_map/ppermute | solution.py:509
  375.6 16.3 %collective-permute-start.29 = (bf16[2,4,48,768]{3,2,1,0:T(8,128)(2,1)S(1)}, bf16[2,4,48,768]{3,2,1,0:T(8,128)(2,1)S(1)}, u32[]{:S(2)}, u32[]{:S(2)}) collective-permute-start(bf16[2,4,48,768]{3,2,1,0:T(8,128)(2,1)S(1)} %pad_maximum_fusion.7), channel_id=1, source_target_pairs={{0,1},{1,0},{2,3},{3,2},{4,5},{5,4},{6,7},{7,6},{8,9},{9,8},{10,11... | collective-permute-start | bytes 1769480 | tf_op jit(solution)/shard_map/ppermute | solution.py:509
  380.8 12.1 %collective-permute-start.28 = (bf16[2,4,48,768]{3,2,1,0:T(8,128)(2,1)S(1)}, bf16[2,4,48,768]{3,2,1,0:T(8,128)(2,1)S(1)}, u32[]{:S(2)}, u32[]{:S(2)}) collective-permute-start(bf16[2,4,48,768]{3,2,1,0:T(8,128)(2,1)S(1)} %pad_maximum_fusion.6), channel_id=1, source_target_pairs={{0,2},{1,3},{2,0},{3,1},{4,6},{5,7},{6,4},{7,5},{8,10},{9,11},{10,... | collective-permute-start | bytes 1769480 | tf_op jit(solution)/shard_map/ppermute | solution.py:509
  388.5 23.6 %collective-permute-start.33 = (bf16[4,1,192,768]{3,2,1,0:T(8,128)(2,1)S(1)}, bf16[4,1,192,768]{3,2,1,0:T(8,128)(2,1)S(1)}, u32[]{:S(2)}, u32[]{:S(2)}) collective-permute-start(bf16[4,1,192,768]{3,2,1,0:T(8,128)(2,1)S(1)} %pad_maximum_fusion.5), channel_id=1, source_target_pairs={{0,2},{1,3},{2,0},{3,1},{4,6},{5,7},{6,4},{7,5},{8,10},{9,11},{10,... | collective-permute-start | bytes 3538952 | tf_op jit(solution)/shard_map/ppermute | solution.py:509
  392.0 26.0 %collective-permute-start.32 = (bf16[4,4,48,768]{3,2,1,0:T(8,128)(2,1)S(1)}, bf16[4,4,48,768]{3,2,1,0:T(8,128)(2,1)S(1)}, u32[]{:S(2)}, u32[]{:S(2)}) collective-permute-start(bf16[4,4,48,768]{3,2,1,0:T(8,128)(2,1)S(1)} %pad_maximum_fusion.4), channel_id=1, source_target_pairs={{0,4},{1,5},{2,6},{3,7},{4,0},{5,1},{6,2},{7,3},{8,12},{9,13},{10,... | collective-permute-start | bytes 3538952 | tf_op jit(solution)/shard_map/ppermute | solution.py:509
  393.0 29.0 %collective-permute-start.31 = (bf16[4,4,48,768]{3,2,1,0:T(8,128)(2,1)S(1)}, bf16[4,4,48,768]{3,2,1,0:T(8,128)(2,1)S(1)}, u32[]{:S(2)}, u32[]{:S(2)}) collective-permute-start(bf16[4,4,48,768]{3,2,1,0:T(8,128)(2,1)S(1)} %pad_maximum_fusion.3), channel_id=1, source_target_pairs={{0,1},{1,0},{2,3},{3,2},{4,5},{5,4},{6,7},{7,6},{8,9},{9,8},{10,11... | collective-permute-start | bytes 3538952 | tf_op jit(solution)/shard_map/ppermute | solution.py:509
  412.4 53.1 %collective-permute-start.35 = (bf16[8,1,192,768]{3,2,1,0:T(8,128)(2,1)S(1)}, bf16[8,1,192,768]{3,2,1,0:T(8,128)(2,1)S(1)}, u32[]{:S(2)}, u32[]{:S(2)}) collective-permute-start(bf16[8,1,192,768]{3,2,1,0:T(8,128)(2,1)S(1)} %pad_maximum_fusion.2.lower), channel_id=1, source_target_pairs={{0,1},{1,0},{2,3},{3,2},{4,5},{5,4},{6,7},{7,6},{8,9},{9,8},{10,11... | collective-permute-start | bytes 7077896 | tf_op jit(solution)/shard_map/ppermute | solution.py:509
  422.2 50.3 %collective-permute-start.34 = (bf16[8,4,48,768]{3,2,1,0:T(8,128)(2,1)S(1)}, bf16[8,4,48,768]{3,2,1,0:T(8,128)(2,1)S(1)}, u32[]{:S(2)}, u32[]{:S(2)}) collective-permute-start(bf16[8,4,48,768]{3,2,1,0:T(8,128)(2,1)S(1)} %pad_maximum_fusion._.lower), channel_id=1, source_target_pairs={{0,4},{1,5},{2,6},{3,7},{4,0},{5,1},{6,2},{7,3},{8,12},{9,13},{10,... | collective-permute-start | bytes 7077896 | tf_op jit(solution)/shard_map/ppermute | solution.py:509
  423.5 59.6 %collective-permute-start.36 = (bf16[8,4,48,768]{3,2,1,0:T(8,128)(2,1)S(1)}, bf16[8,4,48,768]{3,2,1,0:T(8,128)(2,1)S(1)}, u32[]{:S(2)}, u32[]{:S(2)}) collective-permute-start(bf16[8,4,48,768]{3,2,1,0:T(8,128)(2,1)S(1)} %pad_maximum_fusion.1.lower), channel_id=1, source_target_pairs={{0,2},{1,3},{2,0},{3,1},{4,6},{5,7},{6,4},{7,5},{8,10},{9,11},{10,... | collective-permute-start | bytes 7077896 | tf_op jit(solution)/shard_map/ppermute | solution.py:509
  425.1 37.3 %collective-permute-start.22 = (f32[13,768]{1,0:T(8,128)S(1)}, f32[13,768]{1,0:T(8,128)S(1)}, u32[]{:S(2)}, u32[]{:S(2)}) collective-permute-start(f32[13,768]{1,0:T(8,128)S(1)} %add.198), channel_id=1, source_target_pairs={{0,8},{1,9},{2,10},{3,11},{4,12},{5,13},{6,14},{7,15},{8,0},{9,1},... | collective-permute-start | bytes 119816 | tf_op jit(solution)/shard_map/ppermute | solution.py:509
  (107 other events, 737.5 us)

commit v3 on v2

v3 whole, which is shorter than its diff:
```python
import functools

import jax
import jax.numpy as jnp
from jax import lax
from jax.experimental import pallas as pl
from jax.experimental.pallas import tpu as pltpu
from jax.sharding import PartitionSpec as P

HEADS = 12
CHUNKS = 16
PARTS = 2
TILE = 768
UNROLL = 2
KEEP_SCALE = 4.0 / 3.0
EPS = 1e-06
F32 = jnp.float32
BF16 = jnp.bfloat16
VMEM = pl.BlockSpec(memory_space=pltpu.VMEM)
SMEM = pl.BlockSpec(memory_space=pltpu.SMEM)
ANY = pl.BlockSpec(memory_space=pl.ANY)
HBM = pl.BlockSpec(memory_space=pltpu.HBM)
AG, AC, QB, VB, PB, MG, MC, DB, UB = range(9)
NONE = 15


def dot_nn(left, right):
    return lax.dot_general(left, right, (((1,), (0,)), ((), ())), preferred_element_type=F32)


def dot_nt(left, right):
    return lax.dot_general(left, right, (((1,), (1,)), ((), ())), preferred_element_type=F32)


def dot_tn(left, right):
    return lax.dot_general(left, right, (((0,), (0,)), ((), ())), preferred_element_type=F32)


def shaped(*shape, dtype=BF16):
    return jax.ShapeDtypeStruct(shape, dtype)


def scratch(*shape, dtype=BF16):
    return pltpu.VMEM(shape, dtype)


def standardize(stream):
    centred = stream - jnp.mean(stream, axis=-1, keepdims=True)
    inverse = lax.rsqrt(jnp.mean(centred * centred, axis=-1, keepdims=True) + EPS)
    return centred * inverse, inverse


def norm_back(grad, normed, inverse):
    return inverse * (
        grad
        - jnp.mean(grad, axis=-1, keepdims=True)
        - normed * jnp.mean(grad * normed, axis=-1, keepdims=True)
    )


def lanes(start, size):
    return pl.ds(pl.multiple_of(start, 128), size)


def rows_at(start, size):
    return pl.ds(pl.multiple_of(start, 16), size)


def row_mask(length, valid):
    return lax.broadcasted_iota(jnp.int32, (length, 1), 0) < valid


class Copies:
    def __init__(self, sems):
        self.sems, self.used, self.out = sems, 0, []

    def start(self, src, dst):
        copy = pltpu.make_async_copy(src, dst, self.sems.at[self.used])
        self.used += 1
        copy.start()
        return copy

    def send(self, src, dst):
        self.out.append(self.start(src, dst))

    def finish(self):
        for copy in self.out:
            copy.wait()


def loading_forward_kernel(image, *refs):
    (act, valid, keep, ag, ac, qb, vb, pb, mg, mc, db, ub, *mats_in, x_in) = refs[:17]
    outs, vecs, mats, rest = refs[17:27], refs[27], refs[28:32], refs[32:]
    *rest, mat_sems = rest
    gets = [
        pltpu.make_async_copy(a, b, mat_sems.at[i]) for i, (a, b) in enumerate(zip(mats_in, mats))
    ]
    for get in gets:
        get.start()
    width = vecs.shape[1]
    for k, one in enumerate((ag, ac, qb, vb, pb, mg, mc, db)):
        vecs[k : k + 1, :] = one[...]
    vecs[NONE : NONE + 1, :] = jnp.zeros((1, width), F32)
    for k in range(ub.shape[1] // width):
        vecs[UB + k : UB + k + 1, :] = ub[:, k * width : (k + 1) * width]

    @pl.when(act[0] == 0)
    def _():
        for get in gets:
            get.wait()

    forward_kernel(image, 0, gets, act, valid, keep, vecs, *mats, x_in, *outs, *rest)


def forward_kernel(image, skip, gets, *refs):
    (act, valid, keep, vecs, qkvw, pw, uw, dw, x_in) = refs[:9]
    refs = refs[:9] + refs[9 + skip :]
    outs, stat, refs = refs[9:18], refs[18], refs[19:]
    (x, n1, qkv, probs, mixed, h1, n2, slope, gact, h2, sems) = refs
    (n1_out, qkv_out, probs_out, mixed_out, h1_out, n2_out, slope_out, gact_out, h2_out) = outs
    length, width = x.shape
    hidden = uw.shape[1]
    tiles = width // TILE
    low = lax.broadcasted_iota(jnp.int32, (1, 128), 1) < 64

    @pl.when(act[0] == 1)
    def _():
        copies = Copies(sems)
        get_x = copies.start(x_in, x)

        get_x.wait()
        normed, _inv = standardize(x[...].astype(F32))
        n1[...] = (normed * vecs[AG : AG + 1, :] + vecs[AC : AC + 1, :]).astype(BF16)
        copies.send(n1, n1_out)
        if gets:
            gets[0].wait()

        def project(t, _):
            part = t // tiles
            at = lanes(t * TILE, TILE)
            bias = jnp.where(part == 0, QB, jnp.where(part == 1, NONE, VB))
            out = dot_nn(n1[...], qkvw[:, at])
            out = out + vecs[pl.ds(bias, 1), lanes((t - part * tiles) * TILE, TILE)]
            qkv[:, at] = (out * jnp.where(part == 0, 0.125, 1.0)).astype(BF16)
            return 0

        lax.fori_loop(0, 3 * tiles, project, 0)
        copies.send(qkv, qkv_out)

        live = lax.broadcasted_iota(jnp.int32, (1, length), 1) < valid[image]

        def pair(p, _):
            q = qkv[:, lanes(p * 128, 128)]
            k = qkv[:, lanes(width + p * 128, 128)]
            v = qkv[:, lanes(2 * width + p * 128, 128)]
            zero = jnp.zeros_like(q)
            stacked = jnp.concatenate([jnp.where(low, q, zero), jnp.where(low, zero, q)], axis=0)
            scores = dot_nt(stacked, k)
            scores = jnp.where(live, scores, -1e30)
            top = jnp.max(scores, axis=-1, keepdims=True)
            e = jnp.exp(scores - top)
            total = jnp.sum(e, axis=-1, keepdims=True)
            prob = (e * (1.0 / total)).astype(BF16)
            probs[rows_at(p * 2 * length, 2 * length), :] = prob
            out = dot_nn(prob, v)
            mixed[:, lanes(p * 128, 128)] = jnp.where(low, out[:length], out[length:]).astype(BF16)
            return 0

        lax.fori_loop(0, width // 128, pair, 0, unroll=UNROLL)
        copies.send(probs, probs_out)
        copies.send(mixed, mixed_out)

        mask = row_mask(length, valid[image])
        if gets:
            gets[1].wait()
            gets[2].wait()

        def attend_out(t, total):
            at = lanes(t * TILE, TILE)
            a = keep[2 * image] * (dot_nn(mixed[...], pw[:, at]) + vecs[PB : PB + 1, at])
            h1[:, at] = x[:, at].astype(F32) + a
            return total + jnp.sum(jnp.where(mask, a * a, 0.0))

        stat[1] = lax.fori_loop(0, tiles, attend_out, 0.0)
        normed, _inv = standardize(h1[...])
        n2[...] = (normed * vecs[MG : MG + 1, :] + vecs[MC : MC + 1, :]).astype(BF16)
        copies.send(h1, h1_out)
        copies.send(n2, n2_out)


        for block in range(hidden // width):

            def tile(t, _, block=block):
                at = lanes(block * width + t * TILE, TILE)
                u = dot_nn(n2[...], uw[:, at]) + vecs[UB + block : UB + block + 1, lanes(t * TILE, TILE)]
                cdf = 0.5 * (1.0 + lax.erf(u * 0.7071067811865476))
                gact[:, at] = (u * cdf).astype(BF16)
                slope[:, at] = (cdf + u * (jnp.exp(-0.5 * u * u) * 0.3989422804014327)).astype(BF16)
                return 0

            lax.fori_loop(0, tiles, tile, 0)
            at = slice(block * width, (block + 1) * width)
            copies.send(gact.at[:, at], gact_out.at[:, at])
            copies.send(slope.at[:, at], slope_out.at[:, at])

        if gets:
            gets[3].wait()

        def down(t, total):
            at = lanes(t * TILE, TILE)
            m = keep[2 * image + 1] * (dot_nn(gact[...], dw[:, at]) + vecs[DB : DB + 1, at])
            h = h1[:, at] + m
            h2[:, at] = h.astype(BF16)
            return (
                total[0] + jnp.sum(jnp.where(mask, h * h, 0.0)),
                total[1] + jnp.sum(jnp.where(mask, m * m, 0.0)),
            )

        stat[0], stat[2] = lax.fori_loop(0, tiles, down, (0.0, 0.0))
        copies.send(h2, h2_out)
        copies.finish()


def backward_kernel(image, skip, *refs):
    (act, valid, keep, vecs, dw, uw, pw, qkvw) = refs[:8]
    (seed_in, slope_in, h1_in, qkv_in, mixed_in, probs_in, x_in) = refs[8:15]
    refs = refs[15 + skip :]
    (du_out, dy_out, dj_out, dx_out, vec) = refs[:5]
    (seed, slope, h1, qkv, mixed, probs, x, du, dy, dj, dx, dmix, dh1, wide, sems) = refs[5:]
    length, width = x.shape
    hidden = uw.shape[1]
    low = lax.broadcasted_iota(jnp.int32, (1, 128), 1) < 64

    @pl.when(act[0] == 1)
    def _():
        copies = Copies(sems)
        get_seed = copies.start(seed_in, seed)
        get_slope = copies.start(slope_in, slope)
        get_h1 = copies.start(h1_in, h1)
        get = [
            copies.start(a, b) for a, b in ((qkv_in, qkv), (mixed_in, mixed), (probs_in, probs))
        ]
        get_x = copies.start(x_in, x)

        get_seed.wait()
        given = jnp.where(row_mask(length, valid[image]), seed[...].astype(F32), 0.0)
        z = (keep[2 * image + 1] * given).astype(BF16)
        dx[...] = z
        vec[3:4, :] = jnp.sum(z.astype(F32), axis=0, keepdims=True)
        get_slope.wait()
        tiles = width // TILE

        def tile(t, _):
            at = lanes(t * TILE, TILE)
            d = dot_nt(dx[...], dw[rows_at(t * TILE, TILE), :])
            d = (d * slope[:, at].astype(F32)).astype(BF16)
            du[:, at] = d
            vec[pl.ds(4 + t // tiles, 1), lanes((t % tiles) * TILE, TILE)] = jnp.sum(
                d.astype(F32), axis=0, keepdims=True
            )
            return 0

        lax.fori_loop(0, hidden // TILE, tile, 0)
        copies.send(du, du_out)
        get_h1.wait()

        def up_in(t, _):
            wide[:, lanes(t * TILE, TILE)] = dot_nt(du[...], uw[rows_at(t * TILE, TILE), :])
            return 0

        lax.fori_loop(0, tiles, up_in, 0)
        dn2 = wide[...]
        normed, inverse = standardize(h1[...])
        vec[1:2, :] = jnp.sum(dn2 * normed, axis=0, keepdims=True)
        vec[2:3, :] = jnp.sum(dn2, axis=0, keepdims=True)
        given = jnp.where(row_mask(length, valid[image]), seed[...].astype(F32), 0.0)
        d = given + norm_back(dn2 * vecs[MG : MG + 1, :], normed, inverse)
        dh1[...] = d
        y = (keep[2 * image] * d).astype(BF16)
        dy[...] = y
        vec[0:1, :] = jnp.sum(y.astype(F32), axis=0, keepdims=True)
        copies.send(dy, dy_out)

        def mix_in(t, _):
            dmix[:, lanes(t * TILE, TILE)] = dot_nt(dy[...], pw[rows_at(t * TILE, TILE), :]).astype(BF16)
            return 0

        lax.fori_loop(0, tiles, mix_in, 0)
        for copy in get:
            copy.wait()

        def pair(p, _):
            at = lanes(p * 128, 128)
            k_at = lanes(width + p * 128, 128)
            v_at = lanes(2 * width + p * 128, 128)
            q = qkv[:, at]
            k = qkv[:, k_at]
            v = qkv[:, v_at]
            g = dmix[:, at]

            def stack(a):
                zero = jnp.zeros_like(a)
                return jnp.concatenate([jnp.where(low, a, zero), jnp.where(low, zero, a)], axis=0)

            both = stack(g)
            prod = g.astype(F32) * mixed[:, at].astype(F32)
            side = jnp.concatenate(
                [
                    jnp.sum(jnp.where(low, prod, 0.0), axis=-1, keepdims=True),
                    jnp.sum(jnp.where(low, 0.0, prod), axis=-1, keepdims=True),
                ],
                axis=0,
            )
            prob = probs[rows_at(p * 2 * length, 2 * length), :]
            dp = dot_nt(both, v)
            ds = (prob.astype(F32) * (dp - side)).astype(BF16)
            dj[:, v_at] = dot_tn(prob, both).astype(BF16)
            dq = dot_nn(ds, k)
            dj[:, at] = (0.125 * jnp.where(low, dq[:length], dq[length:])).astype(BF16)
            dj[:, k_at] = dot_tn(ds, stack(q)).astype(BF16)
            return 0

        lax.fori_loop(0, width // 128, pair, 0, unroll=UNROLL)
        copies.send(dj, dj_out)
        get_x.wait()
        vec[10:11, :] = jnp.sum(dj[:, 0:width].astype(F32), axis=0, keepdims=True)
        vec[11:12, :] = jnp.sum(dj[:, 2 * width :].astype(F32), axis=0, keepdims=True)

        def stream_in(t, _):
            wide[:, lanes(t * TILE, TILE)] = dot_nt(dj[...], qkvw[rows_at(t * TILE, TILE), :])
            return 0

        lax.fori_loop(0, tiles, stream_in, 0)
        dn1 = wide[...]
        normed, inverse = standardize(x[...].astype(F32))
        vec[8:9, :] = jnp.sum(dn1 * normed, axis=0, keepdims=True)
        vec[9:10, :] = jnp.sum(dn1, axis=0, keepdims=True)
        d = dh1[...] + norm_back(dn1 * vecs[AG : AG + 1, :], normed, inverse)
        dx[...] = d.astype(BF16)
        copies.send(dx, dx_out)
        copies.finish()


def grad_kernel(kind, images, skip, *refs):
    section, codes, valid, keep, refs = *refs[:4], refs[4:]
    groups = {0: 2, 1: 2, 2: 4}[kind]
    n = images
    ins = [refs[k * n : (k + 1) * n] for k in range(2 * groups)]
    refs = refs[2 * groups * n + skip :]
    lower, upper = refs[:PARTS], refs[PARTS : 2 * PARTS]
    thin, wide, full, sems = refs[2 * PARTS :]
    blocks, width, _ = full.shape
    rows = lower[0].shape[1]
    per = width // (rows * PARTS)
    length = ins[0][0].shape[0]
    copies = Copies(sems)

    def load(group, to, at=slice(None)):
        gets = []
        for i in range(images):
            both = [
                pltpu.make_async_copy(
                    ins[s * groups + group][i].at[:, at],
                    to.at[pl.ds(i * length, length), :],
                    sems.at[copies.used],
                )
                for s in (0, 1)
            ]
            copies.used += 1
            pl.when(section[0] == 0)(both[0].start)
            pl.when(section[0] == 1)(both[1].start)
            gets.append(both[0])
        return gets

    def column(b):
        return slice(b * width, (b + 1) * width)

    get_thin = load(0, thin.at[0])
    tail = 1 if kind == 2 else 0
    get_wide = [load(1, wide.at[b], column(b)) for b in range(blocks - tail)]
    if tail:
        get_thin_2 = load(2, thin.at[1])
        get_wide.append(get_thin_2 + load(3, wide.at[blocks - 1]))
    for get in get_thin:
        get.wait()
    if kind == 0:
        for i in range(images):
            r = slice(i * length, (i + 1) * length)
            z = jnp.where(row_mask(length, valid[i]), thin[0, r, :].astype(F32), 0.0)
            thin[0, r, :] = (keep[2 * i + 1] * z).astype(BF16)
    for b in range(blocks):
        for get in get_wide[b]:
            get.wait()
        which = 1 if tail and b == blocks - 1 else 0

        def tile(t, _, b=b, which=which):
            at = lanes(t * TILE, TILE)
            if kind == 0:
                full[b, rows_at(t * TILE, TILE), :] = dot_tn(wide[b, :, at], thin[0]).astype(BF16)
            else:
                full[b, :, at] = dot_tn(thin[which], wide[b, :, at]).astype(BF16)
            return 0

        lax.fori_loop(0, width // TILE, tile, 0)

        for c in range(per * PARTS):
            part = c % PARTS
            place = jnp.bitwise_xor(codes[kind * PARTS + part], b * per + c // PARTS)
            source = full.at[b, c * rows : (c + 1) * rows, :]
            sem = sems.at[copies.used]
            copies.used += 1

            @pl.when(place < CHUNKS // 2)
            def _(source=source, to=lower[part], place=place, sem=sem):
                pltpu.make_async_copy(source, to.at[place], sem).start()

            @pl.when(place >= CHUNKS // 2)
            def _(source=source, to=upper[part], place=place, sem=sem):
                pltpu.make_async_copy(source, to.at[place - CHUNKS // 2], sem).start()

            copies.out.append(pltpu.make_async_copy(source, lower[part].at[0], sem))
    copies.finish()


def call(body, scalars, vecs, arrays, over, after, outs, held, copies, flops, limit):
    tail = [*after, *(o for o, _ in over)]
    ops = (*scalars, *vecs, *(held_in(pltpu.HBM, a) for a in (*arrays, *tail)))
    first = len(scalars) + len(vecs) + len(arrays) + len(after)

    def place(o):
        if isinstance(o, pl.MemoryRef):
            return VMEM
        if o.shape == (8,):
            return SMEM
        return VMEM if o.dtype == F32 and o.shape[0] == 16 else HBM

    moved = sum(o.size * o.dtype.itemsize for o in arrays)
    return pl.pallas_call(
        body,
        out_shape=[pltpu.HBM(o.shape, o.dtype) if place(o) is HBM else o for o in outs],
        in_specs=[SMEM] * len(scalars) + [VMEM] * len(vecs) + [HBM] * (len(arrays) + len(tail)),
        out_specs=[place(o) for o in outs],
        scratch_shapes=[*held, pltpu.SemaphoreType.DMA((copies,))],
        input_output_aliases={first + k: out for k, (_, out) in enumerate(over)},
        compiler_params=pltpu.CompilerParams(vmem_limit_bytes=limit << 20),
        cost_estimate=pl.CostEstimate(flops=int(flops), bytes_accessed=int(moved), transcendentals=0),
    )(*ops)


def held_in(space, array):
    return pltpu.with_memory_space_constraint(array, space)


def like(*arrays):
    return [scratch(*a.shape, dtype=a.dtype) for a in arrays]


def forward(act, valid, keep, x, vecs, mats, image, after, load=False):
    qkvw, pw, uw, dw = mats
    length, width = x.shape
    hidden = uw.shape[1]
    thin, wide = shaped(length, width), shaped(length, hidden)
    outs = [
        thin,
        shaped(length, 3 * width),
        shaped(HEADS * length, length),
        thin,
        shaped(length, width, dtype=F32),
        thin,
        wide,
        wide,
        thin,
    ]
    held = like(x, *outs)
    stat = shaped(8, dtype=F32)
    copies = 8 + 2 * hidden // width
    flops = 2 * length * width * width * 14
    if load:
        loaded = [stat, shaped(16, width, dtype=F32), *(pltpu.VMEM(m.shape, m.dtype) for m in mats)]
        got = call(
            functools.partial(loading_forward_kernel, image),
            (act, valid, keep),
            vecs,
            (qkvw, pw, uw, dw, x),
            (),
            (),
            [*outs, *loaded],
            [*held, pltpu.SemaphoreType.DMA((copies,))],
            len(mats),
            flops=flops,
            limit=36,
        )
        return got[8], got[9], (x, *got[:8]), got[10], [held_in(pltpu.VMEM, m) for m in got[11:]]
    *saved, h2, stat = call(
        functools.partial(forward_kernel, image, len(after), ()),
        (act, valid, keep),
        (vecs, qkvw, pw, uw, dw),
        (x,),
        (),
        after,
        [*outs, stat],
        held,
        copies,
        flops=flops,
        limit=36,
    )
    return h2, stat, (x, *saved)


def backward(act, valid, keep, seed, saved, vecs, mats, image, after):
    qkvw, pw, uw, dw = mats
    (x, n1, qkv, probs, mixed, h1, n2, slope, gact) = saved
    length, width = x.shape
    thin = shaped(length, width)
    outs = [slope, thin, qkv, thin]
    ins = (seed, slope, h1, qkv, mixed, probs, x)
    return call(
        functools.partial(backward_kernel, image, len(after)),
        (act, valid, keep),
        (vecs, dw, uw, pw, qkvw),
        ins,
        (),
        after,
        [*outs, shaped(16, width, dtype=F32)],
        like(*ins, *outs, thin, h1, h1),
        11,
        flops=2 * length * width * width * 16,
        limit=36,
    )


def weight_grad(kind, scalars, groups, width, after):
    images = len(groups[0])
    length = groups[0][0].shape[0]
    total = images * length
    held = [scratch(2 if kind == 2 else 1, total, width), scratch(4, total, width)]
    half = shaped(CHUNKS // 2, 4 * width // (CHUNKS * PARTS), width)
    got = call(
        functools.partial(grad_kernel, kind, images, len(after)),
        scalars,
        (),
        [one for g in groups for one in g],
        (),
        after,
        [half] * (2 * PARTS),
        [*held, scratch(4, width, width)],
        (5 if kind < 2 else 6) * images + CHUNKS * PARTS,
        flops=2 * images * length * 4 * width * width,
        limit=36,
    )
    return list(zip(got[:PARTS], got[PARTS:]))


def orders(bits):
    if bits == 4:
        return (
            ((0, 1, 2, 3), (0, 1, 2, 3)),
            ((1, 0, 2, 3), (2, 0, 1, 3)),
            ((0, 2, 1, 3), (2, 3, 0, 1)),
            ((1, 0, 2, 3), (1, 0, 2, 3)),
            ((2, 0, 1, 3), (2, 0, 1, 3)),
            ((1, 0, 2, 3), (0, 1, 2, 3)),
        )
    plain = (tuple(range(bits)),) * 2
    return (plain,) * (3 * PARTS)


def flipped(block, bits, sections, size):
    route = [(s * size + i, s * size + (i ^ (1 << bits[s]))) for s in sections for i in range(size)]
    return lax.ppermute(block, ("section", "dp"), route)


def chunk_code(order, place):
    code = jnp.zeros((), jnp.int32)
    for k, bit in enumerate(order):
        code = code + (((place >> bit) & 1) << (len(order) - 1 - k))
    return code


STEPS = (
    (2, 1), (1, 1), (3, 1), (0, 1), (6, 0), (3, 2), (1, 2), (0, 2), (3, 3), (5, 1), (1, 3), (6, 1),
    (2, 2), (0, 3), (4, 1), (1, 4), (5, 2), (0, 4), (6, 2), (3, 4), (1, 5), (4, 2), (2, 3), (3, 5),
    (4, 3), (6, 3), (1, 6), (0, 5), (5, 3), (2, 4), (3, 6), (0, 6), (4, 4), (5, 4), (1, 7), (0, 7),
    (2, 5), (5, 5), (4, 5), (2, 6), (3, 7), (4, 6), (2, 7), (5, 6), (4, 7), (5, 7),
)


class Sum:
    def __init__(self, lower, order, first):
        self.lower, self.order, self.arrived, self.have = lower, order, [first], None

    def send(self, step, after):
        if step < 5:
            low, high = (8 >> step, 16 >> step) if step < 4 else (0, 1)
            parts = [a[low:high].astype(F32) for a in (self.lower, *self.arrived)]
            block = sum(parts[1:], parts[0]).astype(BF16)
        else:
            block = jnp.concatenate([self.have, self.last])
        block, _ = lax.optimization_barrier((block, after))
        return block

    def run(self, step, after, size):
        block = self.send(step, after)
        bits = [o[step] if step < 4 else o[7 - step] for o in self.order]
        got = flipped(block, bits, (0, 1), size)
        if step < 4:
            self.arrived.append(got)
        else:
            self.have, self.last = block, got
        return block


def settle_kernel(kind, start, skip, code, *refs):
    halves, refs = refs[:PARTS], refs[PARTS + skip :]
    outs, (wide, sems) = refs[:-2], refs[-2:]
    count, rows, width = halves[0].shape
    waits = []
    for part, half in enumerate(halves):
        for k in range(count):
            slot = part * count + k
            wide[slot] = half[k].astype(F32)
            chunk = jnp.bitwise_xor(code[part], start + k)
            row = (chunk * PARTS + part) * rows
            block = row // width
            sem = sems.at[slot]
            if kind == 0:
                to = outs[0].at[pl.ds(pl.multiple_of(row, 8), rows), :]
                pltpu.make_async_copy(wide.at[slot], to, sem).start()
            else:
                at = pl.ds(pl.multiple_of(row - block * width, 8), rows)
                blocks = outs[0].shape[1] // width

                def first(slot=slot, at=at, block=block, sem=sem):
                    to = outs[0].at[at, pl.ds(pl.multiple_of(block * width, 128), width)]
                    pltpu.make_async_copy(wide.at[slot], to, sem).start()

                def second(slot=slot, at=at, sem=sem):
                    pltpu.make_async_copy(wide.at[slot], outs[1].at[at, :], sem).start()

                if kind == 1:
                    first()
                else:
                    pl.when(block < blocks)(first)
                    pl.when(block >= blocks)(second)
            waits.append(pltpu.make_async_copy(wide.at[slot], outs[0].at[0:rows, 0:width], sem))
    for wait in waits:
        wait.wait()


def settle(kind, start, codes, halves, outs, over):
    count, rows, width = halves[0].shape
    return pl.pallas_call(
        functools.partial(settle_kernel, kind, start, len(over)),
        out_shape=[pltpu.HBM(o.shape, F32) for o in outs],
        in_specs=[SMEM] + [VMEM] * PARTS + [HBM] * len(over),
        out_specs=[HBM] * len(outs),
        scratch_shapes=[
            scratch(PARTS * count, rows, width, dtype=F32),
            pltpu.SemaphoreType.DMA((PARTS * count,)),
        ],
        input_output_aliases={1 + PARTS + k: k for k in range(len(over))},
        compiler_params=pltpu.CompilerParams(vmem_limit_bytes=16 << 20),
    )(jnp.stack(codes), *halves, *(held_in(pltpu.HBM, o) for o in over))


def per_device(size, ends, counts, keep, *params):
    ag, ac, qkvw, qb, vb, pw, pb, mg, mc, uw, ub, dw, db = params
    mats = [item[0] for item in (qkvw, pw, uw, dw)]
    section = lax.axis_index("section")
    place = lax.axis_index("dp")
    first = section == 0
    images, slots, width = ends.shape[1:]
    hidden = ub.shape[1]
    blocks = hidden // width
    vecs = (ag, ac, qb, vb, pb, mg, mc, db, ub)
    length = -(-slots // 32) * 32
    bits = size.bit_length() - 1
    ways = orders(bits)
    starts = [[o[0] for o in way] for way in ways]
    if size == CHUNKS:
        codes = [jnp.where(first, *(chunk_code(o, place) for o in way)) for way in ways]
    else:
        codes = [jnp.zeros((), jnp.int32)] * (3 * PARTS)
    coded = jnp.stack(codes)
    acts = [(section == s).astype(jnp.int32).reshape(1) for s in (0, 1)]
    keeping = (keep[0].astype(F32) * KEEP_SCALE).reshape(-1)
    live = (jnp.arange(slots)[None, :] < counts[:, None])[..., None]

    def padded(block):
        return jnp.pad(block, ((0, length - slots), (0, 0)))

    def crossed(block, source):
        route = [(source * size + i, (1 - source) * size + i) for i in range(size)]
        return lax.ppermute(block, ("section", "dp"), route)

    every = range(images)
    early = size == CHUNKS
    acts_on = {0: acts[0], 1: acts[1]}
    token = []

    def forwards(which, xs, start):
        ran = list(start)
        for i in range(len(ran), images):
            ran.append(forward(acts_on[which], counts, keeping, xs[i], vecs, mats, i, list(token)))
            token[:] = [ran[-1][2][1]]
        return ran

    def backwards(which, seeds, kept):
        back = []
        for i in every:
            back.append(
                backward(acts_on[which], counts, keeping, seeds[i], kept[i], vecs, mats, i, list(token))
            )
            token[:] = [back[-1][0]]
        return back

    def grads(kind, *groups):
        scalars = (section.astype(jnp.int32).reshape(1), coded, counts, keeping)
        halves = weight_grad(kind, scalars, groups, width, list(token))
        token[:] = [halves[0][0]]
        return halves

    def column(kept, k):
        return [one[k] for one in kept]

    x0 = [padded(ends[0, i]) for i in every]
    *one, vecs, mats = forward(acts[0], counts, keeping, x0[0], vecs, mats, 0, (), True)
    token[:] = [one[2][1]]
    ran0 = forwards(0, x0, [one])
    x1 = [crossed(ran0[i][0], 0) for i in every]
    ran1 = forwards(1, x1, ())
    kept0, kept1 = ([r[2] for r in ran] for ran in (ran0, ran1))

    back1 = backwards(1, x0, kept1)
    seed0 = [crossed(back1[i][3], 1) for i in every]
    back0 = backwards(0, seed0, kept0)
    pa = grads(0, seed0, column(kept0, 8), x0, column(kept1, 8))
    pb = grads(1, column(kept0, 6), column(back0, 0), column(kept1, 6), column(back1, 0))
    sources = [
        part
        for kept, back in ((kept0, back0), (kept1, back1))
        for part in (column(kept, 1), column(back, 2), column(kept, 4), column(back, 1))
    ]
    pc = grads(2, *sources)

    def both(a, b):
        return jnp.where(first, sum(a[1:], a[0]), sum(b[1:], b[0]))

    made = both(column(back0, 4), column(back1, 4))
    stats = both(column(ran0, 1), column(ran1, 1))[:3]
    extra = jnp.concatenate([stats, jnp.sum(counts.astype(F32)).reshape(1)])
    extra = jnp.pad(extra, (0, width - 4)).reshape(1, width)
    vec = jnp.concatenate([made[:12], extra])

    pieces = [*pa, *pb, *pc]
    if early:
        sums = []
        for p, way, start in zip(pieces, ways, starts):
            sums.append(Sum(p[0], way, flipped(p[1], start, (0, 1), size)))
        after = pc[0][0]
        for which, step in STEPS:
            if which == len(sums):
                vec, _ = lax.optimization_barrier((vec, after))
                after = vec
                vec = vec + flipped(vec, (step, step), (0, 1), size)
                if step == bits - 1:
                    after = vec
            else:
                after = sums[which].run(step, after, size)
        halves = [(s.have, s.last) for s in sums]
    else:
        halves = [lax.psum(p, "dp") for p in pieces]
        for bit in range(bits):
            vec = vec + flipped(vec, (bit, bit), (0, 1), size)

    shapes = (
        [shaped(hidden, width)],
        [shaped(width, hidden)],
        [shaped(width, 3 * width), shaped(width, width)],
    )

    def settled(half, over):
        done = []
        for k in range(3):
            mine = slice(k * PARTS, (k + 1) * PARTS)
            some = [h[half] for h in halves[mine]]
            done.append(settle(k, half * CHUNKS // 2, codes[mine], some, shapes[k], over[k]))
        return done

    (g_down,), (g_up,), (g_qkv, g_proj) = settled(1, settled(0, ((), (), ())))

    shown = jnp.stack([jnp.where(first, back0[i][3], ran1[i][0])[:slots] for i in every])
    shown = jnp.where(live, shown, jnp.zeros((), BF16))[None]
    rms = jnp.sqrt(vec[-1, 0:3] / (vec[-1, 3] * width)).reshape(1, 3)
    row = lambda k: vec[k : k + 1]
    return (
        shown,
        row(8),
        row(9),
        g_qkv[None],
        row(10),
        row(11),
        g_proj[None],
        row(0),
        row(1),
        row(2),
        g_up[None],
        vec[4 : 4 + blocks].reshape(1, hidden),
        g_down[None],
        row(3),
        rms,
    )


def solution(mesh):
    flat = P("section", None)
    deep = P("section", None, None)
    split = P("section", "dp", None, None)
    ranks = (flat, flat, deep, flat, flat, deep, flat, flat, flat, deep, flat, deep, flat)
    return jax.shard_map(
        functools.partial(per_device, mesh.shape["dp"]),
        mesh=mesh,
        in_specs=(split, P("dp"), P("section", "dp", None), *ranks),
        out_specs=(split, *ranks, flat),
        check_vma=False,
    )
```

time: 502 us -> 425 us (0.85)
  the two profiles are of different devices: /device:TPU:8 before, /device:TPU:0 now
where the time goes in v3:
time: 425 us; the launch traced here: 419 us
  Pallas kernels  164 us (39%)
  waiting for transfers between devices  149 us (35%)
  starting transfers between devices  78.6 us (18%)
  local copies, waits for them, and re-layouts  16.3 us (4%)
  other arithmetic  8.07 us (2%)
    ppermute x52, waiting for transfers between devices, flipped(): return lax.ppermute(block, ('section', 'dp'), route)  149 us
    pallas_call x15, Pallas kernels, call(): pl.pallas_call(body, out_shape=[pltpu.HBM(o.shape, o.dtype) if place(o) i...  147 us
    ppermute x52, starting transfers between devices, flipped(): return lax.ppermute(block, ('section', 'dp'), route)  62.1 us
    pallas_call x6, Pallas kernels, settle(): pl.pallas_call(functools.partial(settle_kernel, kind, start, len(over)),...  17.2 us
    ppermute x6, starting transfers between devices, crossed(): return lax.ppermute(block, ('section', 'dp'), route)  16.6 us
    unnamed x88, local copies, waits for them, and re-layouts  10.3 us
  transfers between devices with their start and end apart: 58, of which 22 were waited for; matrix products, arithmetic and copies ran while one was open for 3% of the time, Pallas kernels for 23%

profile of v3, /device:TPU:0, one launch (start us, length us, event | category | flops | bytes accessed | tf_op | source)
XLA Modules:
  0.0 419.1 jit_solution(2268602386107666409)
XLA Ops:
  3.9 18.7 %shard_map.271 = (bf16[288,768]{1,0:T(8,128)(2,1)}, bf16[288,2304]{1,0:T(8,128)(2,1)}, bf16[3456,288]{1,0:T(8,128)(2,1)}, bf16[288,768]{1,0:T(8,128)(2,1)}, f32[...) custom-call(s32[1]{0:T(128)} %bitcast.refs_0_, ...), custom_call_target="tpu_custom_call" | custom-call | flops 4756340736 | bytes 14598144 | tf_op jit(solution)/shard_map/pallas_call | solution.py:438
  26.8 14.4 %shard_map.272 = (bf16[288,768]{1,0:T(8,128)(2,1)}, bf16[288,2304]{1,0:T(8,128)(2,1)}, bf16[3456,288]{1,0:T(8,128)(2,1)}, bf16[288,768]{1,0:T(8,128)(2,1)}, f32[...) custom-call(s32[1]{0:T(128)} %bitcast.refs_0_, ...), custom_call_target="tpu_custom_call" | custom-call | flops 4756340736 | bytes 442368 | tf_op jit(solution)/shard_map/pallas_call | solution.py:438
  44.1 14.4 %shard_map.273 = (bf16[288,768]{1,0:T(8,128)(2,1)}, bf16[288,2304]{1,0:T(8,128)(2,1)}, bf16[3456,288]{1,0:T(8,128)(2,1)}, bf16[288,768]{1,0:T(8,128)(2,1)}, f32[...) custom-call(s32[1]{0:T(128)} %bitcast.refs_0_, ...), custom_call_target="tpu_custom_call" | custom-call | flops 4756340736 | bytes 442368 | tf_op jit(solution)/shard_map/pallas_call | solution.py:438
  69.5 5.2 %shard_map.275 = (bf16[288,768]{1,0:T(8,128)(2,1)}, bf16[288,2304]{1,0:T(8,128)(2,1)}, bf16[3456,288]{1,0:T(8,128)(2,1)}, bf16[288,768]{1,0:T(8,128)(2,1)}, f32[...) custom-call(s32[1]{0:T(128)} %bitcast.6.refs_0_, ...), custom_call_target="tpu_custom_call" | custom-call | flops 4756340736 | bytes 442368 | tf_op jit(solution)/shard_map/pallas_call | solution.py:438
  74.7 8.5 %shard_map.276 = (bf16[288,768]{1,0:T(8,128)(2,1)}, bf16[288,2304]{1,0:T(8,128)(2,1)}, bf16[3456,288]{1,0:T(8,128)(2,1)}, bf16[288,768]{1,0:T(8,128)(2,1)}, f32[...) custom-call(s32[1]{0:T(128)} %bitcast.6.refs_0_, ...), custom_call_target="tpu_custom_call" | custom-call | flops 4756340736 | bytes 442368 | tf_op jit(solution)/shard_map/pallas_call | solution.py:438
  83.9 6.9 %collective-permute-start.3 = (bf16[288,768]{1,0:T(8,128)(2,1)}, bf16[288,768]{1,0:T(8,128)(2,1)S(1)}, u32[]{:S(2)}, u32[]{:S(2)}) collective-permute-start(bf16[288,768]{1,0:T(8,128)(2,1)} %get-tuple-element.191), channel_id=1, source_target_pairs={{16,0},{17,1},{18,2},{19,3},{20,4},{21,5},{22,6},{23,7},{24,8},{25... | collective-permute-start | bytes 1327112 | tf_op jit(solution)/shard_map/ppermute | solution.py:694
  95.9 20.1 %shard_map.280 = (bf16[288,3072]{1,0:T(8,128)(2,1)}, bf16[288,768]{1,0:T(8,128)(2,1)}, bf16[288,2304]{1,0:T(8,128)(2,1)}, bf16[288,768]{1,0:T(8,128)(2,1)}, f32[16,768]{1,0:T(8,128)S(1)}) custom-call(s32[1]{0:T(128)} %bitcast.refs_0_, s32[3]{0:T(128)S(1)} %copy-done.10, f32[6]{0:T(128)S(1)} %mul.14.refs_2_.refs_3_, f32[16,768]{1,0:T(8,128)S(1)} %copy-done.9, ...), custom_call_target="tpu_custom_call" | custom-call | flops 5435817984 | bytes 7299072 | tf_op jit(solution)/shard_map/pallas_call | solution.py:438
  116.8 14.2 %shard_map.281 = (bf16[288,3072]{1,0:T(8,128)(2,1)}, bf16[288,768]{1,0:T(8,128)(2,1)}, bf16[288,2304]{1,0:T(8,128)(2,1)}, bf16[288,768]{1,0:T(8,128)(2,1)}, f32[16,768]{1,0:T(8,128)S(1)}) custom-call(s32[1]{0:T(128)} %bitcast.refs_0_, s32[3]{0:T(128)S(1)} %copy-done.10, f32[6]{0:T(128)S(1)} %mul.14.refs_2_.refs_3_, f32[16,768]{1,0:T(8,128)S(1)} %copy-done.9, ...), custom_call_target="tpu_custom_call" | custom-call | flops 5435817984 | bytes 7299072 | tf_op jit(solution)/shard_map/pallas_call | solution.py:438
  131.8 14.6 %shard_map.282 = (bf16[288,3072]{1,0:T(8,128)(2,1)}, bf16[288,768]{1,0:T(8,128)(2,1)}, bf16[288,2304]{1,0:T(8,128)(2,1)}, bf16[288,768]{1,0:T(8,128)(2,1)}, f32[16,768]{1,0:T(8,128)S(1)}) custom-call(s32[1]{0:T(128)} %bitcast.refs_0_, s32[3]{0:T(128)S(1)} %copy-done.10, f32[6]{0:T(128)S(1)} %mul.14.refs_2_.refs_3_, f32[16,768]{1,0:T(8,128)S(1)} %copy-done.9, ...), custom_call_target="tpu_custom_call" | custom-call | flops 5435817984 | bytes 7299072 | tf_op jit(solution)/shard_map/pallas_call | solution.py:438
  146.3 11.0 %shard_map.283 = (bf16[8,96,768]{2,1,0:T(8,128)(2,1)}, bf16[8,96,768]{2,1,0:T(8,128)(2,1)}, bf16[8,96,768]{2,1,0:T(8,128)(2,1)}, bf16[8,96,768]{2,1,0:T(8,128)(2,1)}) custom-call(s32[1]{0:T(128)} %bitcast.13.refs_0_, s32[6]{0:T(128)S(1)} %stack.67.refs_1_, s32[3]{0:T(128)S(1)} %copy-done.10, f32[6]{0:T(128)S(1)} %mul.14.refs_2_.refs_3_, ...), custom_call_target="tpu_custom_call" | custom-call | flops 4076863488 | bytes 13271040 | tf_op jit(solution)/shard_map/pallas_call | solution.py:438
  157.4 11.1 %shard_map.284 = (bf16[8,96,768]{2,1,0:T(8,128)(2,1)}, bf16[8,96,768]{2,1,0:T(8,128)(2,1)}, bf16[8,96,768]{2,1,0:T(8,128)(2,1)}, bf16[8,96,768]{2,1,0:T(8,128)(2,1)}) custom-call(s32[1]{0:T(128)} %bitcast.13.refs_0_, s32[6]{0:T(128)S(1)} %stack.67.refs_1_, s32[3]{0:T(128)S(1)} %copy-done.10, f32[6]{0:T(128)S(1)} %mul.14.refs_2_.refs_3_, ...), custom_call_target="tpu_custom_call" | custom-call | flops 4076863488 | bytes 13271040 | tf_op jit(solution)/shard_map/pallas_call | solution.py:438
  175.1 11.2 %shard_map.285 = (bf16[8,96,768]{2,1,0:T(8,128)(2,1)}, bf16[8,96,768]{2,1,0:T(8,128)(2,1)}, bf16[8,96,768]{2,1,0:T(8,128)(2,1)}, bf16[8,96,768]{2,1,0:T(8,128)(2,1)}) custom-call(s32[1]{0:T(128)} %bitcast.13.refs_0_, s32[6]{0:T(128)S(1)} %stack.67.refs_1_, s32[3]{0:T(128)S(1)} %copy-done.10, f32[6]{0:T(128)S(1)} %mul.14.refs_2_.refs_3_, ...), custom_call_target="tpu_custom_call" | custom-call | flops 4076863488 | bytes 15925248 | tf_op jit(solution)/shard_map/pallas_call | solution.py:438
  188.4 10.4 %collective-permute-done.9 = bf16[8,96,768]{2,1,0:T(8,128)(2,1)S(1)} collective-permute-done((bf16[8,96,768]{2,1,0:T(8,128)(2,1)}, bf16[8,96,768]{2,1,0:T(8,128)(2,1)S(1)}, u32[]{:S(2)}, u32[]{:S(2)}) %collective-permute-start.9) | collective-permute-done | bytes 1179680 | tf_op jit(solution)/shard_map/ppermute | solution.py:570
  204.5 19.5 %collective-permute-done.6 = bf16[8,96,768]{2,1,0:T(8,128)(2,1)S(1)} collective-permute-done((bf16[8,96,768]{2,1,0:T(8,128)(2,1)S(1)}, bf16[8,96,768]{2,1,0:T(8,128)(2,1)S(1)}, u32[]{:S(2)}, u32[]{:S(2)}) %collective-permute-start.6) | collective-permute-done | bytes 1179680 | tf_op jit(solution)/shard_map/ppermute | solution.py:570
  228.6 13.3 %collective-permute-done.10 = f32[13,768]{1,0:T(8,128)S(1)} collective-permute-done((f32[13,768]{1,0:T(8,128)S(1)}, f32[13,768]{1,0:T(8,128)S(1)}, u32[]{:S(2)}, u32[]{:S(2)}) %collective-permute-start.10) | collective-permute-done | bytes 39968 | tf_op jit(solution)/shard_map/ppermute | solution.py:570
  246.2 4.7 %collective-permute-done.15 = bf16[2,96,768]{2,1,0:T(8,128)(2,1)S(1)} collective-permute-done((bf16[2,96,768]{2,1,0:T(8,128)(2,1)S(1)}, bf16[2,96,768]{2,1,0:T(8,128)(2,1)S(1)}, u32[]{:S(2)}, u32[]{:S(2)}) %collective-permute-start.15) | collective-permute-done | bytes 294944 | tf_op jit(solution)/shard_map/ppermute | solution.py:570
  255.3 3.4 collective-permute-start.22
  262.9 4.5 %collective-permute-done.22 = bf16[1,96,768]{2,1,0:T(8,128)(2,1)S(1)} collective-permute-done((bf16[1,96,768]{2,1,0:T(8,128)(2,1)S(1)}, bf16[1,96,768]{2,1,0:T(8,128)(2,1)S(1)}, u32[]{:S(2)}, u32[]{:S(2)}) %collective-permute-start.22) | collective-permute-done | bytes 147488 | tf_op jit(solution)/shard_map/ppermute | solution.py:570
  269.3 8.1 %collective-permute-done.26 = bf16[1,96,768]{2,1,0:T(8,128)(2,1)S(1)} collective-permute-done((bf16[1,96,768]{2,1,0:T(8,128)(2,1)S(1)}, bf16[1,96,768]{2,1,0:T(8,128)(2,1)S(1)}, u32[]{:S(2)}, u32[]{:S(2)}) %collective-permute-start.26) | collective-permute-done | bytes 147488 | tf_op jit(solution)/shard_map/ppermute | solution.py:570
  287.7 4.3 %collective-permute-done.37 = bf16[1,96,768]{2,1,0:T(8,128)(2,1)S(1)} collective-permute-done((bf16[1,96,768]{2,1,0:T(8,128)(2,1)S(1)}, bf16[1,96,768]{2,1,0:T(8,128)(2,1)S(1)}, u32[]{:S(2)}, u32[]{:S(2)}) %collective-permute-start.37) | collective-permute-done | bytes 147488 | tf_op jit(solution)/shard_map/ppermute | solution.py:570
  292.1 4.5 %collective-permute-done.33 = bf16[1,96,768]{2,1,0:T(8,128)(2,1)S(1)} collective-permute-done((bf16[1,96,768]{2,1,0:T(8,128)(2,1)S(1)}, bf16[1,96,768]{2,1,0:T(8,128)(2,1)S(1)}, u32[]{:S(2)}, u32[]{:S(2)}) %collective-permute-start.33) | collective-permute-done | bytes 147488 | tf_op jit(solution)/shard_map/ppermute | solution.py:570
  296.7 3.4 collective-permute-start.32
  300.3 8.1 %collective-permute-done.31 = f32[13,768]{1,0:T(8,128)S(1)} collective-permute-done((f32[13,768]{1,0:T(8,128)S(1)}, f32[13,768]{1,0:T(8,128)S(1)}, u32[]{:S(2)}, u32[]{:S(2)}) %collective-permute-start.31) | collective-permute-done | bytes 39968 | tf_op jit(solution)/shard_map/ppermute | solution.py:570
  313.7 4.2 %collective-permute-done.35 = bf16[2,96,768]{2,1,0:T(8,128)(2,1)S(1)} collective-permute-done((bf16[2,96,768]{2,1,0:T(8,128)(2,1)S(1)}, bf16[2,96,768]{2,1,0:T(8,128)(2,1)S(1)}, u32[]{:S(2)}, u32[]{:S(2)}) %collective-permute-start.35) | collective-permute-done | bytes 294944 | tf_op jit(solution)/shard_map/ppermute | solution.py:570
  318.2 5.2 %collective-permute-done.42 = bf16[1,96,768]{2,1,0:T(8,128)(2,1)S(1)} collective-permute-done((bf16[1,96,768]{2,1,0:T(8,128)(2,1)S(1)}, bf16[1,96,768]{2,1,0:T(8,128)(2,1)S(1)}, u32[]{:S(2)}, u32[]{:S(2)}) %collective-permute-start.42) | collective-permute-done | bytes 147488 | tf_op jit(solution)/shard_map/ppermute | solution.py:570
  323.7 4.9 %collective-permute-done.43 = bf16[4,96,768]{2,1,0:T(8,128)(2,1)S(1)} collective-permute-done((bf16[4,96,768]{2,1,0:T(8,128)(2,1)S(1)}, bf16[4,96,768]{2,1,0:T(8,128)(2,1)S(1)}, u32[]{:S(2)}, u32[]{:S(2)}) %collective-permute-start.43) | collective-permute-done | bytes 589856 | tf_op jit(solution)/shard_map/ppermute | solution.py:570
  332.7 7.3 %collective-permute-done.41 = bf16[1,96,768]{2,1,0:T(8,128)(2,1)S(1)} collective-permute-done((bf16[1,96,768]{2,1,0:T(8,128)(2,1)S(1)}, bf16[1,96,768]{2,1,0:T(8,128)(2,1)S(1)}, u32[]{:S(2)}, u32[]{:S(2)}) %collective-permute-start.41) | collective-permute-done | bytes 147488 | tf_op jit(solution)/shard_map/ppermute | solution.py:570
  347.7 3.3 collective-permute-done.45
  352.1 14.1 %collective-permute-done.49 = bf16[2,96,768]{2,1,0:T(8,128)(2,1)S(1)} collective-permute-done((bf16[2,96,768]{2,1,0:T(8,128)(2,1)S(1)}, bf16[2,96,768]{2,1,0:T(8,128)(2,1)S(1)}, u32[]{:S(2)}, u32[]{:S(2)}) %collective-permute-start.49) | collective-permute-done | bytes 294944 | tf_op jit(solution)/shard_map/ppermute | solution.py:570
  371.9 11.4 %collective-permute-done.52 = bf16[4,96,768]{2,1,0:T(8,128)(2,1)S(1)} collective-permute-done((bf16[4,96,768]{2,1,0:T(8,128)(2,1)S(1)}, bf16[4,96,768]{2,1,0:T(8,128)(2,1)S(1)}, u32[]{:S(2)}, u32[]{:S(2)}) %collective-permute-start.52) | collective-permute-done | bytes 589856 | tf_op jit(solution)/shard_map/ppermute | solution.py:570
  394.8 5.7 %collective-permute-done.56.refs_0_ = bf16[8,96,768]{2,1,0:T(8,128)(2,1)S(1)} collective-permute-done((bf16[8,96,768]{2,1,0:T(8,128)(2,1)S(1)}, bf16[8,96,768]{2,1,0:T(8,128)(2,1)S(1)}, u32[]{:S(2)}, u32[]{:S(2)}) %collective-permute-start.56) | collective-permute-done | bytes 1179680 | tf_op jit(solution)/shard_map/ppermute | solution.py:570
  406.3 6.9 %collective-permute-done.54.refs_0_ = bf16[8,96,768]{2,1,0:T(8,128)(2,1)S(1)} collective-permute-done((bf16[8,96,768]{2,1,0:T(8,128)(2,1)S(1)}, bf16[8,96,768]{2,1,0:T(8,128)(2,1)S(1)}, u32[]{:S(2)}, u32[]{:S(2)}) %collective-permute-start.54) | collective-permute-done | bytes 1179680 | tf_op jit(solution)/shard_map/ppermute | solution.py:570
  (264 shorter events, 119.1 us)
Async XLA Ops:
  22.6 38.5 %collective-permute-start = (bf16[288,768]{1,0:T(8,128)(2,1)}, bf16[288,768]{1,0:T(8,128)(2,1)}, u32[]{:S(2)}, u32[]{:S(2)}) collective-permute-start(bf16[288,768]{1,0:T(8,128)(2,1)} %get-tuple-element.177), channel_id=1, source_target_pairs={{0,16},{1,17},{2,18},{3,19},{4,20},{5,21},{6,22},{7,23},{8,24},{9,... | collective-permute-start | bytes 1327112 | tf_op jit(solution)/shard_map/ppermute | solution.py:694
  41.2 28.3 %collective-permute-start.2 = (bf16[288,768]{1,0:T(8,128)(2,1)}, bf16[288,768]{1,0:T(8,128)(2,1)}, u32[]{:S(2)}, u32[]{:S(2)}) collective-permute-start(bf16[288,768]{1,0:T(8,128)(2,1)} %get-tuple-element.187), channel_id=1, source_target_pairs={{0,16},{1,17},{2,18},{3,19},{4,20},{5,21},{6,22},{7,23},{8,24},{9,... | collective-permute-start | bytes 1327112 | tf_op jit(solution)/shard_map/ppermute | solution.py:694
  91.5 24.5 %collective-permute-start.4 = (bf16[288,768]{1,0:T(8,128)(2,1)}, bf16[288,768]{1,0:T(8,128)(2,1)S(1)}, u32[]{:S(2)}, u32[]{:S(2)}) collective-permute-start(bf16[288,768]{1,0:T(8,128)(2,1)} %get-tuple-element.212), channel_id=1, source_target_pairs={{16,0},{17,1},{18,2},{19,3},{20,4},{21,5},{22,6},{23,7},{24,8},{25... | collective-permute-start | bytes 1327112 | tf_op jit(solution)/shard_map/ppermute | solution.py:694
  93.5 37.4 %collective-permute-start.5 = (bf16[288,768]{1,0:T(8,128)(2,1)}, bf16[288,768]{1,0:T(8,128)(2,1)S(1)}, u32[]{:S(2)}, u32[]{:S(2)}) collective-permute-start(bf16[288,768]{1,0:T(8,128)(2,1)} %get-tuple-element.221), channel_id=1, source_target_pairs={{16,0},{17,1},{18,2},{19,3},{20,4},{21,5},{22,6},{23,7},{24,8},{25... | collective-permute-start | bytes 1327112 | tf_op jit(solution)/shard_map/ppermute | solution.py:694
  168.6 30.1 %collective-permute-start.9 = (bf16[8,96,768]{2,1,0:T(8,128)(2,1)}, bf16[8,96,768]{2,1,0:T(8,128)(2,1)S(1)}, u32[]{:S(2)}, u32[]{:S(2)}) collective-permute-start(bf16[8,96,768]{2,1,0:T(8,128)(2,1)} %get-tuple-element.262), channel_id=1, source_target_pairs={{0,1},{1,0},{2,3},{3,2},{4,5},{5,4},{6,7},{7,6},{8,9},{9,8},{10,11... | collective-permute-start | bytes 3538952 | tf_op jit(solution)/shard_map/ppermute | solution.py:570
  172.2 28.7 %collective-permute-start.8 = (bf16[8,96,768]{2,1,0:T(8,128)(2,1)S(1)}, bf16[8,96,768]{2,1,0:T(8,128)(2,1)S(1)}, u32[]{:S(2)}, u32[]{:S(2)}) collective-permute-start(bf16[8,96,768]{2,1,0:T(8,128)(2,1)S(1)} %copy-done.40), channel_id=1, source_target_pairs={{0,2},{1,3},{2,0},{3,1},{4,6},{5,7},{6,4},{7,5},{8,10},{9,11},{10,... | collective-permute-start | bytes 3538952 | tf_op jit(solution)/shard_map/ppermute | solution.py:570
  174.4 28.2 %collective-permute-start.7 = (bf16[8,96,768]{2,1,0:T(8,128)(2,1)}, bf16[8,96,768]{2,1,0:T(8,128)(2,1)S(1)}, u32[]{:S(2)}, u32[]{:S(2)}) collective-permute-start(bf16[8,96,768]{2,1,0:T(8,128)(2,1)} %get-tuple-element.258), channel_id=1, source_target_pairs={{0,2},{1,3},{2,0},{3,1},{4,6},{5,7},{6,4},{7,5},{8,10},{9,11},{10,... | collective-permute-start | bytes 3538952 | tf_op jit(solution)/shard_map/ppermute | solution.py:570
  175.0 49.0 %collective-permute-start.6 = (bf16[8,96,768]{2,1,0:T(8,128)(2,1)S(1)}, bf16[8,96,768]{2,1,0:T(8,128)(2,1)S(1)}, u32[]{:S(2)}, u32[]{:S(2)}) collective-permute-start(bf16[8,96,768]{2,1,0:T(8,128)(2,1)S(1)} %copy-done.39), channel_id=1, source_target_pairs={{0,1},{1,0},{2,3},{3,2},{4,5},{5,4},{6,7},{7,6},{8,9},{9,8},{10,11... | collective-permute-start | bytes 3538952 | tf_op jit(solution)/shard_map/ppermute | solution.py:570
  186.3 39.9 %collective-permute-start.23 = (bf16[8,96,768]{2,1,0:T(8,128)(2,1)}, bf16[8,96,768]{2,1,0:T(8,128)(2,1)S(1)}, u32[]{:S(2)}, u32[]{:S(2)}) collective-permute-start(bf16[8,96,768]{2,1,0:T(8,128)(2,1)} %get-tuple-element.292), channel_id=1, source_target_pairs={{0,4},{1,5},{2,6},{3,7},{4,0},{5,1},{6,2},{7,3},{8,12},{9,13},{10,... | collective-permute-start | bytes 3538952 | tf_op jit(solution)/shard_map/ppermute | solution.py:570
  198.7 29.1 %collective-permute-start.14 = (bf16[8,96,768]{2,1,0:T(8,128)(2,1)}, bf16[8,96,768]{2,1,0:T(8,128)(2,1)S(1)}, u32[]{:S(2)}, u32[]{:S(2)}) collective-permute-start(bf16[8,96,768]{2,1,0:T(8,128)(2,1)} %get-tuple-element.284), channel_id=1, source_target_pairs={{0,2},{1,3},{2,0},{3,1},{4,6},{5,7},{6,4},{7,5},{8,10},{9,11},{10,... | collective-permute-start | bytes 3538952 | tf_op jit(solution)/shard_map/ppermute | solution.py:570
  200.9 45.2 %collective-permute-start.19 = (bf16[4,96,768]{2,1,0:T(8,128)(2,1)S(1)}, bf16[4,96,768]{2,1,0:T(8,128)(2,1)S(1)}, u32[]{:S(2)}, u32[]{:S(2)}) collective-permute-start(bf16[4,96,768]{2,1,0:T(8,128)(2,1)S(1)} %add_convert_fusion.2), channel_id=1, source_target_pairs={{0,4},{1,5},{2,6},{3,7},{4,0},{5,1},{6,2},{7,3},{8,12},{9,13},{10,... | collective-permute-start | bytes 1769480 | tf_op jit(solution)/shard_map/ppermute | solution.py:570
  202.7 41.0 %collective-permute-start.11 = (bf16[4,96,768]{2,1,0:T(8,128)(2,1)S(1)}, bf16[4,96,768]{2,1,0:T(8,128)(2,1)S(1)}, u32[]{:S(2)}, u32[]{:S(2)}) collective-permute-start(bf16[4,96,768]{2,1,0:T(8,128)(2,1)S(1)} %add_convert_fusion.3), channel_id=1, source_target_pairs={{0,1},{1,0},{2,3},{3,2},{4,5},{5,4},{6,7},{7,6},{8,9},{9,8},{10,11... | collective-permute-start | bytes 1769480 | tf_op jit(solution)/shard_map/ppermute | solution.py:570
  224.0 17.9 %collective-permute-start.12 = (bf16[4,96,768]{2,1,0:T(8,128)(2,1)S(1)}, bf16[4,96,768]{2,1,0:T(8,128)(2,1)S(1)}, u32[]{:S(2)}, u32[]{:S(2)}) collective-permute-start(bf16[4,96,768]{2,1,0:T(8,128)(2,1)S(1)} %add_convert_fusion.4), channel_id=1, source_target_pairs={{0,1},{1,0},{2,3},{3,2},{4,5},{5,4},{6,7},{7,6},{8,9},{9,8},{10,11... | collective-permute-start | bytes 1769480 | tf_op jit(solution)/shard_map/ppermute | solution.py:570
  226.2 18.1 %collective-permute-start.16 = (bf16[4,96,768]{2,1,0:T(8,128)(2,1)S(1)}, bf16[4,96,768]{2,1,0:T(8,128)(2,1)S(1)}, u32[]{:S(2)}, u32[]{:S(2)}) collective-permute-start(bf16[4,96,768]{2,1,0:T(8,128)(2,1)S(1)} %add_convert_fusion.5), channel_id=1, source_target_pairs={{0,2},{1,3},{2,0},{3,1},{4,6},{5,7},{6,4},{7,5},{8,10},{9,11},{10,... | collective-permute-start | bytes 1769480 | tf_op jit(solution)/shard_map/ppermute | solution.py:570
  251.0 18.0 %collective-permute-start.27 = (bf16[1,96,768]{2,1,0:T(8,128)(2,1)S(1)}, bf16[1,96,768]{2,1,0:T(8,128)(2,1)S(1)}, u32[]{:S(2)}, u32[]{:S(2)}) collective-permute-start(bf16[1,96,768]{2,1,0:T(8,128)(2,1)S(1)} %add_convert_fusion.22), channel_id=1, source_target_pairs={{0,8},{1,9},{2,10},{3,11},{4,12},{5,13},{6,14},{7,15},{8,0},{9,1},... | collective-permute-start | bytes 442376 | tf_op jit(solution)/shard_map/ppermute | solution.py:570
  253.7 23.9 %collective-permute-start.21 = (bf16[4,96,768]{2,1,0:T(8,128)(2,1)S(1)}, bf16[4,96,768]{2,1,0:T(8,128)(2,1)S(1)}, u32[]{:S(2)}, u32[]{:S(2)}) collective-permute-start(bf16[4,96,768]{2,1,0:T(8,128)(2,1)S(1)} %add_convert_fusion.1), channel_id=1, source_target_pairs={{0,1},{1,0},{2,3},{3,2},{4,5},{5,4},{6,7},{7,6},{8,9},{9,8},{10,11... | collective-permute-start | bytes 1769480 | tf_op jit(solution)/shard_map/ppermute | solution.py:570
  260.0 17.5 %collective-permute-start.30 = (bf16[2,96,768]{2,1,0:T(8,128)(2,1)S(1)}, bf16[2,96,768]{2,1,0:T(8,128)(2,1)S(1)}, u32[]{:S(2)}, u32[]{:S(2)}) collective-permute-start(bf16[2,96,768]{2,1,0:T(8,128)(2,1)S(1)} %add_convert_fusion.8), channel_id=1, source_target_pairs={{0,2},{1,3},{2,0},{3,1},{4,6},{5,7},{6,4},{7,5},{8,10},{9,11},{10,... | collective-permute-start | bytes 884744 | tf_op jit(solution)/shard_map/ppermute | solution.py:570
  281.3 18.9 %collective-permute-start.34 = (bf16[2,96,768]{2,1,0:T(8,128)(2,1)S(1)}, bf16[2,96,768]{2,1,0:T(8,128)(2,1)S(1)}, u32[]{:S(2)}, u32[]{:S(2)}) collective-permute-start(bf16[2,96,768]{2,1,0:T(8,128)(2,1)S(1)} %pad_maximum_fusion.12), channel_id=1, source_target_pairs={{0,4},{1,5},{2,6},{3,7},{4,0},{5,1},{6,2},{7,3},{8,12},{9,13},{10,... | collective-permute-start | bytes 884744 | tf_op jit(solution)/shard_map/ppermute | solution.py:570
  285.8 22.8 %collective-permute-start.38 = (bf16[2,96,768]{2,1,0:T(8,128)(2,1)S(1)}, bf16[2,96,768]{2,1,0:T(8,128)(2,1)S(1)}, u32[]{:S(2)}, u32[]{:S(2)}) collective-permute-start(bf16[2,96,768]{2,1,0:T(8,128)(2,1)S(1)} %add_convert_fusion.7), channel_id=1, source_target_pairs={{0,4},{1,5},{2,6},{3,7},{4,0},{5,1},{6,2},{7,3},{8,12},{9,13},{10,... | collective-permute-start | bytes 884744 | tf_op jit(solution)/shard_map/ppermute | solution.py:570
  292.0 19.3 %collective-permute-start.36 = (bf16[2,96,768]{2,1,0:T(8,128)(2,1)S(1)}, bf16[2,96,768]{2,1,0:T(8,128)(2,1)S(1)}, u32[]{:S(2)}, u32[]{:S(2)}) collective-permute-start(bf16[2,96,768]{2,1,0:T(8,128)(2,1)S(1)} %pad_maximum_fusion.13), channel_id=1, source_target_pairs={{0,4},{1,5},{2,6},{3,7},{4,0},{5,1},{6,2},{7,3},{8,12},{9,13},{10,... | collective-permute-start | bytes 884744 | tf_op jit(solution)/shard_map/ppermute | solution.py:570
  296.7 21.4 %collective-permute-start.32 = (bf16[1,96,768]{2,1,0:T(8,128)(2,1)S(1)}, bf16[1,96,768]{2,1,0:T(8,128)(2,1)S(1)}, u32[]{:S(2)}, u32[]{:S(2)}) collective-permute-start(bf16[1,96,768]{2,1,0:T(8,128)(2,1)S(1)} %add_convert_fusion.17), channel_id=1, source_target_pairs={{0,8},{1,9},{2,10},{3,11},{4,12},{5,13},{6,14},{7,15},{8,0},{9,1},... | collective-permute-start | bytes 442376 | tf_op jit(solution)/shard_map/ppermute | solution.py:570
  330.2 17.4 %collective-permute-start.46 = (bf16[4,96,768]{2,1,0:T(8,128)(2,1)S(1)}, bf16[4,96,768]{2,1,0:T(8,128)(2,1)S(1)}, u32[]{:S(2)}, u32[]{:S(2)}) collective-permute-start(bf16[4,96,768]{2,1,0:T(8,128)(2,1)S(1)} %pad_maximum_fusion.8), channel_id=1, source_target_pairs={{0,1},{1,0},{2,3},{3,2},{4,5},{5,4},{6,7},{7,6},{8,9},{9,8},{10,11... | collective-permute-start | bytes 1769480 | tf_op jit(solution)/shard_map/ppermute | solution.py:570
  343.6 22.7 %collective-permute-start.50 = (bf16[4,96,768]{2,1,0:T(8,128)(2,1)S(1)}, bf16[4,96,768]{2,1,0:T(8,128)(2,1)S(1)}, u32[]{:S(2)}, u32[]{:S(2)}) collective-permute-start(bf16[4,96,768]{2,1,0:T(8,128)(2,1)S(1)} %pad_maximum_fusion.10), channel_id=1, source_target_pairs={{0,4},{1,5},{2,6},{3,7},{4,0},{5,1},{6,2},{7,3},{8,12},{9,13},{10,... | collective-permute-start | bytes 1769480 | tf_op jit(solution)/shard_map/ppermute | solution.py:570
  343.7 22.5 %collective-permute-start.49 = (bf16[2,96,768]{2,1,0:T(8,128)(2,1)S(1)}, bf16[2,96,768]{2,1,0:T(8,128)(2,1)S(1)}, u32[]{:S(2)}, u32[]{:S(2)}) collective-permute-start(bf16[2,96,768]{2,1,0:T(8,128)(2,1)S(1)} %pad_maximum_fusion.16), channel_id=1, source_target_pairs={{0,4},{1,5},{2,6},{3,7},{4,0},{5,1},{6,2},{7,3},{8,12},{9,13},{10,... | collective-permute-start | bytes 884744 | tf_op jit(solution)/shard_map/ppermute | solution.py:570
  345.8 37.6 %collective-permute-start.57 = (bf16[8,96,768]{2,1,0:T(8,128)(2,1)S(1)}, bf16[8,96,768]{2,1,0:T(8,128)(2,1)S(1)}, u32[]{:S(2)}, u32[]{:S(2)}) collective-permute-start(bf16[8,96,768]{2,1,0:T(8,128)(2,1)S(1)} %pad_maximum_fusion.1.refs_1_), channel_id=1, source_target_pairs={{0,2},{1,3},{2,0},{3,1},{4,6},{5,7},{6,4},{7,5},{8,10},{9,11},{10,... | collective-permute-start | bytes 3538952 | tf_op jit(solution)/shard_map/ppermute | solution.py:570
  351.0 19.7 %collective-permute-start.48 = (bf16[4,96,768]{2,1,0:T(8,128)(2,1)S(1)}, bf16[4,96,768]{2,1,0:T(8,128)(2,1)S(1)}, u32[]{:S(2)}, u32[]{:S(2)}) collective-permute-start(bf16[4,96,768]{2,1,0:T(8,128)(2,1)S(1)} %pad_maximum_fusion.9), channel_id=1, source_target_pairs={{0,1},{1,0},{2,3},{3,2},{4,5},{5,4},{6,7},{7,6},{8,9},{9,8},{10,11... | collective-permute-start | bytes 1769480 | tf_op jit(solution)/shard_map/ppermute | solution.py:570
  366.5 16.8 %collective-permute-start.52 = (bf16[4,96,768]{2,1,0:T(8,128)(2,1)S(1)}, bf16[4,96,768]{2,1,0:T(8,128)(2,1)S(1)}, u32[]{:S(2)}, u32[]{:S(2)}) collective-permute-start(bf16[4,96,768]{2,1,0:T(8,128)(2,1)S(1)} %pad_maximum_fusion.11), channel_id=1, source_target_pairs={{0,1},{1,0},{2,3},{3,2},{4,5},{5,4},{6,7},{7,6},{8,9},{9,8},{10,11... | collective-permute-start | bytes 1769480 | tf_op jit(solution)/shard_map/ppermute | solution.py:570
  369.3 31.2 %collective-permute-start.56 = (bf16[8,96,768]{2,1,0:T(8,128)(2,1)S(1)}, bf16[8,96,768]{2,1,0:T(8,128)(2,1)S(1)}, u32[]{:S(2)}, u32[]{:S(2)}) collective-permute-start(bf16[8,96,768]{2,1,0:T(8,128)(2,1)S(1)} %pad_maximum_fusion.refs_0_), channel_id=1, source_target_pairs={{0,1},{1,0},{2,3},{3,2},{4,5},{5,4},{6,7},{7,6},{8,9},{9,8},{10,11... | collective-permute-start | bytes 3538952 | tf_op jit(solution)/shard_map/ppermute | solution.py:570
  370.4 35.9 %collective-permute-start.55 = (bf16[8,96,768]{2,1,0:T(8,128)(2,1)S(1)}, bf16[8,96,768]{2,1,0:T(8,128)(2,1)S(1)}, u32[]{:S(2)}, u32[]{:S(2)}) collective-permute-start(bf16[8,96,768]{2,1,0:T(8,128)(2,1)S(1)} %pad_maximum_fusion.2.refs_1_), channel_id=1, source_target_pairs={{0,2},{1,3},{2,0},{3,1},{4,6},{5,7},{6,4},{7,5},{8,10},{9,11},{10,... | collective-permute-start | bytes 3538952 | tf_op jit(solution)/shard_map/ppermute | solution.py:570
  370.7 42.4 %collective-permute-start.54 = (bf16[8,96,768]{2,1,0:T(8,128)(2,1)S(1)}, bf16[8,96,768]{2,1,0:T(8,128)(2,1)S(1)}, u32[]{:S(2)}, u32[]{:S(2)}) collective-permute-start(bf16[8,96,768]{2,1,0:T(8,128)(2,1)S(1)} %pad_maximum_fusion.4.refs_0_), channel_id=1, source_target_pairs={{0,1},{1,0},{2,3},{3,2},{4,5},{5,4},{6,7},{7,6},{8,9},{9,8},{10,11... | collective-permute-start | bytes 3538952 | tf_op jit(solution)/shard_map/ppermute | solution.py:570
  383.3 32.7 %collective-permute-start.51 = (bf16[8,96,768]{2,1,0:T(8,128)(2,1)S(1)}, bf16[8,96,768]{2,1,0:T(8,128)(2,1)S(1)}, u32[]{:S(2)}, u32[]{:S(2)}) collective-permute-start(bf16[8,96,768]{2,1,0:T(8,128)(2,1)S(1)} %pad_maximum_fusion.3.refs_0_), channel_id=1, source_target_pairs={{0,4},{1,5},{2,6},{3,7},{4,0},{5,1},{6,2},{7,3},{8,12},{9,13},{10,... | collective-permute-start | bytes 3538952 | tf_op jit(solution)/shard_map/ppermute | solution.py:570
  383.4 32.6 %collective-permute-start.53 = (bf16[8,96,768]{2,1,0:T(8,128)(2,1)S(1)}, bf16[8,96,768]{2,1,0:T(8,128)(2,1)S(1)}, u32[]{:S(2)}, u32[]{:S(2)}) collective-permute-start(bf16[8,96,768]{2,1,0:T(8,128)(2,1)S(1)} %pad_maximum_fusion.5.refs_1_), channel_id=1, source_target_pairs={{0,2},{1,3},{2,0},{3,1},{4,6},{5,7},{6,4},{7,5},{8,10},{9,11},{10,... | collective-permute-start | bytes 3538952 | tf_op jit(solution)/shard_map/ppermute | solution.py:570
  (69 other events, 640.9 us)
